TPU v7x, 256 devices: a whole 4x4x8 slice. The times are simulated.
256 devices in a mesh: dp: 8 (over x, core), tm: 8 (over z_hi, y), height: 4 (over z_lo).
Axes of the slice: x: 4, y: 4, z: 8 (z_hi: 2, z_lo: 4; z = z_hi * 4 + z_lo), core: 2. Of those that a mesh axis runs over, the one named last changes fastest.
Arguments:
- queries: bfloat16 [8, 4, 384, 3072], P('tm', 'height', None, 'dp'), may hold values from -6 to 6
- key_vectors: bfloat16 [8, 4, 384, 3072], P('tm', 'height', None, 'dp'), may hold values from -6 to 6
- value_vectors: bfloat16 [8, 4, 384, 3072], P('tm', 'height', None, 'dp'), may hold values from -6 to 6
- out_grads: bfloat16 [8, 4, 384, 3072], P('tm', 'height', None, 'dp'), may hold values from -9 to 9
- query_gain: float32 [128], replicated, may hold values from 0.6 to 5.5
- key_gain: float32 [128], replicated, may hold values from 0.6 to 5.5
- frame_counts: int32 [8], replicated, may hold values from 1 to 6, as said below
- row_counts: int32 [4], replicated, may hold values from 1 to 8, as said below
Outputs:
- d_queries: bfloat16 [8, 4, 384, 3072], P('tm', 'height', None, 'dp')
- d_keys: bfloat16 [8, 4, 384, 3072], P('tm', 'height', None, 'dp')
- d_values: bfloat16 [8, 4, 384, 3072], P('tm', 'height', None, 'dp')
- gain_grads: float32 [2, 128], replicated
Inputs may be any that keep to these rules, and one draw needn't show every extreme that they name: `frame_counts`: exactly one time tile has all 6 frames; the others have fewer. `row_counts`: exactly one height tile has all 8 rows; the others have fewer.
All inputs are finite; a program needn't handle non-finite values.
Results may differ from a plain program's by a relative error of at most 0.004.
The roundings to bfloat16 on the way count: a program that leaves them out, or rounds other values in their place, can miss the bound.
Values may be sent and summed in bfloat16 or wider, within the bound.
No kernel may reach another device: no remote copies, remote signals or barrier semaphores. Data moves between devices by JAX's collectives and lax.ppermute only.
A program may use at most 64 MiB of HBM per device.

v0:
```python
import math

import jax
import jax.numpy as jnp
from jax import lax
from jax.sharding import PartitionSpec as P

HD = 128
TF = 6
TH = 8
TW = 8


NORM_EPSILON = 1e-06


def with_halo(x, sides, width):
    for axis, dim in sides:
        count, length = (lax.axis_size(axis), x.shape[dim])
        up = [(i, (i + 1) % count) for i in range(count - 1)]
        down = [(j, i) for i, j in up]
        last = lax.slice_in_dim(x, length - width, length, axis=dim)
        first = lax.slice_in_dim(x, 0, width, axis=dim)
        before = lax.ppermute(last, axis, up)
        after = lax.ppermute(first, axis, down)
        x = jnp.concatenate([before, x, after], axis=dim)
    return x


def shifted(block, axis, distance):
    devices = range(lax.axis_size(axis))
    route = [(i - distance, i) for i in devices if i - distance in devices]
    return lax.ppermute(block, axis, route)


def pick(table, index):
    return jnp.sum(jnp.where(jnp.arange(table.shape[0], dtype=jnp.int32) == index, table, 0))


def head_norm(raw_values, norm_gain):
    leading = raw_values.shape[:-1]
    head_total = raw_values.shape[-1] // HD
    shaped = raw_values.astype(jnp.float32).reshape(leading + (head_total, HD))
    rms_inverse = lax.rsqrt(jnp.mean(shaped * shaped, axis=-1, keepdims=True) + NORM_EPSILON)
    unit_part = shaped * rms_inverse
    normed = (unit_part * norm_gain).astype(jnp.bfloat16).reshape(raw_values.shape)
    return (normed, unit_part, rms_inverse)


def norm_backward(grad_normed, unit_part, rms_inverse, norm_gain):
    shaped = grad_normed.reshape(unit_part.shape) * norm_gain
    inner = jnp.mean(shaped * unit_part, axis=-1, keepdims=True)
    return (rms_inverse * (shaped - unit_part * inner)).reshape(grad_normed.shape)


def gain_term(grad_normed, unit_part):
    product = grad_normed.reshape(unit_part.shape) * unit_part
    return jnp.sum(product.reshape(-1, HD), axis=0)


def neighbours(time_pos, height_pos, time_count, height_count, frame_counts, row_counts):
    present, frame_limits, row_limits = ([], [], [])
    for time_step in (-1, 0, 1):
        for height_step in (-1, 0, 1):
            time_at = time_pos + time_step
            height_at = height_pos + height_step
            present.append(
                (time_at >= 0)
                & (time_at < time_count)
                & (height_at >= 0)
                & (height_at < height_count)
            )
            time_near = jnp.clip(time_at, 0, time_count - 1)
            height_near = jnp.clip(height_at, 0, height_count - 1)
            frame_limits.append(pick(frame_counts, time_near))
            row_limits.append(pick(row_counts, height_near))
    return (jnp.stack(present), jnp.stack(frame_limits), jnp.stack(row_limits))


def key_mask(present, frame_limits, row_limits):
    positions = jnp.arange(TF * TH * TW, dtype=jnp.int32)
    frame_pos = positions // (TH * TW)
    row_pos = positions % (TH * TW) // TW
    allowed = (
        present[:, None]
        & (frame_pos[None, :] < frame_limits[:, None])
        & (row_pos[None, :] < row_limits[:, None])
    )
    return allowed.reshape(-1)


def tile_backward(query_rows, key_rows, value_rows, grad_rows, allowed):
    row_count = query_rows.shape[0]
    feature_count = query_rows.shape[1]
    scaling = 1.0 / math.sqrt(HD)
    zeros_query = jnp.zeros((row_count, feature_count), jnp.float32)
    zeros_keys = jnp.zeros((key_rows.shape[0], feature_count), jnp.float32)

    def head_step(head_index, running):
        query_grad, key_grad, value_grad = running
        head_start = head_index * HD
        q_head = lax.dynamic_slice_in_dim(query_rows, head_start, HD, 1)
        k_head = lax.dynamic_slice_in_dim(key_rows, head_start, HD, 1)
        v_head = lax.dynamic_slice_in_dim(value_rows, head_start, HD, 1)
        g_head = lax.dynamic_slice_in_dim(grad_rows, head_start, HD, 1)
        scores = jnp.dot(q_head, k_head.T, preferred_element_type=jnp.float32) * scaling
        masked = jnp.where(allowed[None, :], scores, -1e30)
        row_max = jnp.max(masked, axis=1, keepdims=True)
        exponent = jnp.where(allowed[None, :], jnp.exp(masked - row_max), 0.0)
        weights = exponent / jnp.sum(exponent, axis=1, keepdims=True)
        weights_low = weights.astype(jnp.bfloat16)
        attn_out = jnp.dot(weights_low, v_head, preferred_element_type=jnp.float32)
        row_delta = jnp.sum(g_head.astype(jnp.float32) * attn_out, axis=1, keepdims=True)
        weight_grad = jnp.dot(g_head, v_head.T, preferred_element_type=jnp.float32)
        score_grad = (weights * (weight_grad - row_delta) * scaling).astype(jnp.bfloat16)
        query_grad = lax.dynamic_update_slice_in_dim(
            query_grad,
            jnp.dot(score_grad, k_head, preferred_element_type=jnp.float32),
            head_start,
            1,
        )
        key_grad = lax.dynamic_update_slice_in_dim(
            key_grad,
            jnp.dot(score_grad.T, q_head, preferred_element_type=jnp.float32),
            head_start,
            1,
        )
        value_grad = lax.dynamic_update_slice_in_dim(
            value_grad,
            jnp.dot(weights_low.T, g_head, preferred_element_type=jnp.float32),
            head_start,
            1,
        )
        return (query_grad, key_grad, value_grad)

    return lax.fori_loop(0, feature_count // HD, head_step, (zeros_query, zeros_keys, zeros_keys))


def on_device(
    queries, key_vectors, value_vectors, out_grads, query_gain, key_gain, frame_counts, row_counts
):
    time_index = lax.axis_index("tm")
    height_index = lax.axis_index("height")
    time_count = lax.axis_size("tm")
    height_count = lax.axis_size("height")
    row_count = queries.shape[2]
    feature_count = queries.shape[3]
    tile_size = TF * TH * TW
    q_normed, q_unit, q_inverse = head_norm(queries[0, 0], query_gain)
    k_normed, k_unit, k_inverse = head_norm(key_vectors[0, 0], key_gain)
    positions = jnp.arange(row_count, dtype=jnp.int32) % tile_size
    frame_pos = positions // (TH * TW)
    row_pos = positions % (TH * TW) // TW
    query_valid = (frame_pos < pick(frame_counts, time_index)) & (
        row_pos < pick(row_counts, height_index)
    )
    grads_here = out_grads[0, 0]
    masked_grads = jnp.where(query_valid[:, None], grads_here, jnp.zeros_like(grads_here))
    present, frame_limits, row_limits = neighbours(
        time_index, height_index, time_count, height_count, frame_counts, row_counts
    )
    allowed = key_mask(present, frame_limits, row_limits)
    paired = jnp.stack([k_normed, value_vectors[0, 0]])[:, None, None]
    framed = with_halo(paired, (("tm", 1), ("height", 2)), 1)
    query_parts, key_parts, value_parts = ([], [], [])
    keys_here = framed[0, :, :, 0:tile_size].reshape(9 * tile_size, feature_count)
    values_here = framed[1, :, :, 0:tile_size].reshape(9 * tile_size, feature_count)
    query_grad, key_grad, value_grad = tile_backward(
        q_normed, keys_here, values_here, masked_grads, allowed
    )
    query_parts.append(query_grad)
    key_parts.append(key_grad.reshape(3, 3, tile_size, feature_count))
    value_parts.append(value_grad.reshape(3, 3, tile_size, feature_count))
    dq_normed = query_parts[0]
    terms_low = jnp.stack([key_parts[0], value_parts[0]]).astype(jnp.bfloat16)
    terms = lax.optimization_barrier(terms_low)
    moved = {}
    for offset in (-1, 1):
        moved[offset] = shifted(terms[:, offset + 1], "tm", offset)
    groups = {}
    for height_step in (-1, 0, 1):
        groups[height_step] = jnp.stack(
            [
                terms[:, 1, height_step + 1],
                moved[-1][:, height_step + 1],
                moved[1][:, height_step + 1],
            ],
            axis=1,
        )
    summed = jnp.sum(groups[0].astype(jnp.float32), axis=1)
    for offset in (-1, 1):
        landed = shifted(groups[offset], "height", offset)
        summed = summed + jnp.sum(landed.astype(jnp.float32), axis=1)
    d_queries = norm_backward(dq_normed, q_unit, q_inverse, query_gain).astype(jnp.bfloat16)
    d_keys = norm_backward(summed[0], k_unit, k_inverse, key_gain).astype(jnp.bfloat16)
    d_values = summed[1].astype(jnp.bfloat16)
    gain_local = jnp.stack([gain_term(dq_normed, q_unit), gain_term(summed[0], k_unit)])
    gain_total = lax.psum(gain_local, ("dp", "tm", "height"))
    head_total = lax.axis_size("dp") * (feature_count // HD)
    scaling = 1.0 / math.sqrt(time_count * height_count * row_count * head_total)
    gain_grads = gain_total * scaling
    return (d_queries[None, None], d_keys[None, None], d_values[None, None], gain_grads)


def solution(mesh):
    in_specs = (
        P("tm", "height", None, "dp"),
        P("tm", "height", None, "dp"),
        P("tm", "height", None, "dp"),
        P("tm", "height", None, "dp"),
        P(),
        P(),
        P(),
        P(),
    )
    out_specs = (
        P("tm", "height", None, "dp"),
        P("tm", "height", None, "dp"),
        P("tm", "height", None, "dp"),
        P(),
    )
    return jax.shard_map(
        on_device, mesh=mesh, in_specs=in_specs, out_specs=out_specs, check_vma=False
    )
```

profile of v0, /device:TPU:2, one launch (start us, length us, event | category | flops | bytes accessed | tf_op | source)
XLA Modules:
  0.0 372.4 jit_solution(8605042504078632032)
XLA Ops:
  3.6 3.6 collective-permute-start
  8.6 11.2 %collective-permute-done = bf16[2,1,1,384,384]{4,3,0,2,1:T(8,128)(2,1)S(1)} collective-permute-done((bf16[2,1,1,384,384]{4,3,0,2,1:T(8,128)(2,1)S(1)}, bf16[2,1,1,384,384]{4,3,0,2,1:T(8,128)(2,1)S(1)}, u32[]{:S(2)}, u32[]{:S(2)}) %collective-permute-start) | collective-permute-done | bytes 589856 | tf_op jit(solution)/shard_map/ppermute | solution.py:24
  19.8 4.1 %collective-permute-done.1 = bf16[2,1,1,384,384]{4,3,0,2,1:T(8,128)(2,1)S(1)} collective-permute-done((bf16[2,1,1,384,384]{4,3,0,2,1:T(8,128)(2,1)S(1)}, bf16[2,1,1,384,384]{4,3,0,2,1:T(8,128)(2,1)S(1)}, u32[]{:S(2)}, u32[]{:S(2)}) %collective-permute-start.1) | collective-permute-done | bytes 589856 | tf_op jit(solution)/shard_map/ppermute | solution.py:25
  25.4 5.1 %collective-permute-start.2 = (bf16[2,3,1,384,384]{4,3,0,2,1:T(8,128)(2,1)}, bf16[2,3,1,384,384]{4,3,0,2,1:T(8,128)(2,1)}, u32[]{:S(2)}, u32[]{:S(2)}) collective-permute-start(bf16[2,3,1,384,384]{4,3,0,2,1:T(8,128)(2,1)} %pad_maximum_fusion.2), channel_id=1, source_target_pairs={{0,1},{1,2},{2,3},{4,5},{5,6},{6,7},{8,9},{9,10},{10,11},{12,13},{... | collective-permute-start | bytes 5308424 | tf_op jit(solution)/shard_map/ppermute | solution.py:24
  34.0 6.4 %stack.104 = s32[9]{0:T(128)} concatenate(s32[1]{0:T(128)} %bitcast.13, s32[1]{0:T(128)} %bitcast.13, s32[1]{0:T(128)} %bitcast.13, s32[1]{0:T(128)} %bitcast.14, s32[1]{0:T(128)} %bitcast.14, s32[1]{0:T(128)} %bitcast.14, s32[1]{0:T(128)} %bitcast.15, s32[1]{0:T(128)} %bitcast.15, s32[1]{0:T(128)} %bitcast.15), dimensions={0} | concatenate | bytes 72 | tf_op jit(solution)/shard_map/stack | solution.py:77
  41.1 6.4 %stack.108 = s32[9]{0:T(128)} concatenate(s32[1]{0:T(128)} %bitcast.25, s32[1]{0:T(128)} %bitcast.26, s32[1]{0:T(128)} %bitcast.27, s32[1]{0:T(128)} %bitcast.25, s32[1]{0:T(128)} %bitcast.26, s32[1]{0:T(128)} %bitcast.27, s32[1]{0:T(128)} %bitcast.25, s32[1]{0:T(128)} %bitcast.26, s32[1]{0:T(128)} %bitcast.27), dimensions={0} | concatenate | bytes 72 | tf_op jit(solution)/shard_map/stack | solution.py:77
  49.5 28.3 %collective-permute-done.2 = bf16[2,3,1,384,384]{4,3,0,2,1:T(8,128)(2,1)} collective-permute-done((bf16[2,3,1,384,384]{4,3,0,2,1:T(8,128)(2,1)}, bf16[2,3,1,384,384]{4,3,0,2,1:T(8,128)(2,1)}, u32[]{:S(2)}, u32[]{:S(2)}) %collective-permute-start.2) | collective-permute-done | bytes 1769504 | tf_op jit(solution)/shard_map/ppermute | solution.py:24
  77.8 3.0 pad_maximum_fusion
  80.9 2.2 fusion.57
  87.4 45.0 %while.18 = (s32[]{:T(128)}, f32[384,384]{1,0:T(8,128)}, bf16[3456,384]{1,0:T(8,128)(2,1)}, bf16[3456,384]{1,0:T(8,128)(2,1)}, bf16[384,384]{0,1:T(8,128)(2,1)S(...) while((s32[]{:T(128)}, f32[384,384]{1,0:T(8,128)}, ...), condition=%wide.region_14.15_spmd.clone, body=%wide.region_10.14_spmd.clone.sunk | while | flops 2058498432 | bytes 74175752 | solution.py:136
  88.8 2.3 fusion.87
  97.1 3.4 convolution_dynamic-update-slice_fusion.6
  103.8 2.3 fusion.87
  112.1 3.4 convolution_dynamic-update-slice_fusion.6
  118.7 2.3 fusion.87
  127.1 3.4 convolution_dynamic-update-slice_fusion.6
  130.5 1.9 convolution_dynamic-update-slice_fusion.8
  132.4 3.1 pad_maximum_fusion.1
  137.2 4.8 %collective-permute-start.5 = (bf16[2,3,384,384]{3,2,0,1:T(8,128)(2,1)S(1)}, bf16[2,3,384,384]{3,2,0,1:T(8,128)(2,1)S(1)}, u32[]{:S(2)}, u32[]{:S(2)}) collective-permute-start(bf16[2,3,384,384]{3,2,0,1:T(8,128)(2,1)S(1)} %get-tuple-element.287), channel_id=1, source_target_pairs={{0,4},{4,8},{8,12},{12,16},{16,20},{20,24},{24,28},{1,5},{5,9},{9,... | collective-permute-start | bytes 5308424 | tf_op jit(solution)/shard_map/ppermute | solution.py:33
  142.3 33.8 %collective-permute-done.4 = bf16[2,3,384,384]{3,2,0,1:T(8,128)(2,1)S(1)} collective-permute-done((bf16[2,3,384,384]{3,2,0,1:T(8,128)(2,1)S(1)}, bf16[2,3,384,384]{3,2,0,1:T(8,128)(2,1)S(1)}, u32[]{:S(2)}, u32[]{:S(2)}) %collective-permute-start.4) | collective-permute-done | bytes 1769504 | tf_op jit(solution)/shard_map/ppermute | solution.py:33
  182.6 10.0 %collective-permute-start.7 = (bf16[2,3,384,384]{3,2,0,1:T(8,128)(2,1)}, bf16[2,3,384,384]{3,2,0,1:T(8,128)(2,1)}, u32[]{:S(2)}, u32[]{:S(2)}) collective-permute-start(bf16[2,3,384,384]{3,2,0,1:T(8,128)(2,1)} %pad_maximum_fusion.4), channel_id=1, source_target_pairs={{0,1},{1,2},{2,3},{4,5},{5,6},{6,7},{8,9},{9,10},{10,11},{12,13},{... | collective-permute-start | bytes 5308424 | tf_op jit(solution)/shard_map/ppermute | solution.py:33
  204.9 18.5 %collective-permute-done.6 = bf16[2,3,384,384]{3,2,0,1:T(8,128)(2,1)} collective-permute-done((bf16[2,3,384,384]{3,2,0,1:T(8,128)(2,1)}, bf16[2,3,384,384]{3,2,0,1:T(8,128)(2,1)}, u32[]{:S(2)}, u32[]{:S(2)}) %collective-permute-start.6) | collective-permute-done | bytes 1769504 | tf_op jit(solution)/shard_map/ppermute | solution.py:33
  225.3 36.2 %collective-permute-done.7 = bf16[2,3,384,384]{3,2,0,1:T(8,128)(2,1)} collective-permute-done((bf16[2,3,384,384]{3,2,0,1:T(8,128)(2,1)}, bf16[2,3,384,384]{3,2,0,1:T(8,128)(2,1)}, u32[]{:S(2)}, u32[]{:S(2)}) %collective-permute-start.7) | collective-permute-done | bytes 1769504 | tf_op jit(solution)/shard_map/ppermute | solution.py:33
  267.8 101.6 %psum.7 = f32[2,128]{1,0:T(2,128)S(1)} all-reduce(f32[2,128]{1,0:T(2,128)S(1)} %pad_maximum_fusion.5), channel_id=1, replica_groups=mesh['dp'=8,'tm'=8,'height'=4] {'dp','tm','height'}, use_global_device_ids=true, to_apply=%region_22.23 | all-reduce | flops 256 | bytes 2048 | tf_op jit(solution)/shard_map/psum | solution.py:198
  (171 shorter events, 73.6 us)
Async XLA Ops:
  1.8 23.5 %copy-start.2 = (f32[1,1,384,384]{2,3,1,0:T(8,128)}, f32[1,1,384,384]{2,3,1,0:T(8,128)S(1)}, u32[]{:S(2)}) copy-start(f32[1,1,384,384]{2,3,1,0:T(8,128)S(1)} %copy.59) | copy-start | bytes 1769476
  2.6 22.7 %copy-start.4 = (f32[384,3,128]{0,2,1:T(8,128)}, f32[384,3,128]{0,2,1:T(8,128)S(1)}, u32[]{:S(2)}) copy-start(f32[384,3,128]{0,2,1:T(8,128)S(1)} %mul.248) | copy-start | bytes 1769476
  3.5 28.3 %copy-start.14 = (bf16[1,1,384,384]{3,2,1,0:T(8,128)(2,1)S(1)}, bf16[1,1,384,384]{3,2,1,0:T(8,128)(2,1)}, u32[]{:S(2)}) copy-start(bf16[1,1,384,384]{3,2,1,0:T(8,128)(2,1)} %param.13) | copy-start | bytes 884740
  3.5 28.5 %copy-start.15 = (bf16[1,1,384,384]{3,2,1,0:T(8,128)(2,1)S(1)}, bf16[1,1,384,384]{3,2,1,0:T(8,128)(2,1)}, u32[]{:S(2)}) copy-start(bf16[1,1,384,384]{3,2,1,0:T(8,128)(2,1)} %param.10) | copy-start | bytes 884740
  3.6 28.8 %copy-start.27 = (f32[128]{0:T(128)S(1)}, f32[128]{0:T(128)}, u32[]{:S(2)}) copy-start(f32[128]{0:T(128)} %param.14) | copy-start | bytes 1540
  3.6 29.7 %copy-start.30 = (s32[8]{0:T(128)S(1)}, s32[8]{0:T(128)}, u32[]{:S(2)}) copy-start(s32[8]{0:T(128)} %param.16) | copy-start | bytes 100
  3.6 36.8 %copy-start.31 = (s32[4]{0:T(128)S(1)}, s32[4]{0:T(128)}, u32[]{:S(2)}) copy-start(s32[4]{0:T(128)} %param.17) | copy-start | bytes 52
  3.6 16.2 %collective-permute-start = (bf16[2,1,1,384,384]{4,3,0,2,1:T(8,128)(2,1)S(1)}, bf16[2,1,1,384,384]{4,3,0,2,1:T(8,128)(2,1)S(1)}, u32[]{:S(2)}, u32[]{:S(2)}) collective-permute-start(bf16[2,1,1,384,384]{4,3,0,2,1:T(8,128)(2,1)S(1)} %maximum_bitcast_fusion), channel_id=1, source_target_pairs={{0,4},{4,8},{8,12},{12,16},{16,20},{20,24},{24,28},{1,5},{5,9},{9,... | collective-permute-start | bytes 1769480 | tf_op jit(solution)/shard_map/ppermute | solution.py:24
  7.3 16.7 %collective-permute-start.1 = (bf16[2,1,1,384,384]{4,3,0,2,1:T(8,128)(2,1)S(1)}, bf16[2,1,1,384,384]{4,3,0,2,1:T(8,128)(2,1)S(1)}, u32[]{:S(2)}, u32[]{:S(2)}) collective-permute-start(bf16[2,1,1,384,384]{4,3,0,2,1:T(8,128)(2,1)S(1)} %maximum_bitcast_fusion), channel_id=1, source_target_pairs={{4,0},{8,4},{12,8},{16,12},{20,16},{24,20},{28,24},{5,1},{9,5},{13... | collective-permute-start | bytes 1769480 | tf_op jit(solution)/shard_map/ppermute | solution.py:25
  25.4 52.4 %collective-permute-start.2 = (bf16[2,3,1,384,384]{4,3,0,2,1:T(8,128)(2,1)}, bf16[2,3,1,384,384]{4,3,0,2,1:T(8,128)(2,1)}, u32[]{:S(2)}, u32[]{:S(2)}) collective-permute-start(bf16[2,3,1,384,384]{4,3,0,2,1:T(8,128)(2,1)} %pad_maximum_fusion.2), channel_id=1, source_target_pairs={{0,1},{1,2},{2,3},{4,5},{5,6},{6,7},{8,9},{9,10},{10,11},{12,13},{... | collective-permute-start | bytes 5308424 | tf_op jit(solution)/shard_map/ppermute | solution.py:24
  30.4 47.4 %collective-permute-start.3 = (bf16[2,3,1,384,384]{4,3,0,2,1:T(8,128)(2,1)}, bf16[2,3,1,384,384]{4,3,0,2,1:T(8,128)(2,1)}, u32[]{:S(2)}, u32[]{:S(2)}) collective-permute-start(bf16[2,3,1,384,384]{4,3,0,2,1:T(8,128)(2,1)} %pad_maximum_fusion.2), channel_id=1, source_target_pairs={{1,0},{2,1},{3,2},{5,4},{6,5},{7,6},{9,8},{10,9},{11,10},{13,12},{... | collective-permute-start | bytes 5308424 | tf_op jit(solution)/shard_map/ppermute | solution.py:25
  33.1 16.3 %copy-start.24 = (f32[384]{0:T(512)}, f32[384]{0:T(512)S(1)}, u32[]{:S(2)}) copy-start(f32[384]{0:T(512)S(1)} %broadcast_bitcast_fusion.1) | copy-start | bytes 4612
  33.1 16.3 %copy-start.17 = (f32[384,3]{0,1:T(4,128)}, f32[384,3]{0,1:T(4,128)S(1)}, u32[]{:S(2)}) copy-start(f32[384,3]{0,1:T(4,128)S(1)} %add_rsqrt_fusion.1) | copy-start | bytes 13828
  135.9 40.1 %collective-permute-start.4 = (bf16[2,3,384,384]{3,2,0,1:T(8,128)(2,1)S(1)}, bf16[2,3,384,384]{3,2,0,1:T(8,128)(2,1)S(1)}, u32[]{:S(2)}, u32[]{:S(2)}) collective-permute-start(bf16[2,3,384,384]{3,2,0,1:T(8,128)(2,1)S(1)} %get-tuple-element.286), channel_id=1, source_target_pairs={{4,0},{8,4},{12,8},{16,12},{20,16},{24,20},{28,24},{5,1},{9,5},{13... | collective-permute-start | bytes 5308424 | tf_op jit(solution)/shard_map/ppermute | solution.py:33
  137.2 40.0 %collective-permute-start.5 = (bf16[2,3,384,384]{3,2,0,1:T(8,128)(2,1)S(1)}, bf16[2,3,384,384]{3,2,0,1:T(8,128)(2,1)S(1)}, u32[]{:S(2)}, u32[]{:S(2)}) collective-permute-start(bf16[2,3,384,384]{3,2,0,1:T(8,128)(2,1)S(1)} %get-tuple-element.287), channel_id=1, source_target_pairs={{0,4},{4,8},{8,12},{12,16},{16,20},{20,24},{24,28},{1,5},{5,9},{9,... | collective-permute-start | bytes 5308424 | tf_op jit(solution)/shard_map/ppermute | solution.py:33
  179.7 14.0 %copy-start.18 = (f32[384,3]{0,1:T(4,128)S(1)}, f32[384,3]{0,1:T(4,128)}, u32[]{:S(2)}) copy-start(f32[384,3]{0,1:T(4,128)} %copy-done.17) | copy-start | bytes 13828
  179.7 43.7 %collective-permute-start.6 = (bf16[2,3,384,384]{3,2,0,1:T(8,128)(2,1)}, bf16[2,3,384,384]{3,2,0,1:T(8,128)(2,1)}, u32[]{:S(2)}, u32[]{:S(2)}) collective-permute-start(bf16[2,3,384,384]{3,2,0,1:T(8,128)(2,1)} %pad_maximum_fusion.3), channel_id=1, source_target_pairs={{1,0},{2,1},{3,2},{5,4},{6,5},{7,6},{9,8},{10,9},{11,10},{13,12},{... | collective-permute-start | bytes 5308424 | tf_op jit(solution)/shard_map/ppermute | solution.py:33
  182.6 14.9 %copy-start.5 = (f32[384,3,128]{0,2,1:T(8,128)S(1)}, f32[384,3,128]{0,2,1:T(8,128)}, u32[]{:S(2)}) copy-start(f32[384,3,128]{0,2,1:T(8,128)} %copy-done.4) | copy-start | bytes 1769476
  182.6 16.0 %copy-start.8 = (f32[384,384]{1,0:T(8,128)S(1)}, f32[384,384]{1,0:T(8,128)}, u32[]{:S(2)}) copy-start(f32[384,384]{1,0:T(8,128)} %get-tuple-element.160) | copy-start | bytes 1769476
  182.6 78.9 %collective-permute-start.7 = (bf16[2,3,384,384]{3,2,0,1:T(8,128)(2,1)}, bf16[2,3,384,384]{3,2,0,1:T(8,128)(2,1)}, u32[]{:S(2)}, u32[]{:S(2)}) collective-permute-start(bf16[2,3,384,384]{3,2,0,1:T(8,128)(2,1)} %pad_maximum_fusion.4), channel_id=1, source_target_pairs={{0,1},{1,2},{2,3},{4,5},{5,6},{6,7},{8,9},{9,10},{10,11},{12,13},{... | collective-permute-start | bytes 5308424 | tf_op jit(solution)/shard_map/ppermute | solution.py:33
  263.7 106.3 %copy-start.3 = (f32[1,1,384,384]{2,3,1,0:T(8,128)S(1)}, f32[1,1,384,384]{2,3,1,0:T(8,128)}, u32[]{:S(2)}) copy-start(f32[1,1,384,384]{2,3,1,0:T(8,128)} %copy-done.2) | copy-start | bytes 1769476
  263.7 106.3 %copy-start.29 = (f32[128]{0:T(128)S(1)}, f32[128]{0:T(128)}, u32[]{:S(2)}) copy-start(f32[128]{0:T(128)} %param.15) | copy-start | bytes 1540
  265.7 105.8 %copy-start.13 = (f32[1,1,384,384]{3,2,1,0:T(8,128)S(1)}, f32[1,1,384,384]{3,2,1,0:T(8,128)}, u32[]{:S(2)}) copy-start(f32[1,1,384,384]{3,2,1,0:T(8,128)} %copy.70) | copy-start | bytes 1769476
  265.7 105.8 %copy-start.26 = (f32[384]{0:T(512)S(1)}, f32[384]{0:T(512)}, u32[]{:S(2)}) copy-start(f32[384]{0:T(512)} %copy-done.25) | copy-start | bytes 4612
  (24 other events, 71.4 us)
where the time goes:
time: 376 us; the launch traced here: 372 us
  waiting for transfers between devices  132 us (35%)
  blocking collectives  102 us (27%)
  local copies, waits for them, and re-layouts  40.4 us (11%)
  other arithmetic  35.1 us (9%)
  matrix products  32.8 us (9%)
  starting transfers between devices  28.8 us (8%)
    psum x1, blocking collectives, on_device(): gain_total = lax.psum(gain_local, ('dp', 'tm', 'height'))  102 us
    ppermute x4, waiting for transfers between devices, shifted(): return lax.ppermute(block, axis, route)  88.7 us
    ppermute x2, waiting for transfers between devices, with_halo(): before = lax.ppermute(last, axis, up)  39.5 us
    ppermute x4, starting transfers between devices, shifted(): return lax.ppermute(block, axis, route)  17.5 us
    another operation x3, local copies, waits for them, and re-layouts, neighbours(): return (jnp.stack(present), jnp.stack(frame_limits), jnp.stack(row_limits))  13.4 us
    dot_general x3, matrix products, head_step(): jnp.dot(score_grad, k_head, preferred_element_type=jnp.float32)  10.2 us
    ppermute x2, starting transfers between devices, with_halo(): before = lax.ppermute(last, axis, up)  8.71 us
  transfers between devices with their start and end apart: 8, of which 7 were waited for; matrix products, arithmetic and copies ran while one was open for 9% of the time, Pallas kernels for 0%

commit v1 on v0

v1 whole, which is shorter than its diff:
```python
import functools
import math

import jax
import jax.numpy as jnp
from jax import lax
from jax.experimental import pallas as pl
from jax.experimental.pallas import tpu as pltpu
from jax.sharding import PartitionSpec as P

HD = 128
TF = 6
TH = 8
TW = 8
TILE = TF * TH * TW
NORM_EPSILON = 1e-06
SCALE = 1.0 / math.sqrt(HD)
LOG2E = math.log2(math.e)
CHUNK = 128
STEPS = (-1, 0, 1)


def valid_rows(shape, frame_limit, row_limit):
    token = lax.broadcasted_iota(jnp.int32, shape, 0)
    return ((token >> 6) < frame_limit) & (((token >> 3) & 7) < row_limit)


def unit_norm(raw):
    wide = raw.astype(jnp.float32)
    inverse = lax.rsqrt(jnp.mean(wide * wide, axis=-1, keepdims=True) + NORM_EPSILON)
    return wide * inverse, inverse


def norm_back(grad, unit, inverse, gain):
    shaped = grad * gain
    inner = jnp.mean(shaped * unit, axis=-1, keepdims=True)
    return inverse * (shaped - unit * inner)


def fold(x, op):
    return op(x.reshape(x.shape[0] // 8, 8, x.shape[1]), axis=0)


def attention_kernel(limits, query_gain, key_gain, queries, grads, *rest):
    tiles, rest = rest[:9], rest[9:]
    terms, rest = rest[:9], rest[9:]
    d_queries, gains, kn, probs, dps = rest
    q_unit, q_inverse = unit_norm(queries[...])
    gain_q = query_gain[...]
    gain_k = key_gain[...]
    qn = (q_unit * gain_q).astype(jnp.bfloat16)
    gm = jnp.where(
        valid_rows((TILE, HD), limits[4], limits[13]), grads[...], jnp.zeros_like(grads[...])
    )
    qt = qn.T
    gt = gm.T
    order = (4, 1, 7, 3, 5, 0, 2, 6, 8)

    top = jnp.full((1, TILE), -1e30, jnp.float32)
    total = jnp.zeros((1, TILE), jnp.float32)
    tops = {}
    for j in order:
        unit, _ = unit_norm(tiles[j][0])
        normed = (unit * gain_k).astype(jnp.bfloat16)
        kn[j] = normed
        bias = jnp.where(valid_rows((TILE, HD), limits[j], limits[9 + j]), 0.0, -1e30)
        tile_top = jnp.full((8, TILE), -1e30, jnp.float32)
        for c in range(0, TILE, CHUNK):
            s = jnp.dot(normed[c : c + CHUNK], qt, preferred_element_type=jnp.float32)
            b = bias[c : c + CHUNK]
            s = s * (SCALE * LOG2E) + jnp.concatenate([b, b, b], axis=1)
            probs[j, c : c + CHUNK] = s
            tile_top = jnp.maximum(tile_top, fold(s, jnp.max))
        new_top = jnp.maximum(top, jnp.max(tile_top, axis=0, keepdims=True))
        part = jnp.zeros((8, TILE), jnp.float32)
        for c in range(0, TILE, CHUNK):
            e = jnp.exp2(probs[j, c : c + CHUNK] - new_top)
            probs[j, c : c + CHUNK] = e
            part = part + fold(e, jnp.sum)
        total = total * jnp.exp2(top - new_top) + jnp.sum(part, axis=0, keepdims=True)
        top = new_top
        tops[j] = new_top

    inverse_total = 1.0 / total
    delta8 = jnp.zeros((8, TILE), jnp.float32)
    for j in order:
        factor = jnp.exp2(tops[j] - top) * inverse_total
        lows = []
        for c in range(0, TILE, CHUNK):
            dp = jnp.dot(tiles[j][1, c : c + CHUNK], gt, preferred_element_type=jnp.float32)
            p = probs[j, c : c + CHUNK] * factor
            low = p.astype(jnp.bfloat16)
            probs[j, c : c + CHUNK] = p
            dps[j, c : c + CHUNK] = dp
            delta8 = delta8 + fold(low.astype(jnp.float32) * dp, jnp.sum)
            dv = jnp.dot(low, gm, preferred_element_type=jnp.float32)
            terms[j][1, c : c + CHUNK] = dv.astype(jnp.bfloat16)
    delta = jnp.sum(delta8, axis=0, keepdims=True)

    dq_t = jnp.zeros((HD, TILE), jnp.float32)
    key_gain_sum = jnp.zeros((8, HD), jnp.float32)
    for j in order:
        unit, _ = unit_norm(tiles[j][0])
        for c in range(0, TILE, CHUNK):
            ds = (probs[j, c : c + CHUNK] * (dps[j, c : c + CHUNK] - delta) * SCALE).astype(
                jnp.bfloat16
            )
            dk = jnp.dot(ds, qn, preferred_element_type=jnp.float32).astype(jnp.bfloat16)
            terms[j][0, c : c + CHUNK] = dk
            key_gain_sum = key_gain_sum + fold(
                dk.astype(jnp.float32) * unit[c : c + CHUNK], jnp.sum
            )
            dq_t = dq_t + lax.dot_general(
                kn[j, c : c + CHUNK],
                ds,
                (((0,), (0,)), ((), ())),
                preferred_element_type=jnp.float32,
            )
    dq = dq_t.T
    d_queries[...] = norm_back(dq, q_unit, q_inverse, gain_q).astype(jnp.bfloat16)

    @pl.when(pl.program_id(0) == 0)
    def _():
        gains[...] = jnp.zeros_like(gains)

    gains[0:8] += fold(dq * q_unit, jnp.sum)
    gains[8:16] += key_gain_sum


def attention(limits, query_gain, key_gain, queries, grads, tiles):
    heads = queries.shape[1] // HD
    row = pl.BlockSpec((TILE, HD), lambda h: (0, h))
    pair = pl.BlockSpec((2, TILE, HD), lambda h: (0, 0, h))
    whole = pl.BlockSpec((1, HD), lambda h: (0, 0))
    pair_shape = jax.ShapeDtypeStruct((2,) + queries.shape, jnp.bfloat16)
    outs = pl.pallas_call(
        attention_kernel,
        grid=(heads,),
        in_specs=[pl.BlockSpec(memory_space=pltpu.SMEM), whole, whole, row, row] + [pair] * 9,
        out_specs=[pair] * 9 + [row, pl.BlockSpec((16, HD), lambda h: (0, 0))],
        out_shape=[pair_shape] * 9
        + [
            jax.ShapeDtypeStruct(queries.shape, jnp.bfloat16),
            jax.ShapeDtypeStruct((16, HD), jnp.float32),
        ],
        scratch_shapes=[
            pltpu.VMEM((9, TILE, HD), jnp.bfloat16),
            pltpu.VMEM((9, TILE, TILE), jnp.float32),
            pltpu.VMEM((9, TILE, TILE), jnp.float32),
        ],
        compiler_params=pltpu.CompilerParams(vmem_limit_bytes=48 * 2**20),
        cost_estimate=pl.CostEstimate(
            flops=heads * 10 * TILE * TILE * 9 * HD,
            bytes_accessed=40 * TILE * queries.shape[1] * 2,
            transcendentals=heads * 9 * TILE * TILE,
        ),
    )(limits, query_gain[None], key_gain[None], queries, grads, *tiles)
    return outs[:9], outs[9], outs[10]


def finish_kernel(key_gain, keys, *rest):
    parts, (d_keys, d_values) = rest[:-2], rest[-2:]
    total = parts[0][...].astype(jnp.float32)
    for part in parts[1:]:
        total = total + part[...].astype(jnp.float32)
    unit, inverse = unit_norm(keys[...])
    d_keys[...] = norm_back(total[0], unit, inverse, key_gain[...]).astype(jnp.bfloat16)
    d_values[...] = total[1].astype(jnp.bfloat16)


def finish(key_gain, keys, parts):
    heads = keys.shape[1] // HD
    row = pl.BlockSpec((TILE, HD), lambda h: (0, h))
    pair = pl.BlockSpec((2, TILE, HD), lambda h: (0, 0, h))
    whole = pl.BlockSpec((1, HD), lambda h: (0, 0))
    return pl.pallas_call(
        finish_kernel,
        grid=(heads,),
        in_specs=[whole, row] + [pair] * len(parts),
        out_specs=[row, row],
        out_shape=[jax.ShapeDtypeStruct(keys.shape, jnp.bfloat16)] * 2,
        compiler_params=pltpu.CompilerParams(vmem_limit_bytes=16 * 2**20),
    )(key_gain[None], keys, *parts)


def shifted(block, axis, distance):
    devices = range(lax.axis_size(axis))
    route = [(i - distance, i) for i in devices if i - distance in devices]
    return lax.ppermute(block, axis, route)


def total_over(x, axes):
    for axis in axes:
        size = lax.axis_size(axis)
        bit = 1
        while bit < size:
            x = x + lax.ppermute(x, axis, [(i, i ^ bit) for i in range(size)])
            bit *= 2
    return x


def window_limits(frame_counts, row_counts):
    time_index = lax.axis_index("tm")
    height_index = lax.axis_index("height")
    time_count = frame_counts.shape[0]
    height_count = row_counts.shape[0]
    frames = jnp.concatenate([jnp.zeros(1, jnp.int32), frame_counts, jnp.zeros(1, jnp.int32)])
    rows = jnp.concatenate([jnp.zeros(1, jnp.int32), row_counts, jnp.zeros(1, jnp.int32)])
    near_frames = lax.dynamic_slice_in_dim(frames, time_index, 3)
    near_rows = lax.dynamic_slice_in_dim(rows, height_index, 3)
    return jnp.concatenate([jnp.repeat(near_frames, 3), jnp.tile(near_rows, 3)])


def on_device(
    queries, key_vectors, value_vectors, out_grads, query_gain, key_gain, frame_counts, row_counts
):
    time_count = lax.axis_size("tm")
    height_count = lax.axis_size("height")
    row_count = queries.shape[2]
    feature_count = queries.shape[3]
    keys = key_vectors[0, 0]
    own = jnp.stack([keys, value_vectors[0, 0]])
    limits = window_limits(frame_counts, row_counts)

    tiles = {(0, 0): own}
    for a in (-1, 1):
        tiles[a, 0] = shifted(own, "tm", -a)
    for b in (-1, 1):
        tiles[0, b] = shifted(own, "height", -b)
    for a in (-1, 1):
        for b in (-1, 1):
            tiles[a, b] = shifted(tiles[a, 0], "height", -b)

    outs, d_queries, gain_parts = attention(
        limits,
        query_gain,
        key_gain,
        queries[0, 0],
        out_grads[0, 0],
        [tiles[a, b] for a in STEPS for b in STEPS],
    )
    terms = {(a, b): outs[3 * (a + 1) + b + 1] for a in STEPS for b in STEPS}

    landed = {}
    for a in (-1, 1, 0):
        for b in (-1, 1):
            landed[a, b] = shifted(terms[a, b], "height", b)
    parts = [terms[0, 0], landed[0, -1], landed[0, 1]]
    for a in (-1, 1):
        side = (
            terms[a, 0].astype(jnp.float32)
            + landed[a, -1].astype(jnp.float32)
            + landed[a, 1].astype(jnp.float32)
        ).astype(jnp.bfloat16)
        parts.append(shifted(side, "tm", a))
    d_keys, d_values = finish(key_gain, keys, parts)

    gain_local = jnp.sum(gain_parts.reshape(2, 8, HD), axis=1)
    gain_total = total_over(gain_local, ("dp", "tm", "height"))
    head_total = lax.axis_size("dp") * (feature_count // HD)
    scaling = 1.0 / math.sqrt(time_count * height_count * row_count * head_total)
    gain_grads = gain_total * scaling
    return (d_queries[None, None], d_keys[None, None], d_values[None, None], gain_grads)


def solution(mesh):
    split = P("tm", "height", None, "dp")
    return jax.shard_map(
        on_device,
        mesh=mesh,
        in_specs=(split,) * 4 + (P(),) * 4,
        out_specs=(split,) * 3 + (P(),),
        check_vma=False,
    )
```

time: 376 us -> 180 us (0.48)
  blocking collectives: 102 us -> 0 us
  waiting for transfers between devices: 132 us -> 62.1 us
  starting transfers between devices: 28.8 us -> 87.2 us
  local copies, waits for them, and re-layouts: 40.4 us -> 0.45 us
  matrix products: 32.8 us -> 0 us
  other arithmetic: 35.1 us -> 2.49 us
  Pallas kernels: 0 us -> 25 us
    psum x1 -> x0, blocking collectives: 102 us -> none  [on_device(): gain_total = lax.psum(gain_local, ('dp', 'tm', 'height'))]
    ppermute x4 -> x16, waiting for transfers between devices: 88.7 us -> 39.3 us  [shifted(): return lax.ppermute(block, axis, route)]
    ppermute x4 -> x16, starting transfers between devices: 17.5 us -> 55.4 us  [shifted(): return lax.ppermute(block, axis, route)]
    dot_general x18 -> x0, matrix products: 32.8 us -> none  [the longest x3 10.2 us: head_step(): jnp.dot(score_grad, k_head, preferred_element_type=jnp.float32)]
    pallas_call x0 -> x2, Pallas kernels: none -> 25 us  [the longest x1 22.7 us: attention(): pl.pallas_call(attention_kernel, grid=(heads,), in_specs=[pl.BlockSpec(me...]
    ppermute x4 -> x8, waiting for transfers between devices: 43.7 us -> 22.8 us  [total_over(): x = x + lax.ppermute(x, axis, [(i, i ^ bit) for i in range(size)])]
    ppermute x4 -> x8, starting transfers between devices: 11.3 us -> 31.8 us  [total_over(): x = x + lax.ppermute(x, axis, [(i, i ^ bit) for i in range(size)])]
    reduce_sum x14 -> x1, other arithmetic: 14.5 us -> 0.02 us  [on_device(): gain_local = jnp.sum(gain_parts.reshape(2, 8, HD), axis=1)]
  transfers between devices with their start and end apart: 8 -> 24, of which waited for: 7 -> 14; matrix products, arithmetic and copies ran while one was open for 9% -> 1% of each run, Pallas kernels for 0% -> 0%
where the time goes in v1:
time: 180 us; the launch traced here: 178 us
  starting transfers between devices  87.2 us (48%)
  waiting for transfers between devices  62.1 us (34%)
  Pallas kernels  25 us (14%)
  other arithmetic  2.49 us (1%)
    ppermute x16, starting transfers between devices, shifted(): return lax.ppermute(block, axis, route)  55.4 us
    ppermute x16, waiting for transfers between devices, shifted(): return lax.ppermute(block, axis, route)  39.3 us
    ppermute x8, starting transfers between devices, total_over(): x = x + lax.ppermute(x, axis, [(i, i ^ bit) for i in range(size)])  31.8 us
    ppermute x8, waiting for transfers between devices, total_over(): x = x + lax.ppermute(x, axis, [(i, i ^ bit) for i in range(size)])  22.8 us
    pallas_call x1, Pallas kernels, attention(): pl.pallas_call(attention_kernel, grid=(heads,), in_specs=[pl.BlockSpec(me...  22.7 us
  transfers between devices with their start and end apart: 24, of which 14 were waited for; matrix products, arithmetic and copies ran while one was open for 1% of the time, Pallas kernels for 0%

profile of v1, /device:TPU:2, one launch (start us, length us, event | category | flops | bytes accessed | tf_op | source)
XLA Modules:
  0.0 178.1 jit_solution(6000390413865613273)
XLA Ops:
  3.2 4.6 %collective-permute-start = (bf16[2,384,384]{2,1,0:T(8,128)(2,1)S(1)}, bf16[2,384,384]{2,1,0:T(8,128)(2,1)S(1)}, u32[]{:S(2)}, u32[]{:S(2)}) collective-permute-start(bf16[2,384,384]{2,1,0:T(8,128)(2,1)S(1)} %pad_maximum_fusion.rest_4_), channel_id=1, source_target_pairs={{0,4},{4,8},{8,12},{12,16},{16,20},{20,24},{24,28},{1,5},{5,9},{9,... | collective-permute-start | bytes 1769480 | tf_op jit(solution)/shard_map/ppermute | solution.py:189
  9.1 5.4 %collective-permute-start.3 = (bf16[2,384,384]{2,1,0:T(8,128)(2,1)S(1)}, bf16[2,384,384]{2,1,0:T(8,128)(2,1)}, u32[]{:S(2)}, u32[]{:S(2)}) collective-permute-start(bf16[2,384,384]{2,1,0:T(8,128)(2,1)S(1)} %pad_maximum_fusion.rest_4_), channel_id=1, source_target_pairs={{0,1},{1,2},{2,3},{4,5},{5,6},{6,7},{8,9},{9,10},{10,11},{12,13},{... | collective-permute-start | bytes 1769480 | tf_op jit(solution)/shard_map/ppermute | solution.py:189
  14.5 4.4 %collective-permute-done.5.rest_7_ = bf16[2,384,384]{2,1,0:T(8,128)(2,1)S(1)} collective-permute-done((bf16[2,384,384]{2,1,0:T(8,128)(2,1)S(1)}, bf16[2,384,384]{2,1,0:T(8,128)(2,1)S(1)}, u32[]{:S(2)}, u32[]{:S(2)}) %collective-permute-start.5) | collective-permute-done | bytes 589856 | tf_op jit(solution)/shard_map/ppermute | solution.py:189
  20.1 5.4 %collective-permute-start.6 = (bf16[2,384,384]{2,1,0:T(8,128)(2,1)S(1)}, bf16[2,384,384]{2,1,0:T(8,128)(2,1)}, u32[]{:S(2)}, u32[]{:S(2)}) collective-permute-start(bf16[2,384,384]{2,1,0:T(8,128)(2,1)S(1)} %collective-permute-done.5.rest_7_), channel_id=1, source_target_pairs={{0,1},{1,2},{2,3},{4,5},{5,6},{6,7},{8,9},{9,10},{10,11},{12,13},{... | collective-permute-start | bytes 1769480 | tf_op jit(solution)/shard_map/ppermute | solution.py:189
  26.8 14.8 %collective-permute-start.1 = (bf16[2,384,384]{2,1,0:T(8,128)(2,1)S(1)}, bf16[2,384,384]{2,1,0:T(8,128)(2,1)}, u32[]{:S(2)}, u32[]{:S(2)}) collective-permute-start(bf16[2,384,384]{2,1,0:T(8,128)(2,1)S(1)} %collective-permute-done.rest_1_), channel_id=1, source_target_pairs={{0,1},{1,2},{2,3},{4,5},{5,6},{6,7},{8,9},{9,10},{10,11},{12,13},{... | collective-permute-start | bytes 1769480 | tf_op jit(solution)/shard_map/ppermute | solution.py:189
  42.2 10.4 %collective-permute-done.6.rest_6_ = bf16[2,384,384]{2,1,0:T(8,128)(2,1)} collective-permute-done((bf16[2,384,384]{2,1,0:T(8,128)(2,1)S(1)}, bf16[2,384,384]{2,1,0:T(8,128)(2,1)}, u32[]{:S(2)}, u32[]{:S(2)}) %collective-permute-start.6) | collective-permute-done | bytes 589856 | tf_op jit(solution)/shard_map/ppermute | solution.py:189
  52.6 10.8 %collective-permute-done.1.rest_0_ = bf16[2,384,384]{2,1,0:T(8,128)(2,1)} collective-permute-done((bf16[2,384,384]{2,1,0:T(8,128)(2,1)S(1)}, bf16[2,384,384]{2,1,0:T(8,128)(2,1)}, u32[]{:S(2)}, u32[]{:S(2)}) %collective-permute-start.1) | collective-permute-done | bytes 589856 | tf_op jit(solution)/shard_map/ppermute | solution.py:189
  63.5 22.7 %shard_map.111 = (bf16[2,384,384]{2,1,0:T(8,128)(2,1)S(1)}, bf16[2,384,384]{2,1,0:T(8,128)(2,1)S(1)}, bf16[2,384,384]{2,1,0:T(8,128)(2,1)S(1)}, bf16[2,384,384]{...) custom-call(s32[18]{0:T(128)S(1)} %pad_add_fusion.2.limits, ...), custom_call_target="tpu_custom_call" | custom-call | flops 5096079360 | bytes 11796480 | tf_op jit(solution)/shard_map/pallas_call | solution.py:136
  87.5 5.2 %collective-permute-start.11 = (bf16[2,384,384]{2,1,0:T(8,128)(2,1)S(1)}, bf16[2,384,384]{2,1,0:T(8,128)(2,1)S(1)}, u32[]{:S(2)}, u32[]{:S(2)}) collective-permute-start(bf16[2,384,384]{2,1,0:T(8,128)(2,1)S(1)} %get-tuple-element.23), channel_id=1, source_target_pairs={{0,1},{1,2},{2,3},{4,5},{5,6},{6,7},{8,9},{9,10},{10,11},{12,13},{... | collective-permute-start | bytes 1769480 | tf_op jit(solution)/shard_map/ppermute | solution.py:189
  94.0 4.6 %collective-permute-start.14 = (bf16[2,384,384]{2,1,0:T(8,128)(2,1)S(1)}, bf16[2,384,384]{2,1,0:T(8,128)(2,1)S(1)}, u32[]{:S(2)}, u32[]{:S(2)}) collective-permute-start(bf16[2,384,384]{2,1,0:T(8,128)(2,1)S(1)} %get-tuple-element.26), channel_id=1, source_target_pairs={{0,1},{1,2},{2,3},{4,5},{5,6},{6,7},{8,9},{9,10},{10,11},{12,13},{... | collective-permute-start | bytes 1769480 | tf_op jit(solution)/shard_map/ppermute | solution.py:189
  99.9 5.1 %collective-permute-done.10 = bf16[2,384,384]{2,1,0:T(8,128)(2,1)S(1)} collective-permute-done((bf16[2,384,384]{2,1,0:T(8,128)(2,1)S(1)}, bf16[2,384,384]{2,1,0:T(8,128)(2,1)S(1)}, u32[]{:S(2)}, u32[]{:S(2)}) %collective-permute-start.10) | collective-permute-done | bytes 589856 | tf_op jit(solution)/shard_map/ppermute | solution.py:189
  104.9 3.9 %collective-permute-start.9 = (bf16[2,384,384]{2,1,0:T(8,128)(2,1)S(1)}, bf16[2,384,384]{2,1,0:T(8,128)(2,1)S(1)}, u32[]{:S(2)}, u32[]{:S(2)}) collective-permute-start(bf16[2,384,384]{2,1,0:T(8,128)(2,1)S(1)} %get-tuple-element.20), channel_id=1, source_target_pairs={{0,1},{1,2},{2,3},{4,5},{5,6},{6,7},{8,9},{9,10},{10,11},{12,13},{... | collective-permute-start | bytes 1769480 | tf_op jit(solution)/shard_map/ppermute | solution.py:189
  110.4 7.1 %collective-permute-done.13 = bf16[2,384,384]{2,1,0:T(8,128)(2,1)S(1)} collective-permute-done((bf16[2,384,384]{2,1,0:T(8,128)(2,1)S(1)}, bf16[2,384,384]{2,1,0:T(8,128)(2,1)S(1)}, u32[]{:S(2)}, u32[]{:S(2)}) %collective-permute-start.13) | collective-permute-done | bytes 589856 | tf_op jit(solution)/shard_map/ppermute | solution.py:189
  122.4 3.0 %collective-permute-done.17 = f32[2,128]{1,0:T(2,128)S(1)} collective-permute-done((f32[2,128]{1,0:T(2,128)S(1)}, f32[2,128]{1,0:T(2,128)S(1)}, u32[]{:S(2)}, u32[]{:S(2)}) %collective-permute-start.17) | collective-permute-done | bytes 1056 | tf_op jit(solution)/shard_map/ppermute | solution.py:197
  125.4 2.1 %collective-permute-start.18 = (f32[2,128]{1,0:T(2,128)S(1)}, f32[2,128]{1,0:T(2,128)S(1)}, u32[]{:S(2)}, u32[]{:S(2)}) collective-permute-start(f32[2,128]{1,0:T(2,128)S(1)} %add.49), channel_id=1, source_target_pairs={{0,128},{32,160},{64,192},{96,224},{128,0},{160,32},{192,64},{224,... | collective-permute-start | bytes 3080 | tf_op jit(solution)/shard_map/ppermute | solution.py:197
  127.6 2.9 %collective-permute-done.18 = f32[2,128]{1,0:T(2,128)S(1)} collective-permute-done((f32[2,128]{1,0:T(2,128)S(1)}, f32[2,128]{1,0:T(2,128)S(1)}, u32[]{:S(2)}, u32[]{:S(2)}) %collective-permute-start.18) | collective-permute-done | bytes 1056 | tf_op jit(solution)/shard_map/ppermute | solution.py:197
  130.5 3.6 %collective-permute-done.19 = f32[2,128]{1,0:T(2,128)S(1)} collective-permute-done((f32[2,128]{1,0:T(2,128)S(1)}, f32[2,128]{1,0:T(2,128)S(1)}, u32[]{:S(2)}, u32[]{:S(2)}) %collective-permute-start.19) | collective-permute-done | bytes 1056 | tf_op jit(solution)/shard_map/ppermute | solution.py:197
  134.1 20.2 %collective-permute-start.20 = (f32[2,128]{1,0:T(2,128)S(1)}, f32[2,128]{1,0:T(2,128)S(1)}, u32[]{:S(2)}, u32[]{:S(2)}) collective-permute-start(f32[2,128]{1,0:T(2,128)S(1)} %add.51), channel_id=1, source_target_pairs={{0,8},{4,12},{8,0},{12,4},{16,24},{20,28},{24,16},{28,20},{1,9},{5... | collective-permute-start | bytes 3080 | tf_op jit(solution)/shard_map/ppermute | solution.py:197
  154.3 1.5 collective-permute-done.20
  155.8 7.5 %collective-permute-done.21 = f32[2,128]{1,0:T(2,128)S(1)} collective-permute-done((f32[2,128]{1,0:T(2,128)S(1)}, f32[2,128]{1,0:T(2,128)S(1)}, u32[]{:S(2)}, u32[]{:S(2)}) %collective-permute-start.21) | collective-permute-done | bytes 1056 | tf_op jit(solution)/shard_map/ppermute | solution.py:197
  163.3 4.0 %collective-permute-start.22 = (f32[2,128]{1,0:T(2,128)S(1)}, f32[2,128]{1,0:T(2,128)S(1)}, u32[]{:S(2)}, u32[]{:S(2)}) collective-permute-start(f32[2,128]{1,0:T(2,128)S(1)} %add.53), channel_id=1, source_target_pairs={{0,1},{1,0},{2,3},{3,2},{4,5},{5,4},{6,7},{7,6},{8,9},{9,8},{10,11... | collective-permute-start | bytes 3080 | tf_op jit(solution)/shard_map/ppermute | solution.py:197
  167.3 1.5 collective-permute-done.22
  168.8 4.8 %collective-permute-start.23 = (f32[2,128]{1,0:T(2,128)S(1)}, f32[2,128]{1,0:T(2,128)S(1)}, u32[]{:S(2)}, u32[]{:S(2)}) collective-permute-start(f32[2,128]{1,0:T(2,128)S(1)} %add.54), channel_id=1, source_target_pairs={{0,2},{1,3},{2,0},{3,1},{4,6},{5,7},{6,4},{7,5},{8,10},{9,11},{10,... | collective-permute-start | bytes 3080 | tf_op jit(solution)/shard_map/ppermute | solution.py:197
  175.8 2.2 %shard_map.112 = (bf16[384,384]{1,0:T(8,128)(2,1)}, bf16[384,384]{1,0:T(8,128)(2,1)}) custom-call(f32[1,128]{1,0:T(1,128)S(1)} %bitcast.15, bf16[384,384]{1,0:T(8,128)(2,1)S(1)} %bitcast.13, bf16[2,384,384]{2,1,0:T(8,128)(2,1)S(1)} %get-tuple-element.18.rest_0_, bf16[2,384,384]{2,1,0:T(8,128)(2,1)S(1)} %collective-permute-done.8.rest_1_, ...), custom_call_target="tpu_custom_call" | custom-call | tf_op jit(solution)/shard_map/pallas_call | solution.py:176
  (69 shorter events, 19.3 us)
Async XLA Ops:
  1.9 17.0 %collective-permute-start.5 = (bf16[2,384,384]{2,1,0:T(8,128)(2,1)S(1)}, bf16[2,384,384]{2,1,0:T(8,128)(2,1)S(1)}, u32[]{:S(2)}, u32[]{:S(2)}) collective-permute-start(bf16[2,384,384]{2,1,0:T(8,128)(2,1)S(1)} %pad_maximum_fusion.rest_4_), channel_id=1, source_target_pairs={{4,0},{8,4},{12,8},{16,12},{20,16},{24,20},{28,24},{5,1},{9,5},{13... | collective-permute-start | bytes 1769480 | tf_op jit(solution)/shard_map/ppermute | solution.py:189
  3.2 22.3 %collective-permute-start = (bf16[2,384,384]{2,1,0:T(8,128)(2,1)S(1)}, bf16[2,384,384]{2,1,0:T(8,128)(2,1)S(1)}, u32[]{:S(2)}, u32[]{:S(2)}) collective-permute-start(bf16[2,384,384]{2,1,0:T(8,128)(2,1)S(1)} %pad_maximum_fusion.rest_4_), channel_id=1, source_target_pairs={{0,4},{4,8},{8,12},{12,16},{16,20},{20,24},{24,28},{1,5},{5,9},{9,... | collective-permute-start | bytes 1769480 | tf_op jit(solution)/shard_map/ppermute | solution.py:189
  7.8 19.0 %collective-permute-start.4 = (bf16[2,384,384]{2,1,0:T(8,128)(2,1)S(1)}, bf16[2,384,384]{2,1,0:T(8,128)(2,1)S(1)}, u32[]{:S(2)}, u32[]{:S(2)}) collective-permute-start(bf16[2,384,384]{2,1,0:T(8,128)(2,1)S(1)} %pad_maximum_fusion.rest_4_), channel_id=1, source_target_pairs={{1,0},{2,1},{3,2},{5,4},{6,5},{7,6},{9,8},{10,9},{11,10},{13,12},{... | collective-permute-start | bytes 1769480 | tf_op jit(solution)/shard_map/ppermute | solution.py:189
  9.1 33.1 %collective-permute-start.3 = (bf16[2,384,384]{2,1,0:T(8,128)(2,1)S(1)}, bf16[2,384,384]{2,1,0:T(8,128)(2,1)}, u32[]{:S(2)}, u32[]{:S(2)}) collective-permute-start(bf16[2,384,384]{2,1,0:T(8,128)(2,1)S(1)} %pad_maximum_fusion.rest_4_), channel_id=1, source_target_pairs={{0,1},{1,2},{2,3},{4,5},{5,6},{6,7},{8,9},{9,10},{10,11},{12,13},{... | collective-permute-start | bytes 1769480 | tf_op jit(solution)/shard_map/ppermute | solution.py:189
  18.8 23.4 %collective-permute-start.7 = (bf16[2,384,384]{2,1,0:T(8,128)(2,1)S(1)}, bf16[2,384,384]{2,1,0:T(8,128)(2,1)}, u32[]{:S(2)}, u32[]{:S(2)}) collective-permute-start(bf16[2,384,384]{2,1,0:T(8,128)(2,1)S(1)} %collective-permute-done.5.rest_7_), channel_id=1, source_target_pairs={{1,0},{2,1},{3,2},{5,4},{6,5},{7,6},{9,8},{10,9},{11,10},{13,12},{... | collective-permute-start | bytes 1769480 | tf_op jit(solution)/shard_map/ppermute | solution.py:189
  20.1 32.4 %collective-permute-start.6 = (bf16[2,384,384]{2,1,0:T(8,128)(2,1)S(1)}, bf16[2,384,384]{2,1,0:T(8,128)(2,1)}, u32[]{:S(2)}, u32[]{:S(2)}) collective-permute-start(bf16[2,384,384]{2,1,0:T(8,128)(2,1)S(1)} %collective-permute-done.5.rest_7_), channel_id=1, source_target_pairs={{0,1},{1,2},{2,3},{4,5},{5,6},{6,7},{8,9},{9,10},{10,11},{12,13},{... | collective-permute-start | bytes 1769480 | tf_op jit(solution)/shard_map/ppermute | solution.py:189
  25.5 27.1 %collective-permute-start.2 = (bf16[2,384,384]{2,1,0:T(8,128)(2,1)S(1)}, bf16[2,384,384]{2,1,0:T(8,128)(2,1)}, u32[]{:S(2)}, u32[]{:S(2)}) collective-permute-start(bf16[2,384,384]{2,1,0:T(8,128)(2,1)S(1)} %collective-permute-done.rest_1_), channel_id=1, source_target_pairs={{1,0},{2,1},{3,2},{5,4},{6,5},{7,6},{9,8},{10,9},{11,10},{13,12},{... | collective-permute-start | bytes 1769480 | tf_op jit(solution)/shard_map/ppermute | solution.py:189
  26.8 36.6 %collective-permute-start.1 = (bf16[2,384,384]{2,1,0:T(8,128)(2,1)S(1)}, bf16[2,384,384]{2,1,0:T(8,128)(2,1)}, u32[]{:S(2)}, u32[]{:S(2)}) collective-permute-start(bf16[2,384,384]{2,1,0:T(8,128)(2,1)S(1)} %collective-permute-done.rest_1_), channel_id=1, source_target_pairs={{0,1},{1,2},{2,3},{4,5},{5,6},{6,7},{8,9},{9,10},{10,11},{12,13},{... | collective-permute-start | bytes 1769480 | tf_op jit(solution)/shard_map/ppermute | solution.py:189
  86.2 18.7 %collective-permute-start.10 = (bf16[2,384,384]{2,1,0:T(8,128)(2,1)S(1)}, bf16[2,384,384]{2,1,0:T(8,128)(2,1)S(1)}, u32[]{:S(2)}, u32[]{:S(2)}) collective-permute-start(bf16[2,384,384]{2,1,0:T(8,128)(2,1)S(1)} %get-tuple-element.22), channel_id=1, source_target_pairs={{1,0},{2,1},{3,2},{5,4},{6,5},{7,6},{9,8},{10,9},{11,10},{13,12},{... | collective-permute-start | bytes 1769480 | tf_op jit(solution)/shard_map/ppermute | solution.py:189
  87.5 21.4 %collective-permute-start.11 = (bf16[2,384,384]{2,1,0:T(8,128)(2,1)S(1)}, bf16[2,384,384]{2,1,0:T(8,128)(2,1)S(1)}, u32[]{:S(2)}, u32[]{:S(2)}) collective-permute-start(bf16[2,384,384]{2,1,0:T(8,128)(2,1)S(1)} %get-tuple-element.23), channel_id=1, source_target_pairs={{0,1},{1,2},{2,3},{4,5},{5,6},{6,7},{8,9},{9,10},{10,11},{12,13},{... | collective-permute-start | bytes 1769480 | tf_op jit(solution)/shard_map/ppermute | solution.py:189
  92.7 24.9 %collective-permute-start.13 = (bf16[2,384,384]{2,1,0:T(8,128)(2,1)S(1)}, bf16[2,384,384]{2,1,0:T(8,128)(2,1)S(1)}, u32[]{:S(2)}, u32[]{:S(2)}) collective-permute-start(bf16[2,384,384]{2,1,0:T(8,128)(2,1)S(1)} %get-tuple-element.25), channel_id=1, source_target_pairs={{1,0},{2,1},{3,2},{5,4},{6,5},{7,6},{9,8},{10,9},{11,10},{13,12},{... | collective-permute-start | bytes 1769480 | tf_op jit(solution)/shard_map/ppermute | solution.py:189
  94.0 25.1 %collective-permute-start.14 = (bf16[2,384,384]{2,1,0:T(8,128)(2,1)S(1)}, bf16[2,384,384]{2,1,0:T(8,128)(2,1)S(1)}, u32[]{:S(2)}, u32[]{:S(2)}) collective-permute-start(bf16[2,384,384]{2,1,0:T(8,128)(2,1)S(1)} %get-tuple-element.26), channel_id=1, source_target_pairs={{0,1},{1,2},{2,3},{4,5},{5,6},{6,7},{8,9},{9,10},{10,11},{12,13},{... | collective-permute-start | bytes 1769480 | tf_op jit(solution)/shard_map/ppermute | solution.py:189
  98.6 77.2 %collective-permute-start.8 = (bf16[2,384,384]{2,1,0:T(8,128)(2,1)S(1)}, bf16[2,384,384]{2,1,0:T(8,128)(2,1)S(1)}, u32[]{:S(2)}, u32[]{:S(2)}) collective-permute-start(bf16[2,384,384]{2,1,0:T(8,128)(2,1)S(1)} %get-tuple-element.19), channel_id=1, source_target_pairs={{1,0},{2,1},{3,2},{5,4},{6,5},{7,6},{9,8},{10,9},{11,10},{13,12},{... | collective-permute-start | bytes 1769480 | tf_op jit(solution)/shard_map/ppermute | solution.py:189
  104.9 70.9 %collective-permute-start.9 = (bf16[2,384,384]{2,1,0:T(8,128)(2,1)S(1)}, bf16[2,384,384]{2,1,0:T(8,128)(2,1)S(1)}, u32[]{:S(2)}, u32[]{:S(2)}) collective-permute-start(bf16[2,384,384]{2,1,0:T(8,128)(2,1)S(1)} %get-tuple-element.20), channel_id=1, source_target_pairs={{0,1},{1,2},{2,3},{4,5},{5,6},{6,7},{8,9},{9,10},{10,11},{12,13},{... | collective-permute-start | bytes 1769480 | tf_op jit(solution)/shard_map/ppermute | solution.py:189
  109.1 66.7 %collective-permute-start.12 = (bf16[2,384,384]{2,1,0:T(8,128)(2,1)S(1)}, bf16[2,384,384]{2,1,0:T(8,128)(2,1)S(1)}, u32[]{:S(2)}, u32[]{:S(2)}) collective-permute-start(bf16[2,384,384]{2,1,0:T(8,128)(2,1)S(1)} %add_convert_fusion.1), channel_id=1, source_target_pairs={{4,0},{8,4},{12,8},{16,12},{20,16},{24,20},{28,24},{5,1},{9,5},{13... | collective-permute-start | bytes 1769480 | tf_op jit(solution)/shard_map/ppermute | solution.py:189
  119.3 56.5 %collective-permute-start.15 = (bf16[2,384,384]{2,1,0:T(8,128)(2,1)S(1)}, bf16[2,384,384]{2,1,0:T(8,128)(2,1)S(1)}, u32[]{:S(2)}, u32[]{:S(2)}) collective-permute-start(bf16[2,384,384]{2,1,0:T(8,128)(2,1)S(1)} %add_convert_fusion), channel_id=1, source_target_pairs={{0,4},{4,8},{8,12},{12,16},{16,20},{20,24},{24,28},{1,5},{5,9},{9,... | collective-permute-start | bytes 1769480 | tf_op jit(solution)/shard_map/ppermute | solution.py:189
  120.6 1.2 collective-permute-start.16
  121.9 3.6 %collective-permute-start.17 = (f32[2,128]{1,0:T(2,128)S(1)}, f32[2,128]{1,0:T(2,128)S(1)}, u32[]{:S(2)}, u32[]{:S(2)}) collective-permute-start(f32[2,128]{1,0:T(2,128)S(1)} %add.48), channel_id=1, source_target_pairs={{0,64},{32,96},{64,0},{96,32},{128,192},{160,224},{192,128},{224,1... | collective-permute-start | bytes 3080 | tf_op jit(solution)/shard_map/ppermute | solution.py:197
  125.4 5.1 %collective-permute-start.18 = (f32[2,128]{1,0:T(2,128)S(1)}, f32[2,128]{1,0:T(2,128)S(1)}, u32[]{:S(2)}, u32[]{:S(2)}) collective-permute-start(f32[2,128]{1,0:T(2,128)S(1)} %add.49), channel_id=1, source_target_pairs={{0,128},{32,160},{64,192},{96,224},{128,0},{160,32},{192,64},{224,... | collective-permute-start | bytes 3080 | tf_op jit(solution)/shard_map/ppermute | solution.py:197
  130.5 3.6 %collective-permute-start.19 = (f32[2,128]{1,0:T(2,128)S(1)}, f32[2,128]{1,0:T(2,128)S(1)}, u32[]{:S(2)}, u32[]{:S(2)}) collective-permute-start(f32[2,128]{1,0:T(2,128)S(1)} %add.50), channel_id=1, source_target_pairs={{0,4},{4,0},{8,12},{12,8},{16,20},{20,16},{24,28},{28,24},{1,5},{5... | collective-permute-start | bytes 3080 | tf_op jit(solution)/shard_map/ppermute | solution.py:197
  134.1 21.7 %collective-permute-start.20 = (f32[2,128]{1,0:T(2,128)S(1)}, f32[2,128]{1,0:T(2,128)S(1)}, u32[]{:S(2)}, u32[]{:S(2)}) collective-permute-start(f32[2,128]{1,0:T(2,128)S(1)} %add.51), channel_id=1, source_target_pairs={{0,8},{4,12},{8,0},{12,4},{16,24},{20,28},{24,16},{28,20},{1,9},{5... | collective-permute-start | bytes 3080 | tf_op jit(solution)/shard_map/ppermute | solution.py:197
  155.8 7.5 %collective-permute-start.21 = (f32[2,128]{1,0:T(2,128)S(1)}, f32[2,128]{1,0:T(2,128)S(1)}, u32[]{:S(2)}, u32[]{:S(2)}) collective-permute-start(f32[2,128]{1,0:T(2,128)S(1)} %add.52), channel_id=1, source_target_pairs={{0,16},{4,20},{8,24},{12,28},{16,0},{20,4},{24,8},{28,12},{1,17},{... | collective-permute-start | bytes 3080 | tf_op jit(solution)/shard_map/ppermute | solution.py:197
  163.3 5.5 %collective-permute-start.22 = (f32[2,128]{1,0:T(2,128)S(1)}, f32[2,128]{1,0:T(2,128)S(1)}, u32[]{:S(2)}, u32[]{:S(2)}) collective-permute-start(f32[2,128]{1,0:T(2,128)S(1)} %add.53), channel_id=1, source_target_pairs={{0,1},{1,0},{2,3},{3,2},{4,5},{5,4},{6,7},{7,6},{8,9},{9,8},{10,11... | collective-permute-start | bytes 3080 | tf_op jit(solution)/shard_map/ppermute | solution.py:197
  168.8 6.4 %collective-permute-start.23 = (f32[2,128]{1,0:T(2,128)S(1)}, f32[2,128]{1,0:T(2,128)S(1)}, u32[]{:S(2)}, u32[]{:S(2)}) collective-permute-start(f32[2,128]{1,0:T(2,128)S(1)} %add.54), channel_id=1, source_target_pairs={{0,2},{1,3},{2,0},{3,1},{4,6},{5,7},{6,4},{7,5},{8,10},{9,11},{10,... | collective-permute-start | bytes 3080 | tf_op jit(solution)/shard_map/ppermute | solution.py:197
  (11 other events, 570.7 us)

commit v2 on v1

v2 whole, which is shorter than its diff:
```python
import functools
import math

import jax
import jax.numpy as jnp
from jax import lax
from jax.experimental import pallas as pl
from jax.experimental.pallas import tpu as pltpu
from jax.sharding import PartitionSpec as P

HD = 128
TF = 6
TH = 8
TW = 8
TILE = TF * TH * TW
NORM_EPSILON = 1e-06
SCALE = 1.0 / math.sqrt(HD)
LOG2E = math.log2(math.e)
CHUNK = 128


def valid_rows(shape, frame_limit, row_limit):
    token = lax.broadcasted_iota(jnp.int32, shape, 0)
    return ((token >> 6) < frame_limit) & (((token >> 3) & 7) < row_limit)


def unit_norm(raw):
    wide = raw.astype(jnp.float32)
    inverse = lax.rsqrt(jnp.mean(wide * wide, axis=-1, keepdims=True) + NORM_EPSILON)
    return wide * inverse, inverse


def norm_back(grad, unit, inverse, gain):
    shaped = grad * gain
    inner = jnp.mean(shaped * unit, axis=-1, keepdims=True)
    return inverse * (shaped - unit * inner)


def fold(x, op):
    return op(x.reshape(x.shape[0] // 8, 8, x.shape[1]), axis=0)


def near(table, index):
    last = table.shape[0] - 1
    even = index % 2 == 0
    below = jnp.where(index == 0, 0, table[jnp.maximum(index - 1, 0)])
    above = jnp.where(index == last, 0, table[jnp.minimum(index + 1, last)])
    return table[index], jnp.where(even, above, below), jnp.where(even, below, above)


def attention_kernel(frame_counts, row_counts, query_gain, key_gain, queries, grads, *rest):
    ins, (own, h_even, h_odd, ce, te, co, to, x_even, x_odd, d_queries, gains), scratch = (
        rest[:14],
        rest[14:25],
        rest[25:],
    )
    keys, values, t_even, tk_odd, tv_odd, he, ho, c_even, c_odd, vx, zke, zko, zve, zvo = ins
    kn, probs, dps = scratch
    time_index = lax.axis_index("tm")
    across = (time_index == 3) | (time_index == 4)
    f, fe, fo = near(frame_counts, time_index)
    r, re, ro = near(row_counts, lax.axis_index("height"))
    frames = (f, fe, fo, f, f, fe, fe, fo, fo)
    rows = (r, r, r, re, ro, re, ro, re, ro)

    def pick_keys(j):
        if j in (7, 8):
            return jnp.where(across, {7: zke, 8: zko}[j][...], c_odd[j - 7, 0])
        if j in (0, 2):
            return {0: keys, 2: tk_odd}[j][...]
        return {1: t_even, 3: he, 4: ho, 5: c_even.at[0], 6: c_even.at[1]}[j][0]

    def pick_values(j):
        if j in (2, 7, 8):
            plain = tv_odd[...] if j == 2 else c_odd[j - 7, 1]
            return jnp.where(across, {2: vx, 7: zve, 8: zvo}[j][...], plain)
        if j == 0:
            return values[...]
        return {1: t_even, 3: he, 4: ho, 5: c_even.at[0], 6: c_even.at[1]}[j][1]

    targets = {
        0: (own,),
        1: (te,),
        2: (to,),
        3: (h_even,),
        4: (h_odd,),
        5: (ce.at[0],),
        6: (ce.at[1],),
        7: (co.at[0], x_even),
        8: (co.at[1], x_odd),
    }

    q_unit, q_inverse = unit_norm(queries[...])
    gain_q = query_gain[...]
    gain_k = key_gain[...]
    qn = (q_unit * gain_q).astype(jnp.bfloat16)
    gm = jnp.where(
        valid_rows((TILE, HD), f, r), grads[...], jnp.zeros_like(grads[...])
    )
    qt = qn.T
    gt = gm.T

    top = jnp.full((1, TILE), -1e30, jnp.float32)
    total = jnp.zeros((1, TILE), jnp.float32)
    tops = {}
    for j in range(9):
        unit, _ = unit_norm(pick_keys(j))
        normed = (unit * gain_k).astype(jnp.bfloat16)
        kn[j] = normed
        bias = jnp.where(valid_rows((TILE, HD), frames[j], rows[j]), 0.0, -1e30)
        tile_top = jnp.full((8, TILE), -1e30, jnp.float32)
        for c in range(0, TILE, CHUNK):
            s = jnp.dot(normed[c : c + CHUNK], qt, preferred_element_type=jnp.float32)
            b = bias[c : c + CHUNK]
            s = s * (SCALE * LOG2E) + jnp.concatenate([b, b, b], axis=1)
            probs[j, c : c + CHUNK] = s
            tile_top = jnp.maximum(tile_top, fold(s, jnp.max))
        new_top = jnp.maximum(top, jnp.max(tile_top, axis=0, keepdims=True))
        part = jnp.zeros((8, TILE), jnp.float32)
        for c in range(0, TILE, CHUNK):
            e = jnp.exp2(probs[j, c : c + CHUNK] - new_top)
            probs[j, c : c + CHUNK] = e
            part = part + fold(e, jnp.sum)
        total = total * jnp.exp2(top - new_top) + jnp.sum(part, axis=0, keepdims=True)
        top = new_top
        tops[j] = new_top

    inverse_total = 1.0 / total
    delta8 = jnp.zeros((8, TILE), jnp.float32)
    for j in range(9):
        factor = jnp.exp2(tops[j] - top) * inverse_total
        v = pick_values(j)
        for c in range(0, TILE, CHUNK):
            dp = jnp.dot(v[c : c + CHUNK], gt, preferred_element_type=jnp.float32)
            p = probs[j, c : c + CHUNK] * factor
            low = p.astype(jnp.bfloat16)
            probs[j, c : c + CHUNK] = p
            dps[j, c : c + CHUNK] = dp
            delta8 = delta8 + fold(low.astype(jnp.float32) * dp, jnp.sum)
            dv = jnp.dot(low, gm, preferred_element_type=jnp.float32).astype(jnp.bfloat16)
            for target in targets[j]:
                target[1, c : c + CHUNK] = dv
    delta = jnp.sum(delta8, axis=0, keepdims=True)

    dq_t = jnp.zeros((HD, TILE), jnp.float32)
    key_gain_sum = jnp.zeros((8, HD), jnp.float32)
    for j in range(9):
        unit, _ = unit_norm(pick_keys(j))
        for c in range(0, TILE, CHUNK):
            ds = (probs[j, c : c + CHUNK] * (dps[j, c : c + CHUNK] - delta) * SCALE).astype(
                jnp.bfloat16
            )
            dk = jnp.dot(ds, qn, preferred_element_type=jnp.float32).astype(jnp.bfloat16)
            for target in targets[j]:
                target[0, c : c + CHUNK] = dk
            key_gain_sum = key_gain_sum + fold(
                dk.astype(jnp.float32) * unit[c : c + CHUNK], jnp.sum
            )
            dq_t = dq_t + lax.dot_general(
                kn[j, c : c + CHUNK],
                ds,
                (((0,), (0,)), ((), ())),
                preferred_element_type=jnp.float32,
            )
    dq = dq_t.T
    d_queries[...] = norm_back(dq, q_unit, q_inverse, gain_q).astype(jnp.bfloat16)

    @pl.when(pl.program_id(0) == 0)
    def _():
        gains[...] = jnp.zeros_like(gains)

    gains[0:8] += fold(dq * q_unit, jnp.sum)
    gains[8:16] += key_gain_sum


def block_specs():
    row = pl.BlockSpec((TILE, HD), lambda h: (0, h))
    pair = pl.BlockSpec((2, TILE, HD), lambda h: (0, 0, h))
    quad = pl.BlockSpec((2, 2, TILE, HD), lambda h: (0, 0, 0, h))
    whole = pl.BlockSpec((1, HD), lambda h: (0, 0))
    return row, pair, quad, whole


def attention(frame_counts, row_counts, query_gain, key_gain, queries, grads, ins):
    heads = queries.shape[1] // HD
    row, pair, quad, whole = block_specs()
    spec_of = {2: row, 3: pair, 4: quad}
    low = lambda *lead: jax.ShapeDtypeStruct(lead + queries.shape, jnp.bfloat16)
    return pl.pallas_call(
        attention_kernel,
        grid=(heads,),
        in_specs=[pl.BlockSpec(memory_space=pltpu.SMEM)] * 2
        + [whole, whole, row, row]
        + [spec_of[x.ndim] for x in ins],
        out_specs=[pair, pair, pair, quad, pair, quad, pair, pair, pair, row]
        + [pl.BlockSpec((16, HD), lambda h: (0, 0))],
        out_shape=[low(2), low(2), low(2), low(2, 2), low(2), low(2, 2), low(2)]
        + [low(2), low(2), low()]
        + [jax.ShapeDtypeStruct((16, HD), jnp.float32)],
        scratch_shapes=[
            pltpu.VMEM((9, TILE, HD), jnp.bfloat16),
            pltpu.VMEM((9, TILE, TILE), jnp.float32),
            pltpu.VMEM((9, TILE, TILE), jnp.float32),
        ],
        compiler_params=pltpu.CompilerParams(vmem_limit_bytes=36 * 2**20),
        cost_estimate=pl.CostEstimate(
            flops=heads * 10 * TILE * TILE * 9 * HD,
            bytes_accessed=40 * TILE * queries.shape[1] * 2,
            transcendentals=heads * 9 * TILE * TILE,
        ),
    )(frame_counts, row_counts, query_gain[None], key_gain[None], queries, grads, *ins)


def finish_kernel(key_gain, keys, *rest):
    pairs, (tk, tv, vx, d_keys, d_values) = rest[:-5], rest[-5:]
    dk = tk[...].astype(jnp.float32)
    time_index = lax.axis_index("tm")
    dv = jnp.where((time_index == 3) | (time_index == 4), vx[...], tv[...])
    dv = jnp.where((time_index == 0) | (time_index == 7), 0.0, dv.astype(jnp.float32))
    for part in pairs:
        dk = dk + part[0].astype(jnp.float32)
        dv = dv + part[1].astype(jnp.float32)
    unit, inverse = unit_norm(keys[...])
    d_keys[...] = norm_back(dk, unit, inverse, key_gain[...]).astype(jnp.bfloat16)
    d_values[...] = dv.astype(jnp.bfloat16)


def finish(key_gain, keys, pairs, rows):
    heads = keys.shape[1] // HD
    row, pair, _, whole = block_specs()
    return pl.pallas_call(
        finish_kernel,
        grid=(heads,),
        in_specs=[whole, row] + [pair] * len(pairs) + [row] * len(rows),
        out_specs=[row, row],
        out_shape=[jax.ShapeDtypeStruct(keys.shape, jnp.bfloat16)] * 2,
        compiler_params=pltpu.CompilerParams(vmem_limit_bytes=16 * 2**20),
    )(key_gain[None], keys, *pairs, *rows)


def swaps(size, first, skip=()):
    route = []
    for i in range(first, size - 1, 2):
        if i not in skip:
            route += [(i, i + 1), (i + 1, i)]
    return route


def total_over(x, axes):
    for axis in axes:
        size = lax.axis_size(axis)
        bit = 1
        while bit < size:
            x = x + lax.ppermute(x, axis, [(i, i ^ bit) for i in range(size)])
            bit *= 2
    return x


def on_device(
    queries, key_vectors, value_vectors, out_grads, query_gain, key_gain, frame_counts, row_counts
):
    time_count = lax.axis_size("tm")
    height_count = lax.axis_size("height")
    row_count = queries.shape[2]
    feature_count = queries.shape[3]
    keys = key_vectors[0, 0]
    values = value_vectors[0, 0]

    even_t, odd_t = swaps(8, 0), swaps(8, 1, (3,))
    even_h, odd_h = swaps(4, 0), swaps(4, 1)
    key_route = odd_t + [(3, 4), (4, 3)]
    value_route = odd_t + [(3, 0), (4, 7)]
    arrive = [(0, 4), (7, 3)]
    far_even = [(4 * t + i, 4 * t + j) for t in (3, 4) for i, j in even_h]
    far_odd = [(4 * t + i, 4 * t + j) for t in (3, 4) for i, j in odd_h]
    both = ("tm", "height")

    tv = lax.ppermute(values, "tm", value_route)
    tk = lax.ppermute(keys, "tm", key_route)
    own = jnp.stack([keys, values])
    he = lax.ppermute(own, "height", even_h)
    ho = lax.ppermute(own, "height", odd_h)
    te = lax.ppermute(own, "tm", even_t)
    he, ho, te, tv = lax.optimization_barrier((he, ho, te, tv))
    vx = lax.ppermute(tv, "tm", arrive)
    sides = jnp.stack([he, ho])
    ce = lax.ppermute(sides, "tm", even_t)
    sides, tk = lax.optimization_barrier((sides, tk))
    co = lax.ppermute(sides, "tm", odd_t)
    zke = lax.ppermute(tk, both, far_even)
    zko = lax.ppermute(tk, both, far_odd)
    zve = lax.ppermute(vx, both, far_even)
    zvo = lax.ppermute(vx, both, far_odd)

    outs = attention(
        frame_counts,
        row_counts,
        query_gain,
        key_gain,
        queries[0, 0],
        out_grads[0, 0],
        [keys, values, te, tk, tv, he, ho, ce, co, vx, zke, zko, zve, zvo],
    )
    own, he, ho, ce, te, co, to, x_even, x_odd, d_queries, gain_parts = outs

    wide = lambda x: x.astype(jnp.float32)
    xe = lax.ppermute(x_even, both, far_even)
    xo = lax.ppermute(x_odd, both, far_odd)
    ce = lax.ppermute(ce, "tm", even_t)
    co = lax.ppermute(co, "tm", odd_t)
    gain_parts, _ = lax.optimization_barrier((gain_parts, x_odd))
    gain_local = total_over(jnp.sum(gain_parts.reshape(2, 8, HD), axis=1), ("dp",))
    gain_local, xe, xo = lax.optimization_barrier((gain_local, xe, xo))
    to = (wide(to) + wide(xe) + wide(xo)).astype(jnp.bfloat16)
    tv = lax.ppermute(to[1], "tm", value_route)
    tk = lax.ppermute(to[0], "tm", key_route)
    vx = lax.ppermute(tv, "tm", arrive)
    he = (wide(he) + wide(ce[0]) + wide(co[0])).astype(jnp.bfloat16)
    ho = (wide(ho) + wide(ce[1]) + wide(co[1])).astype(jnp.bfloat16)
    te, he, ho = lax.optimization_barrier((te, he, ho))
    he = lax.ppermute(he, "height", even_h)
    ho = lax.ppermute(ho, "height", odd_h)
    te = lax.ppermute(te, "tm", even_t)
    gain_local, te = lax.optimization_barrier((gain_local, te))
    gain_total = total_over(gain_local, ("tm", "height"))
    d_keys, d_values = finish(key_gain, keys, [own, te, he, ho], [tk, tv, vx])

    head_total = lax.axis_size("dp") * (feature_count // HD)
    scaling = 1.0 / math.sqrt(time_count * height_count * row_count * head_total)
    gain_grads = gain_total * scaling
    return (d_queries[None, None], d_keys[None, None], d_values[None, None], gain_grads)


def solution(mesh):
    split = P("tm", "height", None, "dp")
    return jax.shard_map(
        on_device,
        mesh=mesh,
        in_specs=(split,) * 4 + (P(),) * 4,
        out_specs=(split,) * 3 + (P(),),
        check_vma=False,
    )
```

time: 180 us -> 163 us (0.906)
  starting transfers between devices: 87.2 us -> 69.6 us
    ppermute x8, starting transfers between devices: 31.8 us -> 9.26 us  [total_over(): x = x + lax.ppermute(x, axis, [(i, i ^ bit) for i in range(size)])]
    ppermute x16 -> x22, starting transfers between devices: 55.4 us -> 60.4 us  [the longest x1 17.1 us: on_device(): te = lax.ppermute(te, 'tm', even_t)]
    ppermute x16 -> x22, waiting for transfers between devices: 39.3 us -> 40.1 us  [the longest x1 10.8 us: on_device(): ce = lax.ppermute(ce, 'tm', even_t)]
  transfers between devices with their start and end apart: 24 -> 30, of which waited for: 14 -> 13; matrix products, arithmetic and copies ran while one was open for 1% -> 0% of each run, Pallas kernels for 0% -> 1%
where the time goes in v2:
time: 163 us; the launch traced here: 162 us
  starting transfers between devices  69.6 us (43%)
  waiting for transfers between devices  63.9 us (39%)
  Pallas kernels  25.1 us (15%)
  other arithmetic  2.59 us (2%)
    ppermute x8, waiting for transfers between devices, total_over(): x = x + lax.ppermute(x, axis, [(i, i ^ bit) for i in range(size)])  23.8 us
    pallas_call x1, Pallas kernels, attention(): pl.pallas_call(attention_kernel, grid=(heads,), in_specs=[pl.BlockSpec(me...  22.8 us
    ppermute x1, starting transfers between devices, on_device(): te = lax.ppermute(te, 'tm', even_t)  17.1 us
    ppermute x2, starting transfers between devices, on_device(): vx = lax.ppermute(tv, 'tm', arrive)  15 us
    ppermute x1, waiting for transfers between devices, on_device(): ce = lax.ppermute(ce, 'tm', even_t)  10.8 us
    ppermute x8, starting transfers between devices, total_over(): x = x + lax.ppermute(x, axis, [(i, i ^ bit) for i in range(size)])  9.26 us
    ppermute x1, waiting for transfers between devices, on_device(): ce = lax.ppermute(sides, 'tm', even_t)  9.09 us
    ppermute x1, waiting for transfers between devices, on_device(): tv = lax.ppermute(values, 'tm', value_route)  9.01 us
  transfers between devices with their start and end apart: 30, of which 13 were waited for; matrix products, arithmetic and copies ran while one was open for 0% of the time, Pallas kernels for 1%

profile of v2, /device:TPU:2, one launch (start us, length us, event | category | flops | bytes accessed | tf_op | source)
XLA Modules:
  0.0 162.3 jit_solution(15897366686193529226)
XLA Ops:
  1.8 1.7 %collective-permute-start.2 = (bf16[2,384,384]{2,1,0:T(8,128)(2,1)S(1)}, bf16[2,384,384]{2,1,0:T(8,128)(2,1)S(1)}, u32[]{:S(2)}, u32[]{:S(2)}) collective-permute-start(bf16[2,384,384]{2,1,0:T(8,128)(2,1)S(1)} %pad_maximum_fusion.1), channel_id=1, source_target_pairs={{0,4},{4,0},{8,12},{12,8},{16,20},{20,16},{24,28},{28,24},{1,5},{5... | collective-permute-start | bytes 1769480 | tf_op jit(solution)/shard_map/ppermute | solution.py:283
  4.2 5.1 %collective-permute-start = (bf16[2,384,384]{2,1,0:T(8,128)(2,1)S(1)}, bf16[2,384,384]{2,1,0:T(8,128)(2,1)S(1)}, u32[]{:S(2)}, u32[]{:S(2)}) collective-permute-start(bf16[2,384,384]{2,1,0:T(8,128)(2,1)S(1)} %pad_maximum_fusion.1), channel_id=1, source_target_pairs={{0,1},{1,0},{2,3},{3,2},{4,5},{5,4},{6,7},{7,6},{8,9},{9,8},{10,11... | collective-permute-start | bytes 1769480 | tf_op jit(solution)/shard_map/ppermute | solution.py:281
  11.3 9.0 %collective-permute-done.3.rest_4_ = bf16[384,384]{1,0:T(8,128)(2,1)S(1)} collective-permute-done((bf16[384,384]{1,0:T(8,128)(2,1)S(1)}, bf16[384,384]{1,0:T(8,128)(2,1)S(1)}, u32[]{:S(2)}, u32[]{:S(2)}) %collective-permute-start.3) | collective-permute-done | bytes 294944 | tf_op jit(solution)/shard_map/ppermute | solution.py:278
  20.3 1.8 %collective-permute-done.rest_5_ = bf16[2,384,384]{2,1,0:T(8,128)(2,1)S(1)} collective-permute-done((bf16[2,384,384]{2,1,0:T(8,128)(2,1)S(1)}, bf16[2,384,384]{2,1,0:T(8,128)(2,1)S(1)}, u32[]{:S(2)}, u32[]{:S(2)}) %collective-permute-start) | collective-permute-done | bytes 589856 | tf_op jit(solution)/shard_map/ppermute | solution.py:281
  23.2 7.1 %collective-permute-start.5 = (bf16[2,2,384,384]{3,2,1,0:T(8,128)(2,1)S(1)}, bf16[2,2,384,384]{3,2,1,0:T(8,128)(2,1)S(1)}, u32[]{:S(2)}, u32[]{:S(2)}) collective-permute-start(bf16[2,2,384,384]{3,2,1,0:T(8,128)(2,1)S(1)} %pad_maximum_fusion), channel_id=1, source_target_pairs={{0,4},{4,0},{8,12},{12,8},{16,20},{20,16},{24,28},{28,24},{1,5},{5... | collective-permute-start | bytes 3538952 | tf_op jit(solution)/shard_map/ppermute | solution.py:287
  30.3 8.2 %collective-permute-start.7 = (bf16[384,384]{1,0:T(8,128)(2,1)S(1)}, bf16[384,384]{1,0:T(8,128)(2,1)S(1)}, u32[]{:S(2)}, u32[]{:S(2)}) collective-permute-start(bf16[384,384]{1,0:T(8,128)(2,1)S(1)} %collective-permute-done.3.rest_4_), channel_id=1, source_target_pairs={{0,16},{28,12},{1,17},{29,13},{2,18},{30,14},{3,19},{31,15},{32,48... | collective-permute-start | bytes 884744 | tf_op jit(solution)/shard_map/ppermute | solution.py:285
  39.9 3.8 %collective-permute-done.7.rest_9_ = bf16[384,384]{1,0:T(8,128)(2,1)S(1)} collective-permute-done((bf16[384,384]{1,0:T(8,128)(2,1)S(1)}, bf16[384,384]{1,0:T(8,128)(2,1)S(1)}, u32[]{:S(2)}, u32[]{:S(2)}) %collective-permute-start.7) | collective-permute-done | bytes 294944 | tf_op jit(solution)/shard_map/ppermute | solution.py:285
  45.1 9.1 %collective-permute-done.5.rest_7_ = bf16[2,2,384,384]{3,2,1,0:T(8,128)(2,1)S(1)} collective-permute-done((bf16[2,2,384,384]{3,2,1,0:T(8,128)(2,1)S(1)}, bf16[2,2,384,384]{3,2,1,0:T(8,128)(2,1)S(1)}, u32[]{:S(2)}, u32[]{:S(2)}) %collective-permute-start.5) | collective-permute-done | bytes 1179680 | tf_op jit(solution)/shard_map/ppermute | solution.py:287
  54.2 22.8 %shard_map.111 = (bf16[2,384,384]{2,1,0:T(8,128)(2,1)S(1)}, bf16[2,384,384]{2,1,0:T(8,128)(2,1)S(1)}, bf16[2,384,384]{2,1,0:T(8,128)(2,1)S(1)}, bf16[2,2,384,384...) custom-call(s32[8]{0:T(128)S(1)} %copy-done.5, ...), custom_call_target="tpu_custom_call" | custom-call | flops 5096079360 | bytes 11796480 | tf_op jit(solution)/shard_map/pallas_call | solution.py:189
  77.1 1.7 %collective-permute-start.17 = (bf16[2,2,384,384]{3,2,1,0:T(8,128)(2,1)S(1)}, bf16[2,2,384,384]{3,2,1,0:T(8,128)(2,1)S(1)}, u32[]{:S(2)}, u32[]{:S(2)}) collective-permute-start(bf16[2,2,384,384]{3,2,1,0:T(8,128)(2,1)S(1)} %get-tuple-element.47), channel_id=1, source_target_pairs={{0,4},{4,0},{8,12},{12,8},{16,20},{20,16},{24,28},{28,24},{1,5},{5... | collective-permute-start | bytes 3538952 | tf_op jit(solution)/shard_map/ppermute | solution.py:309
  82.9 3.0 %collective-permute-done.13 = f32[2,128]{1,0:T(2,128)S(1)} collective-permute-done((f32[2,128]{1,0:T(2,128)S(1)}, f32[2,128]{1,0:T(2,128)S(1)}, u32[]{:S(2)}, u32[]{:S(2)}) %collective-permute-start.13) | collective-permute-done | bytes 1056 | tf_op jit(solution)/shard_map/ppermute | solution.py:254
  86.0 2.1 %collective-permute-start.14 = (f32[2,128]{1,0:T(2,128)S(1)}, f32[2,128]{1,0:T(2,128)S(1)}, u32[]{:S(2)}, u32[]{:S(2)}) collective-permute-start(f32[2,128]{1,0:T(2,128)S(1)} %add.43), channel_id=1, source_target_pairs={{0,128},{32,160},{64,192},{96,224},{128,0},{160,32},{192,64},{224,... | collective-permute-start | bytes 3080 | tf_op jit(solution)/shard_map/ppermute | solution.py:254
  88.1 3.0 %collective-permute-done.14 = f32[2,128]{1,0:T(2,128)S(1)} collective-permute-done((f32[2,128]{1,0:T(2,128)S(1)}, f32[2,128]{1,0:T(2,128)S(1)}, u32[]{:S(2)}, u32[]{:S(2)}) %collective-permute-start.14) | collective-permute-done | bytes 1056 | tf_op jit(solution)/shard_map/ppermute | solution.py:254
  91.3 10.8 %collective-permute-done.17 = bf16[2,2,384,384]{3,2,1,0:T(8,128)(2,1)S(1)} collective-permute-done((bf16[2,2,384,384]{3,2,1,0:T(8,128)(2,1)S(1)}, bf16[2,2,384,384]{3,2,1,0:T(8,128)(2,1)S(1)}, u32[]{:S(2)}, u32[]{:S(2)}) %collective-permute-start.17) | collective-permute-done | bytes 1179680 | tf_op jit(solution)/shard_map/ppermute | solution.py:309
  102.6 17.1 %collective-permute-start.19 = (bf16[2,384,384]{2,1,0:T(8,128)(2,1)S(1)}, bf16[2,384,384]{2,1,0:T(8,128)(2,1)S(1)}, u32[]{:S(2)}, u32[]{:S(2)}) collective-permute-start(bf16[2,384,384]{2,1,0:T(8,128)(2,1)S(1)} %get-tuple-element.50), channel_id=1, source_target_pairs={{0,4},{4,0},{8,12},{12,8},{16,20},{20,16},{24,28},{28,24},{1,5},{5... | collective-permute-start | bytes 1769480 | tf_op jit(solution)/shard_map/ppermute | solution.py:323
  124.0 5.6 %collective-permute-done.23.rest_5_ = bf16[384,384]{1,0:T(8,128)(2,1)S(1)} collective-permute-done((bf16[384,384]{1,0:T(8,128)(2,1)S(1)}, bf16[384,384]{1,0:T(8,128)(2,1)S(1)}, u32[]{:S(2)}, u32[]{:S(2)}) %collective-permute-start.23) | collective-permute-done | bytes 294944 | tf_op jit(solution)/shard_map/ppermute | solution.py:315
  129.6 6.8 %collective-permute-start.24 = (bf16[384,384]{1,0:T(8,128)(2,1)S(1)}, bf16[384,384]{1,0:T(8,128)(2,1)S(1)}, u32[]{:S(2)}, u32[]{:S(2)}) collective-permute-start(bf16[384,384]{1,0:T(8,128)(2,1)S(1)} %collective-permute-done.23.rest_5_), channel_id=1, source_target_pairs={{0,16},{28,12},{1,17},{29,13},{2,18},{30,14},{3,19},{31,15},{32,48... | collective-permute-start | bytes 884744 | tf_op jit(solution)/shard_map/ppermute | solution.py:317
  136.5 3.6 %collective-permute-done.25 = f32[2,128]{1,0:T(2,128)S(1)} collective-permute-done((f32[2,128]{1,0:T(2,128)S(1)}, f32[2,128]{1,0:T(2,128)S(1)}, u32[]{:S(2)}, u32[]{:S(2)}) %collective-permute-start.25) | collective-permute-done | bytes 1056 | tf_op jit(solution)/shard_map/ppermute | solution.py:254
  140.0 5.1 %collective-permute-done.26 = f32[2,128]{1,0:T(2,128)S(1)} collective-permute-done((f32[2,128]{1,0:T(2,128)S(1)}, f32[2,128]{1,0:T(2,128)S(1)}, u32[]{:S(2)}, u32[]{:S(2)}) %collective-permute-start.26) | collective-permute-done | bytes 1056 | tf_op jit(solution)/shard_map/ppermute | solution.py:254
  146.1 6.5 %collective-permute-done.27 = f32[2,128]{1,0:T(2,128)S(1)} collective-permute-done((f32[2,128]{1,0:T(2,128)S(1)}, f32[2,128]{1,0:T(2,128)S(1)}, u32[]{:S(2)}, u32[]{:S(2)}) %collective-permute-start.27) | collective-permute-done | bytes 1056 | tf_op jit(solution)/shard_map/ppermute | solution.py:254
  152.6 2.6 %collective-permute-start.28 = (f32[2,128]{1,0:T(2,128)S(1)}, f32[2,128]{1,0:T(2,128)S(1)}, u32[]{:S(2)}, u32[]{:S(2)}) collective-permute-start(f32[2,128]{1,0:T(2,128)S(1)} %add.53), channel_id=1, source_target_pairs={{0,1},{1,0},{2,3},{3,2},{4,5},{5,4},{6,7},{7,6},{8,9},{9,8},{10,11... | collective-permute-start | bytes 3080 | tf_op jit(solution)/shard_map/ppermute | solution.py:254
  155.2 1.5 collective-permute-done.28
  156.7 2.7 %collective-permute-start.29 = (f32[2,128]{1,0:T(2,128)S(1)}, f32[2,128]{1,0:T(2,128)S(1)}, u32[]{:S(2)}, u32[]{:S(2)}) collective-permute-start(f32[2,128]{1,0:T(2,128)S(1)} %add.54), channel_id=1, source_target_pairs={{0,2},{1,3},{2,0},{3,1},{4,6},{5,7},{6,4},{7,5},{8,10},{9,11},{10,... | collective-permute-start | bytes 3080 | tf_op jit(solution)/shard_map/ppermute | solution.py:254
  159.4 2.3 %shard_map.112 = (bf16[384,384]{1,0:T(8,128)(2,1)}, bf16[384,384]{1,0:T(8,128)(2,1)}) custom-call(f32[1,128]{1,0:T(1,128)S(1)} %bitcast.49, bf16[384,384]{1,0:T(8,128)(2,1)S(1)} %bitcast.42, bf16[2,384,384]{2,1,0:T(8,128)(2,1)S(1)} %get-tuple-element.39.rest_0_, bf16[2,384,384]{2,1,0:T(8,128)(2,1)S(1)} %collective-permute-done.19.rest_1_, ...), custom_call_target="tpu_custom_call" | custom-call | tf_op jit(solution)/shard_map/pallas_call | solution.py:231
  (68 shorter events, 18.3 us)
Async XLA Ops:
  1.8 18.5 %collective-permute-start.2 = (bf16[2,384,384]{2,1,0:T(8,128)(2,1)S(1)}, bf16[2,384,384]{2,1,0:T(8,128)(2,1)S(1)}, u32[]{:S(2)}, u32[]{:S(2)}) collective-permute-start(bf16[2,384,384]{2,1,0:T(8,128)(2,1)S(1)} %pad_maximum_fusion.1), channel_id=1, source_target_pairs={{0,4},{4,0},{8,12},{12,8},{16,20},{20,16},{24,28},{28,24},{1,5},{5... | collective-permute-start | bytes 1769480 | tf_op jit(solution)/shard_map/ppermute | solution.py:283
  3.5 16.8 %collective-permute-start.1 = (bf16[2,384,384]{2,1,0:T(8,128)(2,1)S(1)}, bf16[2,384,384]{2,1,0:T(8,128)(2,1)S(1)}, u32[]{:S(2)}, u32[]{:S(2)}) collective-permute-start(bf16[2,384,384]{2,1,0:T(8,128)(2,1)S(1)} %pad_maximum_fusion.1), channel_id=1, source_target_pairs={{1,2},{2,1},{5,6},{6,5},{9,10},{10,9},{13,14},{14,13},{17,18},{18,... | collective-permute-start | bytes 1769480 | tf_op jit(solution)/shard_map/ppermute | solution.py:282
  4.2 17.9 %collective-permute-start = (bf16[2,384,384]{2,1,0:T(8,128)(2,1)S(1)}, bf16[2,384,384]{2,1,0:T(8,128)(2,1)S(1)}, u32[]{:S(2)}, u32[]{:S(2)}) collective-permute-start(bf16[2,384,384]{2,1,0:T(8,128)(2,1)S(1)} %pad_maximum_fusion.1), channel_id=1, source_target_pairs={{0,1},{1,0},{2,3},{3,2},{4,5},{5,4},{6,7},{7,6},{8,9},{9,8},{10,11... | collective-permute-start | bytes 1769480 | tf_op jit(solution)/shard_map/ppermute | solution.py:281
  9.3 11.0 %collective-permute-start.3 = (bf16[384,384]{1,0:T(8,128)(2,1)S(1)}, bf16[384,384]{1,0:T(8,128)(2,1)S(1)}, u32[]{:S(2)}, u32[]{:S(2)}) collective-permute-start(bf16[384,384]{1,0:T(8,128)(2,1)S(1)} %bitcast.46), channel_id=1, source_target_pairs={{4,8},{8,4},{20,24},{24,20},{12,0},{16,28},{5,9},{9,5},{21,25},{25... | collective-permute-start | bytes 884744 | tf_op jit(solution)/shard_map/ppermute | solution.py:278
  10.6 11.6 %collective-permute-start.4 = (bf16[384,384]{1,0:T(8,128)(2,1)S(1)}, bf16[384,384]{1,0:T(8,128)(2,1)S(1)}, u32[]{:S(2)}, u32[]{:S(2)}) collective-permute-start(bf16[384,384]{1,0:T(8,128)(2,1)S(1)} %bitcast.40), channel_id=1, source_target_pairs={{4,8},{8,4},{20,24},{24,20},{12,16},{16,12},{5,9},{9,5},{21,25},{2... | collective-permute-start | bytes 884744 | tf_op jit(solution)/shard_map/ppermute | solution.py:279
  22.3 22.8 %collective-permute-start.6 = (bf16[2,2,384,384]{3,2,1,0:T(8,128)(2,1)S(1)}, bf16[2,2,384,384]{3,2,1,0:T(8,128)(2,1)S(1)}, u32[]{:S(2)}, u32[]{:S(2)}) collective-permute-start(bf16[2,2,384,384]{3,2,1,0:T(8,128)(2,1)S(1)} %pad_maximum_fusion), channel_id=1, source_target_pairs={{4,8},{8,4},{20,24},{24,20},{5,9},{9,5},{21,25},{25,21},{6,10},{10... | collective-permute-start | bytes 3538952 | tf_op jit(solution)/shard_map/ppermute | solution.py:289
  23.2 31.1 %collective-permute-start.5 = (bf16[2,2,384,384]{3,2,1,0:T(8,128)(2,1)S(1)}, bf16[2,2,384,384]{3,2,1,0:T(8,128)(2,1)S(1)}, u32[]{:S(2)}, u32[]{:S(2)}) collective-permute-start(bf16[2,2,384,384]{3,2,1,0:T(8,128)(2,1)S(1)} %pad_maximum_fusion), channel_id=1, source_target_pairs={{0,4},{4,0},{8,12},{12,8},{16,20},{20,16},{24,28},{28,24},{1,5},{5... | collective-permute-start | bytes 3538952 | tf_op jit(solution)/shard_map/ppermute | solution.py:287
  30.3 13.4 %collective-permute-start.7 = (bf16[384,384]{1,0:T(8,128)(2,1)S(1)}, bf16[384,384]{1,0:T(8,128)(2,1)S(1)}, u32[]{:S(2)}, u32[]{:S(2)}) collective-permute-start(bf16[384,384]{1,0:T(8,128)(2,1)S(1)} %collective-permute-done.3.rest_4_), channel_id=1, source_target_pairs={{0,16},{28,12},{1,17},{29,13},{2,18},{30,14},{3,19},{31,15},{32,48... | collective-permute-start | bytes 884744 | tf_op jit(solution)/shard_map/ppermute | solution.py:285
  38.5 5.8 %collective-permute-start.9 = (bf16[384,384]{1,0:T(8,128)(2,1)S(1)}, bf16[384,384]{1,0:T(8,128)(2,1)S(1)}, u32[]{:S(2)}, u32[]{:S(2)}) collective-permute-start(bf16[384,384]{1,0:T(8,128)(2,1)S(1)} %collective-permute-done.4.rest_3_), channel_id=1, source_target_pairs={{13,14},{14,13},{17,18},{18,17},{45,46},{46,45},{49,50},{50,49},{7... | collective-permute-start | bytes 884744 | tf_op jit(solution)/shard_map/ppermute | solution.py:291
  39.2 5.9 %collective-permute-start.8 = (bf16[384,384]{1,0:T(8,128)(2,1)S(1)}, bf16[384,384]{1,0:T(8,128)(2,1)S(1)}, u32[]{:S(2)}, u32[]{:S(2)}) collective-permute-start(bf16[384,384]{1,0:T(8,128)(2,1)S(1)} %collective-permute-done.4.rest_3_), channel_id=1, source_target_pairs={{12,13},{13,12},{14,15},{15,14},{16,17},{17,16},{18,19},{19,18},{4... | collective-permute-start | bytes 884744 | tf_op jit(solution)/shard_map/ppermute | solution.py:290
  77.1 25.0 %collective-permute-start.17 = (bf16[2,2,384,384]{3,2,1,0:T(8,128)(2,1)S(1)}, bf16[2,2,384,384]{3,2,1,0:T(8,128)(2,1)S(1)}, u32[]{:S(2)}, u32[]{:S(2)}) collective-permute-start(bf16[2,2,384,384]{3,2,1,0:T(8,128)(2,1)S(1)} %get-tuple-element.47), channel_id=1, source_target_pairs={{0,4},{4,0},{8,12},{12,8},{16,20},{20,16},{24,28},{28,24},{1,5},{5... | collective-permute-start | bytes 3538952 | tf_op jit(solution)/shard_map/ppermute | solution.py:309
  78.8 23.3 %collective-permute-start.18 = (bf16[2,2,384,384]{3,2,1,0:T(8,128)(2,1)S(1)}, bf16[2,2,384,384]{3,2,1,0:T(8,128)(2,1)S(1)}, u32[]{:S(2)}, u32[]{:S(2)}) collective-permute-start(bf16[2,2,384,384]{3,2,1,0:T(8,128)(2,1)S(1)} %get-tuple-element.48), channel_id=1, source_target_pairs={{4,8},{8,4},{20,24},{24,20},{5,9},{9,5},{21,25},{25,21},{6,10},{10... | collective-permute-start | bytes 3538952 | tf_op jit(solution)/shard_map/ppermute | solution.py:310
  79.5 11.5 %collective-permute-start.15 = (bf16[2,384,384]{2,1,0:T(8,128)(2,1)S(1)}, bf16[2,384,384]{2,1,0:T(8,128)(2,1)S(1)}, u32[]{:S(2)}, u32[]{:S(2)}) collective-permute-start(bf16[2,384,384]{2,1,0:T(8,128)(2,1)S(1)} %get-tuple-element.43), channel_id=1, source_target_pairs={{12,13},{13,12},{14,15},{15,14},{16,17},{17,16},{18,19},{19,18},{4... | collective-permute-start | bytes 1769480 | tf_op jit(solution)/shard_map/ppermute | solution.py:307
  80.3 10.8 %collective-permute-start.16 = (bf16[2,384,384]{2,1,0:T(8,128)(2,1)S(1)}, bf16[2,384,384]{2,1,0:T(8,128)(2,1)S(1)}, u32[]{:S(2)}, u32[]{:S(2)}) collective-permute-start(bf16[2,384,384]{2,1,0:T(8,128)(2,1)S(1)} %get-tuple-element.41), channel_id=1, source_target_pairs={{13,14},{14,13},{17,18},{18,17},{45,46},{46,45},{49,50},{50,49},{7... | collective-permute-start | bytes 1769480 | tf_op jit(solution)/shard_map/ppermute | solution.py:308
  86.0 5.1 %collective-permute-start.14 = (f32[2,128]{1,0:T(2,128)S(1)}, f32[2,128]{1,0:T(2,128)S(1)}, u32[]{:S(2)}, u32[]{:S(2)}) collective-permute-start(f32[2,128]{1,0:T(2,128)S(1)} %add.43), channel_id=1, source_target_pairs={{0,128},{32,160},{64,192},{96,224},{128,0},{160,32},{192,64},{224,... | collective-permute-start | bytes 3080 | tf_op jit(solution)/shard_map/ppermute | solution.py:254
  102.6 33.8 %collective-permute-start.19 = (bf16[2,384,384]{2,1,0:T(8,128)(2,1)S(1)}, bf16[2,384,384]{2,1,0:T(8,128)(2,1)S(1)}, u32[]{:S(2)}, u32[]{:S(2)}) collective-permute-start(bf16[2,384,384]{2,1,0:T(8,128)(2,1)S(1)} %get-tuple-element.50), channel_id=1, source_target_pairs={{0,4},{4,0},{8,12},{12,8},{16,20},{20,16},{24,28},{28,24},{1,5},{5... | collective-permute-start | bytes 1769480 | tf_op jit(solution)/shard_map/ppermute | solution.py:323
  119.7 9.8 %collective-permute-start.23 = (bf16[384,384]{1,0:T(8,128)(2,1)S(1)}, bf16[384,384]{1,0:T(8,128)(2,1)S(1)}, u32[]{:S(2)}, u32[]{:S(2)}) collective-permute-start(bf16[384,384]{1,0:T(8,128)(2,1)S(1)} %get-tuple-element.62), channel_id=1, source_target_pairs={{4,8},{8,4},{20,24},{24,20},{12,0},{16,28},{5,9},{9,5},{21,25},{25... | collective-permute-start | bytes 884744 | tf_op jit(solution)/shard_map/ppermute | solution.py:315
  121.0 38.4 %collective-permute-start.20 = (bf16[2,384,384]{2,1,0:T(8,128)(2,1)S(1)}, bf16[2,384,384]{2,1,0:T(8,128)(2,1)S(1)}, u32[]{:S(2)}, u32[]{:S(2)}) collective-permute-start(bf16[2,384,384]{2,1,0:T(8,128)(2,1)S(1)} %get-tuple-element.52), channel_id=1, source_target_pairs={{0,1},{1,0},{2,3},{3,2},{4,5},{5,4},{6,7},{7,6},{8,9},{9,8},{10,11... | collective-permute-start | bytes 1769480 | tf_op jit(solution)/shard_map/ppermute | solution.py:321
  122.6 36.9 %collective-permute-start.21 = (bf16[2,384,384]{2,1,0:T(8,128)(2,1)S(1)}, bf16[2,384,384]{2,1,0:T(8,128)(2,1)S(1)}, u32[]{:S(2)}, u32[]{:S(2)}) collective-permute-start(bf16[2,384,384]{2,1,0:T(8,128)(2,1)S(1)} %get-tuple-element.53), channel_id=1, source_target_pairs={{1,2},{2,1},{5,6},{6,5},{9,10},{10,9},{13,14},{14,13},{17,18},{18,... | collective-permute-start | bytes 1769480 | tf_op jit(solution)/shard_map/ppermute | solution.py:322
  123.3 36.1 %collective-permute-start.22 = (bf16[384,384]{1,0:T(8,128)(2,1)S(1)}, bf16[384,384]{1,0:T(8,128)(2,1)S(1)}, u32[]{:S(2)}, u32[]{:S(2)}) collective-permute-start(bf16[384,384]{1,0:T(8,128)(2,1)S(1)} %get-tuple-element.63), channel_id=1, source_target_pairs={{4,8},{8,4},{20,24},{24,20},{12,16},{16,12},{5,9},{9,5},{21,25},{2... | collective-permute-start | bytes 884744 | tf_op jit(solution)/shard_map/ppermute | solution.py:316
  129.6 29.9 %collective-permute-start.24 = (bf16[384,384]{1,0:T(8,128)(2,1)S(1)}, bf16[384,384]{1,0:T(8,128)(2,1)S(1)}, u32[]{:S(2)}, u32[]{:S(2)}) collective-permute-start(bf16[384,384]{1,0:T(8,128)(2,1)S(1)} %collective-permute-done.23.rest_5_), channel_id=1, source_target_pairs={{0,16},{28,12},{1,17},{29,13},{2,18},{30,14},{3,19},{31,15},{32,48... | collective-permute-start | bytes 884744 | tf_op jit(solution)/shard_map/ppermute | solution.py:317
  140.0 5.1 %collective-permute-start.26 = (f32[2,128]{1,0:T(2,128)S(1)}, f32[2,128]{1,0:T(2,128)S(1)}, u32[]{:S(2)}, u32[]{:S(2)}) collective-permute-start(f32[2,128]{1,0:T(2,128)S(1)} %add.51), channel_id=1, source_target_pairs={{0,8},{4,12},{8,0},{12,4},{16,24},{20,28},{24,16},{28,20},{1,9},{5... | collective-permute-start | bytes 3080 | tf_op jit(solution)/shard_map/ppermute | solution.py:254
  145.1 7.5 %collective-permute-start.27 = (f32[2,128]{1,0:T(2,128)S(1)}, f32[2,128]{1,0:T(2,128)S(1)}, u32[]{:S(2)}, u32[]{:S(2)}) collective-permute-start(f32[2,128]{1,0:T(2,128)S(1)} %add.52), channel_id=1, source_target_pairs={{0,16},{4,20},{8,24},{12,28},{16,0},{20,4},{24,8},{28,12},{1,17},{... | collective-permute-start | bytes 3080 | tf_op jit(solution)/shard_map/ppermute | solution.py:254
  156.7 5.0 %collective-permute-start.29 = (f32[2,128]{1,0:T(2,128)S(1)}, f32[2,128]{1,0:T(2,128)S(1)}, u32[]{:S(2)}, u32[]{:S(2)}) collective-permute-start(f32[2,128]{1,0:T(2,128)S(1)} %add.54), channel_id=1, source_target_pairs={{0,2},{1,3},{2,0},{3,1},{4,6},{5,7},{6,4},{7,5},{8,10},{9,11},{10,... | collective-permute-start | bytes 3080 | tf_op jit(solution)/shard_map/ppermute | solution.py:254
  (14 other events, 226.3 us)

commit v3 on v2

v3 whole, which is shorter than its diff:
```python
import functools
import math

import jax
import jax.numpy as jnp
from jax import lax
from jax.experimental import pallas as pl
from jax.experimental.pallas import tpu as pltpu
from jax.sharding import PartitionSpec as P

HD = 128
TF = 6
TH = 8
TW = 8
TILE = TF * TH * TW
NORM_EPSILON = 1e-06
SCALE = 1.0 / math.sqrt(HD)
LOG2E = math.log2(math.e)
CHUNK = 384


def valid_rows(shape, frame_limit, row_limit):
    token = lax.broadcasted_iota(jnp.int32, shape, 0)
    return ((token >> 6) < frame_limit) & (((token >> 3) & 7) < row_limit)


def unit_norm(raw):
    wide = raw.astype(jnp.float32)
    inverse = lax.rsqrt(jnp.mean(wide * wide, axis=-1, keepdims=True) + NORM_EPSILON)
    return wide * inverse, inverse


def norm_back(grad, unit, inverse, gain):
    shaped = grad * gain
    inner = jnp.mean(shaped * unit, axis=-1, keepdims=True)
    return inverse * (shaped - unit * inner)


def fold(x, op):
    return op(x.reshape(x.shape[0] // 8, 8, x.shape[1]), axis=0)


def near(table, index):
    last = table.shape[0] - 1
    even = index % 2 == 0
    below = jnp.where(index == 0, 0, table[jnp.maximum(index - 1, 0)])
    above = jnp.where(index == last, 0, table[jnp.minimum(index + 1, last)])
    return table[index], jnp.where(even, above, below), jnp.where(even, below, above)


def attention_kernel(frame_counts, row_counts, query_gain, key_gain, queries, grads, *rest):
    ins, outs, scratch = rest[:8], rest[8:18], rest[18:]
    own_in, te_in, to_in, he_in, ho_in, ce_in, ze_in, zo_in = ins
    own, te, to, he, ho, ce, ze, zo, d_queries, gains = outs
    kn, probs, dps = scratch
    f, fe, fo = near(frame_counts, lax.axis_index("tm"))
    r, re, ro = near(row_counts, lax.axis_index("height"))
    frames = (f, fe, fo, f, f, fe, fe, fo, fo)
    rows = (r, r, r, re, ro, re, ro, re, ro)
    sources = (own_in, te_in, to_in, he_in, ho_in, ce_in.at[0], ce_in.at[1], ze_in, zo_in)
    targets = (own, te, to, he, ho, ce.at[0], ce.at[1], ze, zo)

    q_unit, q_inverse = unit_norm(queries[...])
    gain_q = query_gain[...]
    gain_k = key_gain[...]
    qn = (q_unit * gain_q).astype(jnp.bfloat16)
    gm = jnp.where(
        valid_rows((TILE, HD), f, r), grads[...], jnp.zeros_like(grads[...])
    )
    qt = qn.T
    gt = gm.T

    top = jnp.full((1, TILE), -1e30, jnp.float32)
    total = jnp.zeros((1, TILE), jnp.float32)
    tops = {}
    for j in range(9):
        unit, _ = unit_norm(sources[j][0])
        normed = (unit * gain_k).astype(jnp.bfloat16)
        kn[j] = normed
        bias = jnp.where(valid_rows((TILE, HD), frames[j], rows[j]), 0.0, -1e30)
        tile_top = jnp.full((8, TILE), -1e30, jnp.float32)
        for c in range(0, TILE, CHUNK):
            s = jnp.dot(normed[c : c + CHUNK], qt, preferred_element_type=jnp.float32)
            b = bias[c : c + CHUNK]
            s = s * (SCALE * LOG2E) + jnp.concatenate([b, b, b], axis=1)
            probs[j, c : c + CHUNK] = s
            tile_top = jnp.maximum(tile_top, fold(s, jnp.max))
        new_top = jnp.maximum(top, jnp.max(tile_top, axis=0, keepdims=True))
        part = jnp.zeros((8, TILE), jnp.float32)
        for c in range(0, TILE, CHUNK):
            e = jnp.exp2(probs[j, c : c + CHUNK] - new_top)
            probs[j, c : c + CHUNK] = e
            part = part + fold(e, jnp.sum)
        total = total * jnp.exp2(top - new_top) + jnp.sum(part, axis=0, keepdims=True)
        top = new_top
        tops[j] = new_top

    inverse_total = 1.0 / total
    delta8 = jnp.zeros((8, TILE), jnp.float32)
    for j in range(9):
        factor = jnp.exp2(tops[j] - top) * inverse_total
        v = sources[j][1]
        for c in range(0, TILE, CHUNK):
            dp = jnp.dot(v[c : c + CHUNK], gt, preferred_element_type=jnp.float32)
            p = probs[j, c : c + CHUNK] * factor
            low = p.astype(jnp.bfloat16)
            probs[j, c : c + CHUNK] = p
            dps[j, c : c + CHUNK] = dp
            delta8 = delta8 + fold(low.astype(jnp.float32) * dp, jnp.sum)
            dv = jnp.dot(low, gm, preferred_element_type=jnp.float32).astype(jnp.bfloat16)
            targets[j][1, c : c + CHUNK] = dv
    delta = jnp.sum(delta8, axis=0, keepdims=True)

    dq_t = jnp.zeros((HD, TILE), jnp.float32)
    key_gain_sum = jnp.zeros((8, HD), jnp.float32)
    for j in range(9):
        unit, _ = unit_norm(sources[j][0])
        for c in range(0, TILE, CHUNK):
            ds = (probs[j, c : c + CHUNK] * (dps[j, c : c + CHUNK] - delta) * SCALE).astype(
                jnp.bfloat16
            )
            dk = jnp.dot(ds, qn, preferred_element_type=jnp.float32).astype(jnp.bfloat16)
            targets[j][0, c : c + CHUNK] = dk
            key_gain_sum = key_gain_sum + fold(
                dk.astype(jnp.float32) * unit[c : c + CHUNK], jnp.sum
            )
            dq_t = dq_t + lax.dot_general(
                kn[j, c : c + CHUNK],
                ds,
                (((0,), (0,)), ((), ())),
                preferred_element_type=jnp.float32,
            )
    dq = dq_t.T
    d_queries[...] = norm_back(dq, q_unit, q_inverse, gain_q).astype(jnp.bfloat16)

    @pl.when(pl.program_id(0) == 0)
    def _():
        gains[...] = jnp.zeros_like(gains)

    gains[0:8] += fold(dq * q_unit, jnp.sum)
    gains[8:16] += key_gain_sum


def block_specs():
    row = pl.BlockSpec((TILE, HD), lambda h: (0, h))
    pair = pl.BlockSpec((2, TILE, HD), lambda h: (0, 0, h))
    whole = pl.BlockSpec((1, HD), lambda h: (0, 0))
    return row, pair, whole


def attention(frame_counts, row_counts, query_gain, key_gain, queries, grads, ins):
    heads = queries.shape[1] // HD
    row, pair, whole = block_specs()
    quad = pl.BlockSpec((2, 2, TILE, HD), lambda h: (0, 0, 0, h))
    spec_of = {3: pair, 4: quad}
    low = lambda *lead: jax.ShapeDtypeStruct(lead + queries.shape, jnp.bfloat16)
    return pl.pallas_call(
        attention_kernel,
        grid=(heads,),
        in_specs=[pl.BlockSpec(memory_space=pltpu.SMEM)] * 2
        + [whole, whole, row, row]
        + [spec_of[x.ndim] for x in ins],
        out_specs=[pair] * 5
        + [quad, pair, pair, row, pl.BlockSpec((16, HD), lambda h: (0, 0))],
        out_shape=[low(2)] * 5
        + [low(2, 2), low(2), low(2), low(), jax.ShapeDtypeStruct((16, HD), jnp.float32)],
        scratch_shapes=[
            pltpu.VMEM((9, TILE, HD), jnp.bfloat16),
            pltpu.VMEM((9, TILE, TILE), jnp.float32),
            pltpu.VMEM((9, TILE, TILE), jnp.float32),
        ],
        compiler_params=pltpu.CompilerParams(vmem_limit_bytes=36 * 2**20),
        cost_estimate=pl.CostEstimate(
            flops=heads * 10 * TILE * TILE * 9 * HD,
            bytes_accessed=40 * TILE * queries.shape[1] * 2,
            transcendentals=heads * 9 * TILE * TILE,
        ),
    )(frame_counts, row_counts, query_gain[None], key_gain[None], queries, grads, *ins)


def finish_kernel(key_gain, keys, *rest):
    pairs, (d_keys, d_values) = rest[:-2], rest[-2:]
    dk = jnp.zeros(keys.shape, jnp.float32)
    dv = jnp.zeros(keys.shape, jnp.float32)
    for part in pairs:
        dk = dk + part[0].astype(jnp.float32)
        dv = dv + part[1].astype(jnp.float32)
    unit, inverse = unit_norm(keys[...])
    d_keys[...] = norm_back(dk, unit, inverse, key_gain[...]).astype(jnp.bfloat16)
    d_values[...] = dv.astype(jnp.bfloat16)


def finish(key_gain, keys, pairs):
    heads = keys.shape[1] // HD
    row, pair, whole = block_specs()
    return pl.pallas_call(
        finish_kernel,
        grid=(heads,),
        in_specs=[whole, row] + [pair] * len(pairs),
        out_specs=[row, row],
        out_shape=[jax.ShapeDtypeStruct(keys.shape, jnp.bfloat16)] * 2,
        compiler_params=pltpu.CompilerParams(vmem_limit_bytes=16 * 2**20),
    )(key_gain[None], keys, *pairs)


def swaps(size, first, skip=()):
    route = []
    for i in range(first, size - 1, 2):
        if i not in skip:
            route += [(i, i + 1), (i + 1, i)]
    return route


def total_over(x, axis, bits):
    size = lax.axis_size(axis)
    for bit in bits:
        x = x + lax.ppermute(x, axis, [(i, i ^ bit) for i in range(size)])
    return x


def on_device(
    queries, key_vectors, value_vectors, out_grads, query_gain, key_gain, frame_counts, row_counts
):
    time_count = lax.axis_size("tm")
    height_count = lax.axis_size("height")
    row_count = queries.shape[2]
    feature_count = queries.shape[3]
    keys = key_vectors[0, 0]
    values = value_vectors[0, 0]

    even_t, odd_t = swaps(8, 0), swaps(8, 1, (3,))
    even_h, odd_h = swaps(4, 0), swaps(4, 1)
    key_route = odd_t + [(3, 4), (4, 3)]
    value_route = odd_t + [(3, 0), (4, 7)]
    arrive = [(0, 4), (7, 3)]
    time_index = lax.axis_index("tm")
    across = (time_index == 3) | (time_index == 4)

    tv = lax.ppermute(values, "tm", value_route)
    tk = lax.ppermute(keys, "tm", key_route)
    own = jnp.stack([keys, values])
    he = lax.ppermute(own, "height", even_h)
    ho = lax.ppermute(own, "height", odd_h)
    te = lax.ppermute(own, "tm", even_t)
    vx = lax.ppermute(tv, "tm", arrive)
    he, ho, te, tk = lax.optimization_barrier((he, ho, te, tk))
    ce = lax.ppermute(jnp.stack([he, ho]), "tm", even_t)
    to = jnp.stack([tk, jnp.where(across, vx, tv)])
    ze = lax.ppermute(to, "height", even_h)
    zo = lax.ppermute(to, "height", odd_h)

    outs = attention(
        frame_counts,
        row_counts,
        query_gain,
        key_gain,
        queries[0, 0],
        out_grads[0, 0],
        [own, te, to, he, ho, ce, ze, zo],
    )
    own, te, to, he, ho, ce, ze, zo, d_queries, gain_parts = outs

    def add(*parts):
        return sum(x.astype(jnp.float32) for x in parts).astype(jnp.bfloat16)

    ze = lax.ppermute(ze, "height", even_h)
    zo = lax.ppermute(zo, "height", odd_h)
    ce = lax.ppermute(ce, "tm", even_t)
    gain_local = jnp.sum(gain_parts.reshape(2, 8, HD), axis=1)
    gain_local = total_over(gain_local, "dp", (1, 2, 4))
    gain_local, ze, zo = lax.optimization_barrier((gain_local, ze, zo))
    to = add(to, ze, zo)
    gain_local, _ = lax.optimization_barrier((gain_local, to))
    to = lax.ppermute(to, "tm", key_route)
    he = lax.ppermute(add(he, ce[0]), "height", even_h)
    ho = lax.ppermute(add(ho, ce[1]), "height", odd_h)
    gain_local, te = lax.optimization_barrier((total_over(gain_local, "tm", (1, 2)), te))
    te = lax.ppermute(te, "tm", even_t)
    inner = [t for t in range(8) if t % 4 in (1, 2)]
    x = gain_local
    x = x + lax.ppermute(x, "tm", [(t, t ^ 4) for t in inner])
    for bit in (1, 2):
        route = [(4 * t + h, 4 * t + (h ^ bit)) for t in inner for h in range(4)]
        x = x + lax.ppermute(x, ("tm", "height"), route)
    outer = lax.ppermute(x, "tm", [(1, 0), (2, 3), (5, 4), (6, 7)])
    place = lax.rem(lax.axis_index("tm"), 4)
    gain_total = jnp.where((place == 1) | (place == 2), x, outer)
    d_keys, d_values = finish(key_gain, keys, [own, te, to, he, ho])

    head_total = lax.axis_size("dp") * (feature_count // HD)
    scaling = 1.0 / math.sqrt(time_count * height_count * row_count * head_total)
    gain_grads = gain_total * scaling
    return (d_queries[None, None], d_keys[None, None], d_values[None, None], gain_grads)


def solution(mesh):
    split = P("tm", "height", None, "dp")
    return jax.shard_map(
        on_device,
        mesh=mesh,
        in_specs=(split,) * 4 + (P(),) * 4,
        out_specs=(split,) * 3 + (P(),),
        check_vma=False,
    )
```

time: 163 us -> 157 us (0.963)
  starting transfers between devices: 69.6 us -> 46.9 us
  waiting for transfers between devices: 63.9 us -> 78 us
  other arithmetic: 2.59 us -> 6.46 us
  Pallas kernels: 25.1 us -> 22.6 us
    ppermute x13 -> x12, waiting for transfers between devices: 14.7 us -> 44.2 us  [the longest x1 28.8 us: on_device(): outer = lax.ppermute(x, 'tm', [(1, 0), (2, 3), (5, 4), (6, 7)])]
    ppermute x1, starting transfers between devices: 17.1 us -> 1.33 us  [on_device(): te = lax.ppermute(te, 'tm', even_t)]
    ppermute x1, waiting for transfers between devices: 10.8 us -> 0.01 us  [on_device(): ce = lax.ppermute(ce, 'tm', even_t)]
    ppermute x8 -> x5, starting transfers between devices: 9.26 us -> 18.3 us  [total_over(): x = x + lax.ppermute(x, axis, [(i, i ^ bit) for i in range(size)])]
    ppermute x2 -> x1, starting transfers between devices: 15 us -> 6.52 us  [on_device(): vx = lax.ppermute(tv, 'tm', arrive)]
    ppermute x13 -> x12, starting transfers between devices: 17 us -> 11.1 us  [the longest x1 2.77 us: on_device(): ze = lax.ppermute(to, 'height', even_h)]
    ppermute x8 -> x5, waiting for transfers between devices: 23.8 us -> 17.8 us  [total_over(): x = x + lax.ppermute(x, axis, [(i, i ^ bit) for i in range(size)])]
    ppermute x2 -> x1, waiting for transfers between devices: 3.79 us -> 6.95 us  [on_device(): vx = lax.ppermute(tv, 'tm', arrive)]
  transfers between devices with their start and end apart: 30 -> 25, of which waited for: 13 -> 11; matrix products, arithmetic and copies ran while one was open for 0% -> 3% of each run, Pallas kernels for 1% -> 0%
where the time goes in v3:
time: 157 us
  waiting for transfers between devices  78 us (50%)
  starting transfers between devices  46.9 us (30%)
  Pallas kernels  22.6 us (14%)
  other arithmetic  6.46 us (4%)
  local copies, waits for them, and re-layouts  1.68 us (1%)
    ppermute x1, waiting for transfers between devices, on_device(): outer = lax.ppermute(x, 'tm', [(1, 0), (2, 3), (5, 4), (6, 7)])  28.8 us
    pallas_call x1, Pallas kernels, attention(): pl.pallas_call(attention_kernel, grid=(heads,), in_specs=[pl.BlockSpec(me...  20.4 us
    ppermute x5, starting transfers between devices, total_over(): x = x + lax.ppermute(x, axis, [(i, i ^ bit) for i in range(size)])  18.3 us
    ppermute x5, waiting for transfers between devices, total_over(): x = x + lax.ppermute(x, axis, [(i, i ^ bit) for i in range(size)])  17.8 us
    ppermute x1, waiting for transfers between devices, on_device(): ze = lax.ppermute(to, 'height', even_h)  10.4 us
    ppermute x1, waiting for transfers between devices, on_device(): tv = lax.ppermute(values, 'tm', value_route)  9.01 us
    ppermute x1, waiting for transfers between devices, on_device(): vx = lax.ppermute(tv, 'tm', arrive)  6.95 us
    ppermute x1, starting transfers between devices, on_device(): vx = lax.ppermute(tv, 'tm', arrive)  6.52 us
  transfers between devices with their start and end apart: 25, of which 11 were waited for; matrix products, arithmetic and copies ran while one was open for 3% of the time, Pallas kernels for 0%

profile of v3, /device:TPU:2, one launch (start us, length us, event | category | flops | bytes accessed | tf_op | source)
XLA Modules:
  0.0 156.6 jit_solution(13288949281992474976)
XLA Ops:
  0.7 1.2 pad_maximum_fusion.1.rest_0_
  1.8 1.7 %collective-permute-start.2 = (bf16[2,384,384]{2,1,0:T(8,128)(2,1)S(1)}, bf16[2,384,384]{2,1,0:T(8,128)(2,1)S(1)}, u32[]{:S(2)}, u32[]{:S(2)}) collective-permute-start(bf16[2,384,384]{2,1,0:T(8,128)(2,1)S(1)} %pad_maximum_fusion.1.rest_0_), channel_id=1, source_target_pairs={{0,4},{4,0},{8,12},{12,8},{16,20},{20,16},{24,28},{28,24},{1,5},{5... | collective-permute-start | bytes 1769480 | tf_op jit(solution)/shard_map/ppermute | solution.py:244
  4.2 5.1 %collective-permute-start = (bf16[2,384,384]{2,1,0:T(8,128)(2,1)S(1)}, bf16[2,384,384]{2,1,0:T(8,128)(2,1)S(1)}, u32[]{:S(2)}, u32[]{:S(2)}) collective-permute-start(bf16[2,384,384]{2,1,0:T(8,128)(2,1)S(1)} %pad_maximum_fusion.1.rest_0_), channel_id=1, source_target_pairs={{0,1},{1,0},{2,3},{3,2},{4,5},{5,4},{6,7},{7,6},{8,9},{9,8},{10,11... | collective-permute-start | bytes 1769480 | tf_op jit(solution)/shard_map/ppermute | solution.py:242
  9.3 1.3 collective-permute-start.4
  11.3 9.0 %collective-permute-done.4 = bf16[384,384]{1,0:T(8,128)(2,1)S(1)} collective-permute-done((bf16[384,384]{1,0:T(8,128)(2,1)S(1)}, bf16[384,384]{1,0:T(8,128)(2,1)S(1)}, u32[]{:S(2)}, u32[]{:S(2)}) %collective-permute-start.4) | collective-permute-done | bytes 294944 | tf_op jit(solution)/shard_map/ppermute | solution.py:239
  20.3 6.5 %collective-permute-start.5 = (bf16[384,384]{1,0:T(8,128)(2,1)S(1)}, bf16[384,384]{1,0:T(8,128)(2,1)}, u32[]{:S(2)}, u32[]{:S(2)}) collective-permute-start(bf16[384,384]{1,0:T(8,128)(2,1)S(1)} %collective-permute-done.4), channel_id=1, source_target_pairs={{0,16},{28,12},{1,17},{29,13},{2,18},{30,14},{3,19},{31,15},{32,48... | collective-permute-start | bytes 884744 | tf_op jit(solution)/shard_map/ppermute | solution.py:245
  27.6 1.2 pad_maximum_fusion
  28.9 6.9 %collective-permute-done.5 = bf16[384,384]{1,0:T(8,128)(2,1)} collective-permute-done((bf16[384,384]{1,0:T(8,128)(2,1)S(1)}, bf16[384,384]{1,0:T(8,128)(2,1)}, u32[]{:S(2)}, u32[]{:S(2)}) %collective-permute-start.5) | collective-permute-done | bytes 294944 | tf_op jit(solution)/shard_map/ppermute | solution.py:245
  37.6 2.8 %collective-permute-start.7 = (bf16[2,384,384]{2,1,0:T(8,128)(2,1)S(1)}, bf16[2,384,384]{2,1,0:T(8,128)(2,1)S(1)}, u32[]{:S(2)}, u32[]{:S(2)}) collective-permute-start(bf16[2,384,384]{2,1,0:T(8,128)(2,1)S(1)} %pad_maximum_fusion.2.rest_2_), channel_id=1, source_target_pairs={{0,1},{1,0},{2,3},{3,2},{4,5},{5,4},{6,7},{7,6},{8,9},{9,8},{10,11... | collective-permute-start | bytes 1769480 | tf_op jit(solution)/shard_map/ppermute | solution.py:249
  40.4 10.4 %collective-permute-done.7.rest_6_ = bf16[2,384,384]{2,1,0:T(8,128)(2,1)S(1)} collective-permute-done((bf16[2,384,384]{2,1,0:T(8,128)(2,1)S(1)}, bf16[2,384,384]{2,1,0:T(8,128)(2,1)S(1)}, u32[]{:S(2)}, u32[]{:S(2)}) %collective-permute-start.7) | collective-permute-done | bytes 589856 | tf_op jit(solution)/shard_map/ppermute | solution.py:249
  50.7 4.1 %collective-permute-done.6.rest_5_ = bf16[2,2,384,384]{3,2,1,0:T(8,128)(2,1)} collective-permute-done((bf16[2,2,384,384]{3,2,1,0:T(8,128)(2,1)}, bf16[2,2,384,384]{3,2,1,0:T(8,128)(2,1)}, u32[]{:S(2)}, u32[]{:S(2)}) %collective-permute-start.6) | collective-permute-done | bytes 1179680 | tf_op jit(solution)/shard_map/ppermute | solution.py:247
  55.8 20.4 %shard_map.111 = (bf16[2,384,384]{2,1,0:T(8,128)(2,1)S(1)}, bf16[2,384,384]{2,1,0:T(8,128)(2,1)}, bf16[2,384,384]{2,1,0:T(8,128)(2,1)S(1)}, bf16[2,384,384]{2,1,...) custom-call(s32[8]{0:T(128)S(1)} %copy-done.4, ...), custom_call_target="tpu_custom_call" | custom-call | flops 5096079360 | bytes 11796480 | tf_op jit(solution)/shard_map/pallas_call | solution.py:157
  79.5 3.0 %collective-permute-done.10 = f32[2,128]{1,0:T(2,128)S(1)} collective-permute-done((f32[2,128]{1,0:T(2,128)S(1)}, f32[2,128]{1,0:T(2,128)S(1)}, u32[]{:S(2)}, u32[]{:S(2)}) %collective-permute-start.10) | collective-permute-done | bytes 1056 | tf_op jit(solution)/shard_map/ppermute | solution.py:217
  82.6 2.1 %collective-permute-start.11 = (f32[2,128]{1,0:T(2,128)S(1)}, f32[2,128]{1,0:T(2,128)S(1)}, u32[]{:S(2)}, u32[]{:S(2)}) collective-permute-start(f32[2,128]{1,0:T(2,128)S(1)} %add.37), channel_id=1, source_target_pairs={{0,128},{32,160},{64,192},{96,224},{128,0},{160,32},{192,64},{224,... | collective-permute-start | bytes 3080 | tf_op jit(solution)/shard_map/ppermute | solution.py:217
  84.7 2.9 %collective-permute-done.11 = f32[2,128]{1,0:T(2,128)S(1)} collective-permute-done((f32[2,128]{1,0:T(2,128)S(1)}, f32[2,128]{1,0:T(2,128)S(1)}, u32[]{:S(2)}, u32[]{:S(2)}) %collective-permute-start.11) | collective-permute-done | bytes 1056 | tf_op jit(solution)/shard_map/ppermute | solution.py:217
  89.6 1.5 collective-permute-start.14
  91.1 9.9 %collective-permute-done.14 = f32[2,128]{1,0:T(2,128)S(1)} collective-permute-done((f32[2,128]{1,0:T(2,128)S(1)}, f32[2,128]{1,0:T(2,128)S(1)}, u32[]{:S(2)}, u32[]{:S(2)}) %collective-permute-start.14) | collective-permute-done | bytes 1056 | tf_op jit(solution)/shard_map/ppermute | solution.py:217
  101.0 14.1 %collective-permute-start.15 = (f32[2,128]{1,0:T(2,128)S(1)}, f32[2,128]{1,0:T(2,128)S(1)}, u32[]{:S(2)}, u32[]{:S(2)}) collective-permute-start(f32[2,128]{1,0:T(2,128)S(1)} %add.41), channel_id=1, source_target_pairs={{0,8},{4,12},{8,0},{12,4},{16,24},{20,28},{24,16},{28,20},{1,9},{5... | collective-permute-start | bytes 3080 | tf_op jit(solution)/shard_map/ppermute | solution.py:217
  116.6 1.3 collective-permute-start.16
  117.9 1.4 fusion
  120.0 1.6 %collective-permute-start.19 = (bf16[2,384,384]{2,1,0:T(8,128)(2,1)}, bf16[2,384,384]{2,1,0:T(8,128)(2,1)S(1)}, u32[]{:S(2)}, u32[]{:S(2)}) collective-permute-start(bf16[2,384,384]{2,1,0:T(8,128)(2,1)} %get-tuple-element.49), channel_id=1, source_target_pairs={{0,1},{1,0},{2,3},{3,2},{4,5},{5,4},{6,7},{7,6},{8,9},{9,8},{10,11... | collective-permute-start | bytes 1769480 | tf_op jit(solution)/shard_map/ppermute | solution.py:275
  123.7 1.3 collective-permute-start.24
  125.0 28.8 %collective-permute-done.24 = f32[2,128]{1,0:T(2,128)S(1)} collective-permute-done((f32[2,128]{1,0:T(2,128)S(1)}, f32[2,128]{1,0:T(2,128)S(1)}, u32[]{:S(2)}, u32[]{:S(2)}) %collective-permute-start.24) | collective-permute-done | bytes 1056 | tf_op jit(solution)/shard_map/ppermute | solution.py:285
  154.4 2.2 %shard_map.112 = (bf16[384,384]{1,0:T(8,128)(2,1)}, bf16[384,384]{1,0:T(8,128)(2,1)}) custom-call(f32[1,128]{1,0:T(1,128)S(1)} %bitcast.34, bf16[384,384]{1,0:T(8,128)(2,1)S(1)} %bitcast.30, bf16[2,384,384]{2,1,0:T(8,128)(2,1)S(1)} %get-tuple-element.31.rest_0_, bf16[2,384,384]{2,1,0:T(8,128)(2,1)S(1)} %collective-permute-done.16.rest_1_, ...), custom_call_target="tpu_custom_call" | custom-call | tf_op jit(solution)/shard_map/pallas_call | solution.py:196
  (62 shorter events, 15.1 us)
Async XLA Ops:
  1.8 25.0 %collective-permute-start.2 = (bf16[2,384,384]{2,1,0:T(8,128)(2,1)S(1)}, bf16[2,384,384]{2,1,0:T(8,128)(2,1)S(1)}, u32[]{:S(2)}, u32[]{:S(2)}) collective-permute-start(bf16[2,384,384]{2,1,0:T(8,128)(2,1)S(1)} %pad_maximum_fusion.1.rest_0_), channel_id=1, source_target_pairs={{0,4},{4,0},{8,12},{12,8},{16,20},{20,16},{24,28},{28,24},{1,5},{5... | collective-permute-start | bytes 1769480 | tf_op jit(solution)/shard_map/ppermute | solution.py:244
  3.5 23.4 %collective-permute-start.1 = (bf16[2,384,384]{2,1,0:T(8,128)(2,1)S(1)}, bf16[2,384,384]{2,1,0:T(8,128)(2,1)S(1)}, u32[]{:S(2)}, u32[]{:S(2)}) collective-permute-start(bf16[2,384,384]{2,1,0:T(8,128)(2,1)S(1)} %pad_maximum_fusion.1.rest_0_), channel_id=1, source_target_pairs={{1,2},{2,1},{5,6},{6,5},{9,10},{10,9},{13,14},{14,13},{17,18},{18,... | collective-permute-start | bytes 1769480 | tf_op jit(solution)/shard_map/ppermute | solution.py:243
  4.2 22.7 %collective-permute-start = (bf16[2,384,384]{2,1,0:T(8,128)(2,1)S(1)}, bf16[2,384,384]{2,1,0:T(8,128)(2,1)S(1)}, u32[]{:S(2)}, u32[]{:S(2)}) collective-permute-start(bf16[2,384,384]{2,1,0:T(8,128)(2,1)S(1)} %pad_maximum_fusion.1.rest_0_), channel_id=1, source_target_pairs={{0,1},{1,0},{2,3},{3,2},{4,5},{5,4},{6,7},{7,6},{8,9},{9,8},{10,11... | collective-permute-start | bytes 1769480 | tf_op jit(solution)/shard_map/ppermute | solution.py:242
  9.3 11.0 %collective-permute-start.4 = (bf16[384,384]{1,0:T(8,128)(2,1)S(1)}, bf16[384,384]{1,0:T(8,128)(2,1)S(1)}, u32[]{:S(2)}, u32[]{:S(2)}) collective-permute-start(bf16[384,384]{1,0:T(8,128)(2,1)S(1)} %bitcast.39), channel_id=1, source_target_pairs={{4,8},{8,4},{20,24},{24,20},{12,0},{16,28},{5,9},{9,5},{21,25},{25... | collective-permute-start | bytes 884744 | tf_op jit(solution)/shard_map/ppermute | solution.py:239
  10.6 16.2 %collective-permute-start.3 = (bf16[384,384]{1,0:T(8,128)(2,1)S(1)}, bf16[384,384]{1,0:T(8,128)(2,1)S(1)}, u32[]{:S(2)}, u32[]{:S(2)}) collective-permute-start(bf16[384,384]{1,0:T(8,128)(2,1)S(1)} %bitcast.29), channel_id=1, source_target_pairs={{4,8},{8,4},{20,24},{24,20},{12,16},{16,12},{5,9},{9,5},{21,25},{2... | collective-permute-start | bytes 884744 | tf_op jit(solution)/shard_map/ppermute | solution.py:240
  20.3 15.5 %collective-permute-start.5 = (bf16[384,384]{1,0:T(8,128)(2,1)S(1)}, bf16[384,384]{1,0:T(8,128)(2,1)}, u32[]{:S(2)}, u32[]{:S(2)}) collective-permute-start(bf16[384,384]{1,0:T(8,128)(2,1)S(1)} %collective-permute-done.4), channel_id=1, source_target_pairs={{0,16},{28,12},{1,17},{29,13},{2,18},{30,14},{3,19},{31,15},{32,48... | collective-permute-start | bytes 884744 | tf_op jit(solution)/shard_map/ppermute | solution.py:245
  28.8 26.1 %collective-permute-start.6 = (bf16[2,2,384,384]{3,2,1,0:T(8,128)(2,1)}, bf16[2,2,384,384]{3,2,1,0:T(8,128)(2,1)}, u32[]{:S(2)}, u32[]{:S(2)}) collective-permute-start(bf16[2,2,384,384]{3,2,1,0:T(8,128)(2,1)} %pad_maximum_fusion), channel_id=1, source_target_pairs={{0,4},{4,0},{8,12},{12,8},{16,20},{20,16},{24,28},{28,24},{1,5},{5... | collective-permute-start | bytes 3538952 | tf_op jit(solution)/shard_map/ppermute | solution.py:247
  36.9 3.5 %collective-permute-start.8 = (bf16[2,384,384]{2,1,0:T(8,128)(2,1)S(1)}, bf16[2,384,384]{2,1,0:T(8,128)(2,1)S(1)}, u32[]{:S(2)}, u32[]{:S(2)}) collective-permute-start(bf16[2,384,384]{2,1,0:T(8,128)(2,1)S(1)} %pad_maximum_fusion.2.rest_2_), channel_id=1, source_target_pairs={{1,2},{2,1},{5,6},{6,5},{9,10},{10,9},{13,14},{14,13},{17,18},{18,... | collective-permute-start | bytes 1769480 | tf_op jit(solution)/shard_map/ppermute | solution.py:250
  37.6 13.1 %collective-permute-start.7 = (bf16[2,384,384]{2,1,0:T(8,128)(2,1)S(1)}, bf16[2,384,384]{2,1,0:T(8,128)(2,1)S(1)}, u32[]{:S(2)}, u32[]{:S(2)}) collective-permute-start(bf16[2,384,384]{2,1,0:T(8,128)(2,1)S(1)} %pad_maximum_fusion.2.rest_2_), channel_id=1, source_target_pairs={{0,1},{1,0},{2,3},{3,2},{4,5},{5,4},{6,7},{7,6},{8,9},{9,8},{10,11... | collective-permute-start | bytes 1769480 | tf_op jit(solution)/shard_map/ppermute | solution.py:249
  76.2 41.8 %collective-permute-start.18 = (bf16[2,2,384,384]{3,2,1,0:T(8,128)(2,1)S(1)}, bf16[2,2,384,384]{3,2,1,0:T(8,128)(2,1)S(1)}, u32[]{:S(2)}, u32[]{:S(2)}) collective-permute-start(bf16[2,2,384,384]{3,2,1,0:T(8,128)(2,1)S(1)} %get-tuple-element.43), channel_id=1, source_target_pairs={{0,4},{4,0},{8,12},{12,8},{16,20},{20,16},{24,28},{28,24},{1,5},{5... | collective-permute-start | bytes 3538952 | tf_op jit(solution)/shard_map/ppermute | solution.py:268
  76.5 12.1 %collective-permute-start.12 = (bf16[2,384,384]{2,1,0:T(8,128)(2,1)S(1)}, bf16[2,384,384]{2,1,0:T(8,128)(2,1)S(1)}, u32[]{:S(2)}, u32[]{:S(2)}) collective-permute-start(bf16[2,384,384]{2,1,0:T(8,128)(2,1)S(1)} %get-tuple-element.33), channel_id=1, source_target_pairs={{0,1},{1,0},{2,3},{3,2},{4,5},{5,4},{6,7},{7,6},{8,9},{9,8},{10,11... | collective-permute-start | bytes 1769480 | tf_op jit(solution)/shard_map/ppermute | solution.py:266
  77.1 11.5 %collective-permute-start.13 = (bf16[2,384,384]{2,1,0:T(8,128)(2,1)S(1)}, bf16[2,384,384]{2,1,0:T(8,128)(2,1)S(1)}, u32[]{:S(2)}, u32[]{:S(2)}) collective-permute-start(bf16[2,384,384]{2,1,0:T(8,128)(2,1)S(1)} %get-tuple-element.34), channel_id=1, source_target_pairs={{1,2},{2,1},{5,6},{6,5},{9,10},{10,9},{13,14},{14,13},{17,18},{18,... | collective-permute-start | bytes 1769480 | tf_op jit(solution)/shard_map/ppermute | solution.py:267
  77.8 1.2 collective-permute-start.9
  79.0 3.6 %collective-permute-start.10 = (f32[2,128]{1,0:T(2,128)S(1)}, f32[2,128]{1,0:T(2,128)S(1)}, u32[]{:S(2)}, u32[]{:S(2)}) collective-permute-start(f32[2,128]{1,0:T(2,128)S(1)} %add.36), channel_id=1, source_target_pairs={{0,64},{32,96},{64,0},{96,32},{128,192},{160,224},{192,128},{224,1... | collective-permute-start | bytes 3080 | tf_op jit(solution)/shard_map/ppermute | solution.py:217
  82.6 5.1 %collective-permute-start.11 = (f32[2,128]{1,0:T(2,128)S(1)}, f32[2,128]{1,0:T(2,128)S(1)}, u32[]{:S(2)}, u32[]{:S(2)}) collective-permute-start(f32[2,128]{1,0:T(2,128)S(1)} %add.37), channel_id=1, source_target_pairs={{0,128},{32,160},{64,192},{96,224},{128,0},{160,32},{192,64},{224,... | collective-permute-start | bytes 3080 | tf_op jit(solution)/shard_map/ppermute | solution.py:217
  89.6 11.3 %collective-permute-start.14 = (f32[2,128]{1,0:T(2,128)S(1)}, f32[2,128]{1,0:T(2,128)S(1)}, u32[]{:S(2)}, u32[]{:S(2)}) collective-permute-start(f32[2,128]{1,0:T(2,128)S(1)} %add.38), channel_id=1, source_target_pairs={{0,4},{4,0},{8,12},{12,8},{16,20},{20,16},{24,28},{28,24},{1,5},{5... | collective-permute-start | bytes 3080 | tf_op jit(solution)/shard_map/ppermute | solution.py:217
  101.0 15.6 %collective-permute-start.15 = (f32[2,128]{1,0:T(2,128)S(1)}, f32[2,128]{1,0:T(2,128)S(1)}, u32[]{:S(2)}, u32[]{:S(2)}) collective-permute-start(f32[2,128]{1,0:T(2,128)S(1)} %add.41), channel_id=1, source_target_pairs={{0,8},{4,12},{8,0},{12,4},{16,24},{20,28},{24,16},{28,20},{1,9},{5... | collective-permute-start | bytes 3080 | tf_op jit(solution)/shard_map/ppermute | solution.py:217
  115.1 39.3 %collective-permute-start.17 = (bf16[2,384,384]{2,1,0:T(8,128)(2,1)}, bf16[2,384,384]{2,1,0:T(8,128)(2,1)S(1)}, u32[]{:S(2)}, u32[]{:S(2)}) collective-permute-start(bf16[2,384,384]{2,1,0:T(8,128)(2,1)} %add_convert_fusion), channel_id=1, source_target_pairs={{4,8},{8,4},{20,24},{24,20},{12,16},{16,12},{5,9},{9,5},{21,25},{2... | collective-permute-start | bytes 1769480 | tf_op jit(solution)/shard_map/ppermute | solution.py:274
  116.6 37.7 %collective-permute-start.16 = (bf16[2,384,384]{2,1,0:T(8,128)(2,1)}, bf16[2,384,384]{2,1,0:T(8,128)(2,1)S(1)}, u32[]{:S(2)}, u32[]{:S(2)}) collective-permute-start(bf16[2,384,384]{2,1,0:T(8,128)(2,1)} %get-tuple-element.41), channel_id=1, source_target_pairs={{0,4},{4,0},{8,12},{12,8},{16,20},{20,16},{24,28},{28,24},{1,5},{5... | collective-permute-start | bytes 1769480 | tf_op jit(solution)/shard_map/ppermute | solution.py:278
  119.3 35.1 %collective-permute-start.20 = (bf16[2,384,384]{2,1,0:T(8,128)(2,1)}, bf16[2,384,384]{2,1,0:T(8,128)(2,1)S(1)}, u32[]{:S(2)}, u32[]{:S(2)}) collective-permute-start(bf16[2,384,384]{2,1,0:T(8,128)(2,1)} %get-tuple-element.48), channel_id=1, source_target_pairs={{1,2},{2,1},{5,6},{6,5},{9,10},{10,9},{13,14},{14,13},{17,18},{18,... | collective-permute-start | bytes 1769480 | tf_op jit(solution)/shard_map/ppermute | solution.py:276
  120.0 34.4 %collective-permute-start.19 = (bf16[2,384,384]{2,1,0:T(8,128)(2,1)}, bf16[2,384,384]{2,1,0:T(8,128)(2,1)S(1)}, u32[]{:S(2)}, u32[]{:S(2)}) collective-permute-start(bf16[2,384,384]{2,1,0:T(8,128)(2,1)} %get-tuple-element.49), channel_id=1, source_target_pairs={{0,1},{1,0},{2,3},{3,2},{4,5},{5,4},{6,7},{7,6},{8,9},{9,8},{10,11... | collective-permute-start | bytes 1769480 | tf_op jit(solution)/shard_map/ppermute | solution.py:275
  122.3 0.7 collective-permute-start.22
  123.0 0.7 collective-permute-start.23
  123.7 30.1 %collective-permute-start.24 = (f32[2,128]{1,0:T(2,128)S(1)}, f32[2,128]{1,0:T(2,128)S(1)}, u32[]{:S(2)}, u32[]{:S(2)}) collective-permute-start(f32[2,128]{1,0:T(2,128)S(1)} %add.47), channel_id=1, source_target_pairs={{4,0},{8,12},{20,16},{24,28},{5,1},{9,13},{21,17},{25,29},{6,2},{1... | collective-permute-start | bytes 3080 | tf_op jit(solution)/shard_map/ppermute | solution.py:285
  (10 other events, 151.5 us)

commit v4 on v3

--- a/solution.py
+++ b/solution.py
@@ -49,16 +49,12 @@
 
 
 def attention_kernel(frame_counts, row_counts, query_gain, key_gain, queries, grads, *rest):
-    ins, outs, scratch = rest[:8], rest[8:18], rest[18:]
-    own_in, te_in, to_in, he_in, ho_in, ce_in, ze_in, zo_in = ins
-    own, te, to, he, ho, ce, ze, zo, d_queries, gains = outs
-    kn, probs, dps = scratch
+    sources, targets, rest = rest[:9], rest[9:18], rest[18:]
+    d_queries, gains, kn, probs, dps = rest
     f, fe, fo = near(frame_counts, lax.axis_index("tm"))
     r, re, ro = near(row_counts, lax.axis_index("height"))
     frames = (f, fe, fo, f, f, fe, fe, fo, fo)
     rows = (r, r, r, re, ro, re, ro, re, ro)
-    sources = (own_in, te_in, to_in, he_in, ho_in, ce_in.at[0], ce_in.at[1], ze_in, zo_in)
-    targets = (own, te, to, he, ho, ce.at[0], ce.at[1], ze, zo)
 
     q_unit, q_inverse = unit_norm(queries[...])
     gain_q = query_gain[...]
@@ -151,19 +147,15 @@
 def attention(frame_counts, row_counts, query_gain, key_gain, queries, grads, ins):
     heads = queries.shape[1] // HD
     row, pair, whole = block_specs()
-    quad = pl.BlockSpec((2, 2, TILE, HD), lambda h: (0, 0, 0, h))
-    spec_of = {3: pair, 4: quad}
     low = lambda *lead: jax.ShapeDtypeStruct(lead + queries.shape, jnp.bfloat16)
     return pl.pallas_call(
         attention_kernel,
         grid=(heads,),
         in_specs=[pl.BlockSpec(memory_space=pltpu.SMEM)] * 2
         + [whole, whole, row, row]
-        + [spec_of[x.ndim] for x in ins],
-        out_specs=[pair] * 5
-        + [quad, pair, pair, row, pl.BlockSpec((16, HD), lambda h: (0, 0))],
-        out_shape=[low(2)] * 5
-        + [low(2, 2), low(2), low(2), low(), jax.ShapeDtypeStruct((16, HD), jnp.float32)],
+        + [pair] * 9,
+        out_specs=[pair] * 9 + [row, pl.BlockSpec((16, HD), lambda h: (0, 0))],
+        out_shape=[low(2)] * 9 + [low(), jax.ShapeDtypeStruct((16, HD), jnp.float32)],
         scratch_shapes=[
             pltpu.VMEM((9, TILE, HD), jnp.bfloat16),
             pltpu.VMEM((9, TILE, TILE), jnp.float32),
@@ -243,8 +235,9 @@
     ho = lax.ppermute(own, "height", odd_h)
     te = lax.ppermute(own, "tm", even_t)
     vx = lax.ppermute(tv, "tm", arrive)
-    he, ho, te, tk = lax.optimization_barrier((he, ho, te, tk))
-    ce = lax.ppermute(jnp.stack([he, ho]), "tm", even_t)
+    he, ho, te = lax.optimization_barrier((he, ho, te))
+    ce = lax.ppermute(he, "tm", even_t)
+    co = lax.ppermute(ho, "tm", even_t)
     to = jnp.stack([tk, jnp.where(across, vx, tv)])
     ze = lax.ppermute(to, "height", even_h)
     zo = lax.ppermute(to, "height", odd_h)
@@ -256,9 +249,9 @@
         key_gain,
         queries[0, 0],
         out_grads[0, 0],
-        [own, te, to, he, ho, ce, ze, zo],
+        [own, te, to, he, ho, ce, co, ze, zo],
     )
-    own, te, to, he, ho, ce, ze, zo, d_queries, gain_parts = outs
+    own, te, to, he, ho, ce, co, ze, zo, d_queries, gain_parts = outs
 
     def add(*parts):
         return sum(x.astype(jnp.float32) for x in parts).astype(jnp.bfloat16)
@@ -266,14 +259,15 @@
     ze = lax.ppermute(ze, "height", even_h)
     zo = lax.ppermute(zo, "height", odd_h)
     ce = lax.ppermute(ce, "tm", even_t)
+    co = lax.ppermute(co, "tm", even_t)
     gain_local = jnp.sum(gain_parts.reshape(2, 8, HD), axis=1)
     gain_local = total_over(gain_local, "dp", (1, 2, 4))
     gain_local, ze, zo = lax.optimization_barrier((gain_local, ze, zo))
     to = add(to, ze, zo)
     gain_local, _ = lax.optimization_barrier((gain_local, to))
     to = lax.ppermute(to, "tm", key_route)
-    he = lax.ppermute(add(he, ce[0]), "height", even_h)
-    ho = lax.ppermute(add(ho, ce[1]), "height", odd_h)
+    he = lax.ppermute(add(he, ce), "height", even_h)
+    ho = lax.ppermute(add(ho, co), "height", odd_h)
     gain_local, te = lax.optimization_barrier((total_over(gain_local, "tm", (1, 2)), te))
     te = lax.ppermute(te, "tm", even_t)
     inner = [t for t in range(8) if t % 4 in (1, 2)]

time: 157 us -> 141 us (0.90)
  waiting for transfers between devices: 78 us -> 63.2 us
  local copies, waits for them, and re-layouts: 1.68 us -> 0.05 us
    ppermute x1, waiting for transfers between devices: 10.4 us -> 0.01 us  [on_device(): ze = lax.ppermute(to, 'height', even_h)]
    ppermute x5, waiting for transfers between devices: 17.8 us -> 7.59 us  [total_over(): x = x + lax.ppermute(x, axis, [(i, i ^ bit) for i in range(size)])]
    ppermute x3 -> x5, waiting for transfers between devices: 4.08 us -> 14.3 us  [the longest x1 9.4 us: on_device(): co = lax.ppermute(ho, 'tm', even_t)]
    ppermute x3 -> x5, starting transfers between devices: 2.37 us -> 7.04 us  [the longest x1 2.51 us: on_device(): he = lax.ppermute(add(he, ce), 'height', even_h)]
    ppermute x1, waiting for transfers between devices: 28.8 us -> 24.2 us  [on_device(): outer = lax.ppermute(x, 'tm', [(1, 0), (2, 3), (5, 4), (6, 7)])]
    ppermute x1, starting transfers between devices: 2.77 us -> 0.09 us  [on_device(): ze = lax.ppermute(to, 'height', even_h)]
    unnamed x18 -> x16, local copies, waits for them, and re-layouts: 1.68 us -> 0.05 us
  transfers between devices with their start and end apart: 25 -> 27, of which waited for: 11 -> 9; matrix products, arithmetic and copies ran while one was open for 3% -> 3% of each run, Pallas kernels for 0% -> 0%
where the time goes in v4:
time: 141 us; the launch traced here: 140 us
  waiting for transfers between devices  63.2 us (45%)
  starting transfers between devices  47.8 us (34%)
  Pallas kernels  22.4 us (16%)
  other arithmetic  5.93 us (4%)
    ppermute x1, waiting for transfers between devices, on_device(): outer = lax.ppermute(x, 'tm', [(1, 0), (2, 3), (5, 4), (6, 7)])  24.2 us
    pallas_call x1, Pallas kernels, attention(): pl.pallas_call(attention_kernel, grid=(heads,), in_specs=[pl.BlockSpec(me...  20.2 us
    ppermute x5, starting transfers between devices, total_over(): x = x + lax.ppermute(x, axis, [(i, i ^ bit) for i in range(size)])  17.9 us
    ppermute x1, waiting for transfers between devices, on_device(): tv = lax.ppermute(values, 'tm', value_route)  9.71 us
    ppermute x1, waiting for transfers between devices, on_device(): co = lax.ppermute(ho, 'tm', even_t)  9.4 us
    ppermute x5, waiting for transfers between devices, total_over(): x = x + lax.ppermute(x, axis, [(i, i ^ bit) for i in range(size)])  7.59 us
    ppermute x1, waiting for transfers between devices, on_device(): vx = lax.ppermute(tv, 'tm', arrive)  7.36 us
    ppermute x1, starting transfers between devices, on_device(): vx = lax.ppermute(tv, 'tm', arrive)  5.79 us
  transfers between devices with their start and end apart: 27, of which 9 were waited for; matrix products, arithmetic and copies ran while one was open for 3% of the time, Pallas kernels for 0%

profile of v4, /device:TPU:2, one launch (start us, length us, event | category | flops | bytes accessed | tf_op | source)
XLA Modules:
  0.0 140.3 jit_solution(6595536721889473072)
XLA Ops:
  0.7 1.2 pad_maximum_fusion.rest_0_
  1.8 1.7 %collective-permute-start.2 = (bf16[2,384,384]{2,1,0:T(8,128)(2,1)S(1)}, bf16[2,384,384]{2,1,0:T(8,128)(2,1)S(1)}, u32[]{:S(2)}, u32[]{:S(2)}) collective-permute-start(bf16[2,384,384]{2,1,0:T(8,128)(2,1)S(1)} %pad_maximum_fusion.rest_0_), channel_id=1, source_target_pairs={{0,4},{4,0},{8,12},{12,8},{16,20},{20,16},{24,28},{28,24},{1,5},{5... | collective-permute-start | bytes 1769480 | tf_op jit(solution)/shard_map/ppermute | solution.py:236
  4.2 5.1 %collective-permute-start = (bf16[2,384,384]{2,1,0:T(8,128)(2,1)S(1)}, bf16[2,384,384]{2,1,0:T(8,128)(2,1)S(1)}, u32[]{:S(2)}, u32[]{:S(2)}) collective-permute-start(bf16[2,384,384]{2,1,0:T(8,128)(2,1)S(1)} %pad_maximum_fusion.rest_0_), channel_id=1, source_target_pairs={{0,1},{1,0},{2,3},{3,2},{4,5},{5,4},{6,7},{7,6},{8,9},{9,8},{10,11... | collective-permute-start | bytes 1769480 | tf_op jit(solution)/shard_map/ppermute | solution.py:234
  9.3 1.3 collective-permute-start.4
  10.6 9.7 %collective-permute-done.4 = bf16[384,384]{1,0:T(8,128)(2,1)S(1)} collective-permute-done((bf16[384,384]{1,0:T(8,128)(2,1)S(1)}, bf16[384,384]{1,0:T(8,128)(2,1)S(1)}, u32[]{:S(2)}, u32[]{:S(2)}) %collective-permute-start.4) | collective-permute-done | bytes 294944 | tf_op jit(solution)/shard_map/ppermute | solution.py:231
  20.3 5.8 %collective-permute-start.5 = (bf16[384,384]{1,0:T(8,128)(2,1)S(1)}, bf16[384,384]{1,0:T(8,128)(2,1)S(1)}, u32[]{:S(2)}, u32[]{:S(2)}) collective-permute-start(bf16[384,384]{1,0:T(8,128)(2,1)S(1)} %collective-permute-done.4), channel_id=1, source_target_pairs={{0,16},{28,12},{1,17},{29,13},{2,18},{30,14},{3,19},{31,15},{32,48... | collective-permute-start | bytes 884744 | tf_op jit(solution)/shard_map/ppermute | solution.py:237
  26.1 1.4 collective-permute-start.3
  27.6 2.0 %collective-permute-start.7 = (bf16[2,384,384]{2,1,0:T(8,128)(2,1)S(1)}, bf16[2,384,384]{2,1,0:T(8,128)(2,1)S(1)}, u32[]{:S(2)}, u32[]{:S(2)}) collective-permute-start(bf16[2,384,384]{2,1,0:T(8,128)(2,1)S(1)} %collective-permute-done.1.rest_4_), channel_id=1, source_target_pairs={{0,4},{4,0},{8,12},{12,8},{16,20},{20,16},{24,28},{28,24},{1,5},{5... | collective-permute-start | bytes 1769480 | tf_op jit(solution)/shard_map/ppermute | solution.py:240
  29.6 7.4 %collective-permute-done.5 = bf16[384,384]{1,0:T(8,128)(2,1)S(1)} collective-permute-done((bf16[384,384]{1,0:T(8,128)(2,1)S(1)}, bf16[384,384]{1,0:T(8,128)(2,1)S(1)}, u32[]{:S(2)}, u32[]{:S(2)}) %collective-permute-start.5) | collective-permute-done | bytes 294944 | tf_op jit(solution)/shard_map/ppermute | solution.py:237
  37.1 1.1 pad_maximum_fusion.1.rest_2_
  39.0 4.9 %collective-permute-done.6.rest_5_ = bf16[2,384,384]{2,1,0:T(8,128)(2,1)S(1)} collective-permute-done((bf16[2,384,384]{2,1,0:T(8,128)(2,1)S(1)}, bf16[2,384,384]{2,1,0:T(8,128)(2,1)S(1)}, u32[]{:S(2)}, u32[]{:S(2)}) %collective-permute-start.6) | collective-permute-done | bytes 589856 | tf_op jit(solution)/shard_map/ppermute | solution.py:239
  43.9 9.4 %collective-permute-done.7.rest_6_ = bf16[2,384,384]{2,1,0:T(8,128)(2,1)S(1)} collective-permute-done((bf16[2,384,384]{2,1,0:T(8,128)(2,1)S(1)}, bf16[2,384,384]{2,1,0:T(8,128)(2,1)S(1)}, u32[]{:S(2)}, u32[]{:S(2)}) %collective-permute-start.7) | collective-permute-done | bytes 589856 | tf_op jit(solution)/shard_map/ppermute | solution.py:240
  53.3 20.2 %shard_map.111 = (bf16[2,384,384]{2,1,0:T(8,128)(2,1)S(1)}, bf16[2,384,384]{2,1,0:T(8,128)(2,1)}, bf16[2,384,384]{2,1,0:T(8,128)(2,1)S(1)}, bf16[2,384,384]{2,1,...) custom-call(s32[8]{0:T(128)S(1)} %copy-done.4, ...), custom_call_target="tpu_custom_call" | custom-call | flops 5096079360 | bytes 11796480 | tf_op jit(solution)/shard_map/pallas_call | solution.py:151
  75.2 1.7 %collective-permute-start.21 = (bf16[2,384,384]{2,1,0:T(8,128)(2,1)S(1)}, bf16[2,384,384]{2,1,0:T(8,128)(2,1)S(1)}, u32[]{:S(2)}, u32[]{:S(2)}) collective-permute-start(bf16[2,384,384]{2,1,0:T(8,128)(2,1)S(1)} %get-tuple-element.44), channel_id=1, source_target_pairs={{0,4},{4,0},{8,12},{12,8},{16,20},{20,16},{24,28},{28,24},{1,5},{5... | collective-permute-start | bytes 1769480 | tf_op jit(solution)/shard_map/ppermute | solution.py:262
  76.9 1.1 collective-permute-done.10
  78.6 3.0 %collective-permute-done.11 = f32[2,128]{1,0:T(2,128)S(1)} collective-permute-done((f32[2,128]{1,0:T(2,128)S(1)}, f32[2,128]{1,0:T(2,128)S(1)}, u32[]{:S(2)}, u32[]{:S(2)}) %collective-permute-start.11) | collective-permute-done | bytes 1056 | tf_op jit(solution)/shard_map/ppermute | solution.py:209
  81.7 2.1 %collective-permute-start.12 = (f32[2,128]{1,0:T(2,128)S(1)}, f32[2,128]{1,0:T(2,128)S(1)}, u32[]{:S(2)}, u32[]{:S(2)}) collective-permute-start(f32[2,128]{1,0:T(2,128)S(1)} %add.37), channel_id=1, source_target_pairs={{0,128},{32,160},{64,192},{96,224},{128,0},{160,32},{192,64},{224,... | collective-permute-start | bytes 3080 | tf_op jit(solution)/shard_map/ppermute | solution.py:209
  83.8 2.9 %collective-permute-done.12 = f32[2,128]{1,0:T(2,128)S(1)} collective-permute-done((f32[2,128]{1,0:T(2,128)S(1)}, f32[2,128]{1,0:T(2,128)S(1)}, u32[]{:S(2)}, u32[]{:S(2)}) %collective-permute-start.12) | collective-permute-done | bytes 1056 | tf_op jit(solution)/shard_map/ppermute | solution.py:209
  88.5 7.8 %collective-permute-start.15 = (f32[2,128]{1,0:T(2,128)S(1)}, f32[2,128]{1,0:T(2,128)S(1)}, u32[]{:S(2)}, u32[]{:S(2)}) collective-permute-start(f32[2,128]{1,0:T(2,128)S(1)} %add.38), channel_id=1, source_target_pairs={{0,4},{4,0},{8,12},{12,8},{16,20},{20,16},{24,28},{28,24},{1,5},{5... | collective-permute-start | bytes 3080 | tf_op jit(solution)/shard_map/ppermute | solution.py:209
  97.3 2.5 %collective-permute-start.20 = (bf16[2,384,384]{2,1,0:T(8,128)(2,1)}, bf16[2,384,384]{2,1,0:T(8,128)(2,1)S(1)}, u32[]{:S(2)}, u32[]{:S(2)}) collective-permute-start(bf16[2,384,384]{2,1,0:T(8,128)(2,1)} %add_convert_fusion.1), channel_id=1, source_target_pairs={{0,1},{1,0},{2,3},{3,2},{4,5},{5,4},{6,7},{7,6},{8,9},{9,8},{10,11... | collective-permute-start | bytes 1769480 | tf_op jit(solution)/shard_map/ppermute | solution.py:269
  100.3 7.5 %collective-permute-start.16 = (f32[2,128]{1,0:T(2,128)S(1)}, f32[2,128]{1,0:T(2,128)S(1)}, u32[]{:S(2)}, u32[]{:S(2)}) collective-permute-start(f32[2,128]{1,0:T(2,128)S(1)} %add.41), channel_id=1, source_target_pairs={{0,8},{4,12},{8,0},{12,4},{16,24},{20,28},{24,16},{28,20},{1,9},{5... | collective-permute-start | bytes 3080 | tf_op jit(solution)/shard_map/ppermute | solution.py:209
  112.0 1.3 collective-permute-start.26
  113.3 24.2 %collective-permute-done.26 = f32[2,128]{1,0:T(2,128)S(1)} collective-permute-done((f32[2,128]{1,0:T(2,128)S(1)}, f32[2,128]{1,0:T(2,128)S(1)}, u32[]{:S(2)}, u32[]{:S(2)}) %collective-permute-start.26) | collective-permute-done | bytes 1056 | tf_op jit(solution)/shard_map/ppermute | solution.py:279
  138.1 2.2 %shard_map.112 = (bf16[384,384]{1,0:T(8,128)(2,1)}, bf16[384,384]{1,0:T(8,128)(2,1)}) custom-call(f32[1,128]{1,0:T(1,128)S(1)} %bitcast.20, bf16[384,384]{1,0:T(8,128)(2,1)S(1)} %bitcast.18, bf16[2,384,384]{2,1,0:T(8,128)(2,1)S(1)} %get-tuple-element.30.rest_0_, bf16[2,384,384]{2,1,0:T(8,128)(2,1)S(1)} %collective-permute-done.17.rest_1_, ...), custom_call_target="tpu_custom_call" | custom-call | tf_op jit(solution)/shard_map/pallas_call | solution.py:188
  (64 shorter events, 11.8 us)
Async XLA Ops:
  1.8 25.7 %collective-permute-start.2 = (bf16[2,384,384]{2,1,0:T(8,128)(2,1)S(1)}, bf16[2,384,384]{2,1,0:T(8,128)(2,1)S(1)}, u32[]{:S(2)}, u32[]{:S(2)}) collective-permute-start(bf16[2,384,384]{2,1,0:T(8,128)(2,1)S(1)} %pad_maximum_fusion.rest_0_), channel_id=1, source_target_pairs={{0,4},{4,0},{8,12},{12,8},{16,20},{20,16},{24,28},{28,24},{1,5},{5... | collective-permute-start | bytes 1769480 | tf_op jit(solution)/shard_map/ppermute | solution.py:236
  3.5 24.0 %collective-permute-start.1 = (bf16[2,384,384]{2,1,0:T(8,128)(2,1)S(1)}, bf16[2,384,384]{2,1,0:T(8,128)(2,1)S(1)}, u32[]{:S(2)}, u32[]{:S(2)}) collective-permute-start(bf16[2,384,384]{2,1,0:T(8,128)(2,1)S(1)} %pad_maximum_fusion.rest_0_), channel_id=1, source_target_pairs={{1,2},{2,1},{5,6},{6,5},{9,10},{10,9},{13,14},{14,13},{17,18},{18,... | collective-permute-start | bytes 1769480 | tf_op jit(solution)/shard_map/ppermute | solution.py:235
  4.2 23.3 %collective-permute-start = (bf16[2,384,384]{2,1,0:T(8,128)(2,1)S(1)}, bf16[2,384,384]{2,1,0:T(8,128)(2,1)S(1)}, u32[]{:S(2)}, u32[]{:S(2)}) collective-permute-start(bf16[2,384,384]{2,1,0:T(8,128)(2,1)S(1)} %pad_maximum_fusion.rest_0_), channel_id=1, source_target_pairs={{0,1},{1,0},{2,3},{3,2},{4,5},{5,4},{6,7},{7,6},{8,9},{9,8},{10,11... | collective-permute-start | bytes 1769480 | tf_op jit(solution)/shard_map/ppermute | solution.py:234
  9.3 11.0 %collective-permute-start.4 = (bf16[384,384]{1,0:T(8,128)(2,1)S(1)}, bf16[384,384]{1,0:T(8,128)(2,1)S(1)}, u32[]{:S(2)}, u32[]{:S(2)}) collective-permute-start(bf16[384,384]{1,0:T(8,128)(2,1)S(1)} %bitcast.25), channel_id=1, source_target_pairs={{4,8},{8,4},{20,24},{24,20},{12,0},{16,28},{5,9},{9,5},{21,25},{25... | collective-permute-start | bytes 884744 | tf_op jit(solution)/shard_map/ppermute | solution.py:231
  20.3 16.7 %collective-permute-start.5 = (bf16[384,384]{1,0:T(8,128)(2,1)S(1)}, bf16[384,384]{1,0:T(8,128)(2,1)S(1)}, u32[]{:S(2)}, u32[]{:S(2)}) collective-permute-start(bf16[384,384]{1,0:T(8,128)(2,1)S(1)} %collective-permute-done.4), channel_id=1, source_target_pairs={{0,16},{28,12},{1,17},{29,13},{2,18},{30,14},{3,19},{31,15},{32,48... | collective-permute-start | bytes 884744 | tf_op jit(solution)/shard_map/ppermute | solution.py:237
  26.1 10.9 %collective-permute-start.3 = (bf16[384,384]{1,0:T(8,128)(2,1)S(1)}, bf16[384,384]{1,0:T(8,128)(2,1)}, u32[]{:S(2)}, u32[]{:S(2)}) collective-permute-start(bf16[384,384]{1,0:T(8,128)(2,1)S(1)} %bitcast.17), channel_id=1, source_target_pairs={{4,8},{8,4},{20,24},{24,20},{12,16},{16,12},{5,9},{9,5},{21,25},{2... | collective-permute-start | bytes 884744 | tf_op jit(solution)/shard_map/ppermute | solution.py:232
  27.5 16.4 %collective-permute-start.6 = (bf16[2,384,384]{2,1,0:T(8,128)(2,1)S(1)}, bf16[2,384,384]{2,1,0:T(8,128)(2,1)S(1)}, u32[]{:S(2)}, u32[]{:S(2)}) collective-permute-start(bf16[2,384,384]{2,1,0:T(8,128)(2,1)S(1)} %collective-permute-done.rest_3_), channel_id=1, source_target_pairs={{0,4},{4,0},{8,12},{12,8},{16,20},{20,16},{24,28},{28,24},{1,5},{5... | collective-permute-start | bytes 1769480 | tf_op jit(solution)/shard_map/ppermute | solution.py:239
  27.6 25.6 %collective-permute-start.7 = (bf16[2,384,384]{2,1,0:T(8,128)(2,1)S(1)}, bf16[2,384,384]{2,1,0:T(8,128)(2,1)S(1)}, u32[]{:S(2)}, u32[]{:S(2)}) collective-permute-start(bf16[2,384,384]{2,1,0:T(8,128)(2,1)S(1)} %collective-permute-done.1.rest_4_), channel_id=1, source_target_pairs={{0,4},{4,0},{8,12},{12,8},{16,20},{20,16},{24,28},{28,24},{1,5},{5... | collective-permute-start | bytes 1769480 | tf_op jit(solution)/shard_map/ppermute | solution.py:240
  38.2 15.1 %collective-permute-start.9 = (bf16[2,384,384]{2,1,0:T(8,128)(2,1)S(1)}, bf16[2,384,384]{2,1,0:T(8,128)(2,1)S(1)}, u32[]{:S(2)}, u32[]{:S(2)}) collective-permute-start(bf16[2,384,384]{2,1,0:T(8,128)(2,1)S(1)} %pad_maximum_fusion.1.rest_2_), channel_id=1, source_target_pairs={{1,2},{2,1},{5,6},{6,5},{9,10},{10,9},{13,14},{14,13},{17,18},{18,... | collective-permute-start | bytes 1769480 | tf_op jit(solution)/shard_map/ppermute | solution.py:243
  38.9 14.4 %collective-permute-start.8 = (bf16[2,384,384]{2,1,0:T(8,128)(2,1)S(1)}, bf16[2,384,384]{2,1,0:T(8,128)(2,1)S(1)}, u32[]{:S(2)}, u32[]{:S(2)}) collective-permute-start(bf16[2,384,384]{2,1,0:T(8,128)(2,1)S(1)} %pad_maximum_fusion.1.rest_2_), channel_id=1, source_target_pairs={{0,1},{1,0},{2,3},{3,2},{4,5},{5,4},{6,7},{7,6},{8,9},{9,8},{10,11... | collective-permute-start | bytes 1769480 | tf_op jit(solution)/shard_map/ppermute | solution.py:242
  73.5 13.2 %collective-permute-start.13 = (bf16[2,384,384]{2,1,0:T(8,128)(2,1)S(1)}, bf16[2,384,384]{2,1,0:T(8,128)(2,1)S(1)}, u32[]{:S(2)}, u32[]{:S(2)}) collective-permute-start(bf16[2,384,384]{2,1,0:T(8,128)(2,1)S(1)} %get-tuple-element.32), channel_id=1, source_target_pairs={{0,1},{1,0},{2,3},{3,2},{4,5},{5,4},{6,7},{7,6},{8,9},{9,8},{10,11... | collective-permute-start | bytes 1769480 | tf_op jit(solution)/shard_map/ppermute | solution.py:259
  74.1 12.6 %collective-permute-start.14 = (bf16[2,384,384]{2,1,0:T(8,128)(2,1)S(1)}, bf16[2,384,384]{2,1,0:T(8,128)(2,1)S(1)}, u32[]{:S(2)}, u32[]{:S(2)}) collective-permute-start(bf16[2,384,384]{2,1,0:T(8,128)(2,1)S(1)} %get-tuple-element.33), channel_id=1, source_target_pairs={{1,2},{2,1},{5,6},{6,5},{9,10},{10,9},{13,14},{14,13},{17,18},{18,... | collective-permute-start | bytes 1769480 | tf_op jit(solution)/shard_map/ppermute | solution.py:260
  74.8 21.5 %collective-permute-start.19 = (bf16[2,384,384]{2,1,0:T(8,128)(2,1)S(1)}, bf16[2,384,384]{2,1,0:T(8,128)(2,1)S(1)}, u32[]{:S(2)}, u32[]{:S(2)}) collective-permute-start(bf16[2,384,384]{2,1,0:T(8,128)(2,1)S(1)} %get-tuple-element.42), channel_id=1, source_target_pairs={{0,4},{4,0},{8,12},{12,8},{16,20},{20,16},{24,28},{28,24},{1,5},{5... | collective-permute-start | bytes 1769480 | tf_op jit(solution)/shard_map/ppermute | solution.py:261
  75.2 32.6 %collective-permute-start.21 = (bf16[2,384,384]{2,1,0:T(8,128)(2,1)S(1)}, bf16[2,384,384]{2,1,0:T(8,128)(2,1)S(1)}, u32[]{:S(2)}, u32[]{:S(2)}) collective-permute-start(bf16[2,384,384]{2,1,0:T(8,128)(2,1)S(1)} %get-tuple-element.44), channel_id=1, source_target_pairs={{0,4},{4,0},{8,12},{12,8},{16,20},{20,16},{24,28},{28,24},{1,5},{5... | collective-permute-start | bytes 1769480 | tf_op jit(solution)/shard_map/ppermute | solution.py:262
  76.9 1.1 collective-permute-start.10
  78.1 3.6 %collective-permute-start.11 = (f32[2,128]{1,0:T(2,128)S(1)}, f32[2,128]{1,0:T(2,128)S(1)}, u32[]{:S(2)}, u32[]{:S(2)}) collective-permute-start(f32[2,128]{1,0:T(2,128)S(1)} %add.36), channel_id=1, source_target_pairs={{0,64},{32,96},{64,0},{96,32},{128,192},{160,224},{192,128},{224,1... | collective-permute-start | bytes 3080 | tf_op jit(solution)/shard_map/ppermute | solution.py:209
  81.7 5.1 %collective-permute-start.12 = (f32[2,128]{1,0:T(2,128)S(1)}, f32[2,128]{1,0:T(2,128)S(1)}, u32[]{:S(2)}, u32[]{:S(2)}) collective-permute-start(f32[2,128]{1,0:T(2,128)S(1)} %add.37), channel_id=1, source_target_pairs={{0,128},{32,160},{64,192},{96,224},{128,0},{160,32},{192,64},{224,... | collective-permute-start | bytes 3080 | tf_op jit(solution)/shard_map/ppermute | solution.py:209
  87.8 50.3 %collective-permute-start.18 = (bf16[2,384,384]{2,1,0:T(8,128)(2,1)}, bf16[2,384,384]{2,1,0:T(8,128)(2,1)S(1)}, u32[]{:S(2)}, u32[]{:S(2)}) collective-permute-start(bf16[2,384,384]{2,1,0:T(8,128)(2,1)} %add_convert_fusion.2), channel_id=1, source_target_pairs={{4,8},{8,4},{20,24},{24,20},{12,16},{16,12},{5,9},{9,5},{21,25},{2... | collective-permute-start | bytes 1769480 | tf_op jit(solution)/shard_map/ppermute | solution.py:268
  88.5 11.8 %collective-permute-start.15 = (f32[2,128]{1,0:T(2,128)S(1)}, f32[2,128]{1,0:T(2,128)S(1)}, u32[]{:S(2)}, u32[]{:S(2)}) collective-permute-start(f32[2,128]{1,0:T(2,128)S(1)} %add.38), channel_id=1, source_target_pairs={{0,4},{4,0},{8,12},{12,8},{16,20},{20,16},{24,28},{28,24},{1,5},{5... | collective-permute-start | bytes 3080 | tf_op jit(solution)/shard_map/ppermute | solution.py:209
  97.3 40.8 %collective-permute-start.20 = (bf16[2,384,384]{2,1,0:T(8,128)(2,1)}, bf16[2,384,384]{2,1,0:T(8,128)(2,1)S(1)}, u32[]{:S(2)}, u32[]{:S(2)}) collective-permute-start(bf16[2,384,384]{2,1,0:T(8,128)(2,1)} %add_convert_fusion.1), channel_id=1, source_target_pairs={{0,1},{1,0},{2,3},{3,2},{4,5},{5,4},{6,7},{7,6},{8,9},{9,8},{10,11... | collective-permute-start | bytes 1769480 | tf_op jit(solution)/shard_map/ppermute | solution.py:269
  100.3 9.1 %collective-permute-start.16 = (f32[2,128]{1,0:T(2,128)S(1)}, f32[2,128]{1,0:T(2,128)S(1)}, u32[]{:S(2)}, u32[]{:S(2)}) collective-permute-start(f32[2,128]{1,0:T(2,128)S(1)} %add.41), channel_id=1, source_target_pairs={{0,8},{4,12},{8,0},{12,4},{16,24},{20,28},{24,16},{28,20},{1,9},{5... | collective-permute-start | bytes 3080 | tf_op jit(solution)/shard_map/ppermute | solution.py:209
  108.7 29.3 %collective-permute-start.22 = (bf16[2,384,384]{2,1,0:T(8,128)(2,1)}, bf16[2,384,384]{2,1,0:T(8,128)(2,1)S(1)}, u32[]{:S(2)}, u32[]{:S(2)}) collective-permute-start(bf16[2,384,384]{2,1,0:T(8,128)(2,1)} %add_convert_fusion), channel_id=1, source_target_pairs={{1,2},{2,1},{5,6},{6,5},{9,10},{10,9},{13,14},{14,13},{17,18},{18,... | collective-permute-start | bytes 1769480 | tf_op jit(solution)/shard_map/ppermute | solution.py:270
  109.4 28.6 %collective-permute-start.17 = (bf16[2,384,384]{2,1,0:T(8,128)(2,1)}, bf16[2,384,384]{2,1,0:T(8,128)(2,1)S(1)}, u32[]{:S(2)}, u32[]{:S(2)}) collective-permute-start(bf16[2,384,384]{2,1,0:T(8,128)(2,1)} %get-tuple-element.40), channel_id=1, source_target_pairs={{0,4},{4,0},{8,12},{12,8},{16,20},{20,16},{24,28},{28,24},{1,5},{5... | collective-permute-start | bytes 1769480 | tf_op jit(solution)/shard_map/ppermute | solution.py:272
  112.0 25.5 %collective-permute-start.26 = (f32[2,128]{1,0:T(2,128)S(1)}, f32[2,128]{1,0:T(2,128)S(1)}, u32[]{:S(2)}, u32[]{:S(2)}) collective-permute-start(f32[2,128]{1,0:T(2,128)S(1)} %add.47), channel_id=1, source_target_pairs={{4,0},{8,12},{20,16},{24,28},{5,1},{9,13},{21,17},{25,29},{6,2},{1... | collective-permute-start | bytes 3080 | tf_op jit(solution)/shard_map/ppermute | solution.py:279
  (11 other events, 133.5 us)

commit v5 on v4

--- a/solution.py
+++ b/solution.py
@@ -49,6 +49,18 @@
 
 
 def attention_kernel(frame_counts, row_counts, query_gain, key_gain, queries, grads, *rest):
+    for head in range(queries.shape[-1] // HD):
+        part = pl.ds(head * HD, HD)
+        cut = [x.at[..., part] for x in rest[:19]]
+        one_head(
+            head, frame_counts, row_counts, query_gain, key_gain,
+            queries.at[:, part], grads.at[:, part], *cut, *rest[19:],
+        )
+
+
+def one_head(
+    head, frame_counts, row_counts, query_gain, key_gain, queries, grads, *rest
+):
     sources, targets, rest = rest[:9], rest[9:18], rest[18:]
     d_queries, gains, kn, probs, dps = rest
     f, fe, fo = near(frame_counts, lax.axis_index("tm"))
@@ -129,8 +141,7 @@
     dq = dq_t.T
     d_queries[...] = norm_back(dq, q_unit, q_inverse, gain_q).astype(jnp.bfloat16)
 
-    @pl.when(pl.program_id(0) == 0)
-    def _():
+    if head == 0:
         gains[...] = jnp.zeros_like(gains)
 
     gains[0:8] += fold(dq * q_unit, jnp.sum)
@@ -150,11 +161,9 @@
     low = lambda *lead: jax.ShapeDtypeStruct(lead + queries.shape, jnp.bfloat16)
     return pl.pallas_call(
         attention_kernel,
-        grid=(heads,),
         in_specs=[pl.BlockSpec(memory_space=pltpu.SMEM)] * 2
-        + [whole, whole, row, row]
-        + [pair] * 9,
-        out_specs=[pair] * 9 + [row, pl.BlockSpec((16, HD), lambda h: (0, 0))],
+        + [pl.BlockSpec(memory_space=pltpu.VMEM)] * 13,
+        out_specs=[pl.BlockSpec(memory_space=pltpu.VMEM)] * 11,
         out_shape=[low(2)] * 9 + [low(), jax.ShapeDtypeStruct((16, HD), jnp.float32)],
         scratch_shapes=[
             pltpu.VMEM((9, TILE, HD), jnp.bfloat16),
@@ -172,26 +181,23 @@
 
 def finish_kernel(key_gain, keys, *rest):
     pairs, (d_keys, d_values) = rest[:-2], rest[-2:]
-    dk = jnp.zeros(keys.shape, jnp.float32)
-    dv = jnp.zeros(keys.shape, jnp.float32)
-    for part in pairs:
-        dk = dk + part[0].astype(jnp.float32)
-        dv = dv + part[1].astype(jnp.float32)
-    unit, inverse = unit_norm(keys[...])
-    d_keys[...] = norm_back(dk, unit, inverse, key_gain[...]).astype(jnp.bfloat16)
-    d_values[...] = dv.astype(jnp.bfloat16)
+    for head in range(keys.shape[-1] // HD):
+        part = pl.ds(head * HD, HD)
+        total = pairs[0][:, :, part].astype(jnp.float32)
+        for pair in pairs[1:]:
+            total = total + pair[:, :, part].astype(jnp.float32)
+        unit, inverse = unit_norm(keys[:, part])
+        d_keys[:, part] = norm_back(total[0], unit, inverse, key_gain[...]).astype(jnp.bfloat16)
+        d_values[:, part] = total[1].astype(jnp.bfloat16)
 
 
 def finish(key_gain, keys, pairs):
-    heads = keys.shape[1] // HD
-    row, pair, whole = block_specs()
     return pl.pallas_call(
         finish_kernel,
-        grid=(heads,),
-        in_specs=[whole, row] + [pair] * len(pairs),
-        out_specs=[row, row],
+        in_specs=[pl.BlockSpec(memory_space=pltpu.VMEM)] * (2 + len(pairs)),
+        out_specs=[pl.BlockSpec(memory_space=pltpu.VMEM)] * 2,
         out_shape=[jax.ShapeDtypeStruct(keys.shape, jnp.bfloat16)] * 2,
-        compiler_params=pltpu.CompilerParams(vmem_limit_bytes=16 * 2**20),
+        compiler_params=pltpu.CompilerParams(vmem_limit_bytes=24 * 2**20),
     )(key_gain[None], keys, *pairs)
 
 
@@ -261,14 +267,15 @@
     ce = lax.ppermute(ce, "tm", even_t)
     co = lax.ppermute(co, "tm", even_t)
     gain_local = jnp.sum(gain_parts.reshape(2, 8, HD), axis=1)
-    gain_local = total_over(gain_local, "dp", (1, 2, 4))
+    gain_local = total_over(total_over(gain_local, "tm", (3,)), "dp", (1, 2))
     gain_local, ze, zo = lax.optimization_barrier((gain_local, ze, zo))
     to = add(to, ze, zo)
     gain_local, _ = lax.optimization_barrier((gain_local, to))
     to = lax.ppermute(to, "tm", key_route)
     he = lax.ppermute(add(he, ce), "height", even_h)
     ho = lax.ppermute(add(ho, co), "height", odd_h)
-    gain_local, te = lax.optimization_barrier((total_over(gain_local, "tm", (1, 2)), te))
+    gain_local = total_over(total_over(gain_local, "dp", (4,)), "tm", (1,))
+    gain_local, te = lax.optimization_barrier((gain_local, te))
     te = lax.ppermute(te, "tm", even_t)
     inner = [t for t in range(8) if t % 4 in (1, 2)]
     x = gain_local

time: 141 us -> 140 us (level)
  the two profiles are of different devices: /device:TPU:2 before, /device:TPU:31 now
where the time goes in v5:
time: 140 us; the launch traced here: 139 us
  waiting for transfers between devices  65 us (46%)
  starting transfers between devices  47.5 us (34%)
  Pallas kernels  20 us (14%)
  other arithmetic  5.94 us (4%)
    ppermute x1, waiting for transfers between devices, on_device(): outer = lax.ppermute(x, 'tm', [(1, 0), (2, 3), (5, 4), (6, 7)])  19.5 us
    pallas_call x1, Pallas kernels, attention(): pl.pallas_call(attention_kernel, in_specs=[pl.BlockSpec(memory_space=pltp...  18.6 us
    ppermute x1, waiting for transfers between devices, on_device(): he = lax.ppermute(add(he, ce), 'height', even_h)  9.8 us
    ppermute x1, starting transfers between devices, on_device(): tk = lax.ppermute(keys, 'tm', key_route)  8.64 us
    ppermute x1, starting transfers between devices, on_device(): to = lax.ppermute(to, 'tm', key_route)  7.72 us
    ppermute x5, waiting for transfers between devices, total_over(): x = x + lax.ppermute(x, axis, [(i, i ^ bit) for i in range(size)])  7.64 us
    ppermute x1, waiting for transfers between devices, on_device(): co = lax.ppermute(ho, 'tm', even_t)  7.41 us
    ppermute x1, waiting for transfers between devices, on_device(): vx = lax.ppermute(tv, 'tm', arrive)  7.13 us
  transfers between devices with their start and end apart: 27, of which 11 were waited for; matrix products, arithmetic and copies ran while one was open for 3% of the time, Pallas kernels for 0%

profile of v5, /device:TPU:31, one launch (start us, length us, event | category | flops | bytes accessed | tf_op | source)
XLA Modules:
  0.0 139.5 jit_solution(14975503441957334267)
XLA Ops:
  3.1 4.6 %collective-permute-start = (bf16[2,384,384]{2,1,0:T(8,128)(2,1)S(1)}, bf16[2,384,384]{2,1,0:T(8,128)(2,1)S(1)}, u32[]{:S(2)}, u32[]{:S(2)}) collective-permute-start(bf16[2,384,384]{2,1,0:T(8,128)(2,1)S(1)} %pad_maximum_fusion.rest_0_), channel_id=1, source_target_pairs={{0,1},{1,0},{2,3},{3,2},{4,5},{5,4},{6,7},{7,6},{8,9},{9,8},{10,11... | collective-permute-start | bytes 1769480 | tf_op jit(solution)/shard_map/ppermute | solution.py:240
  7.7 2.7 %collective-permute-start.4 = (bf16[384,384]{1,0:T(8,128)(2,1)S(1)}, bf16[384,384]{1,0:T(8,128)(2,1)S(1)}, u32[]{:S(2)}, u32[]{:S(2)}) collective-permute-start(bf16[384,384]{1,0:T(8,128)(2,1)S(1)} %bitcast.25), channel_id=1, source_target_pairs={{4,8},{8,4},{20,24},{24,20},{12,0},{16,28},{5,9},{9,5},{21,25},{25... | collective-permute-start | bytes 884744 | tf_op jit(solution)/shard_map/ppermute | solution.py:237
  10.3 4.7 %collective-permute-done.4 = bf16[384,384]{1,0:T(8,128)(2,1)S(1)} collective-permute-done((bf16[384,384]{1,0:T(8,128)(2,1)S(1)}, bf16[384,384]{1,0:T(8,128)(2,1)S(1)}, u32[]{:S(2)}, u32[]{:S(2)}) %collective-permute-start.4) | collective-permute-done | bytes 294944 | tf_op jit(solution)/shard_map/ppermute | solution.py:237
  15.1 1.3 collective-permute-start.5
  16.4 8.6 %collective-permute-start.3 = (bf16[384,384]{1,0:T(8,128)(2,1)S(1)}, bf16[384,384]{1,0:T(8,128)(2,1)}, u32[]{:S(2)}, u32[]{:S(2)}) collective-permute-start(bf16[384,384]{1,0:T(8,128)(2,1)S(1)} %bitcast.17), channel_id=1, source_target_pairs={{4,8},{8,4},{20,24},{24,20},{12,16},{16,12},{5,9},{9,5},{21,25},{2... | collective-permute-start | bytes 884744 | tf_op jit(solution)/shard_map/ppermute | solution.py:238
  25.2 1.5 %collective-permute-start.7 = (bf16[2,384,384]{2,1,0:T(8,128)(2,1)S(1)}, bf16[2,384,384]{2,1,0:T(8,128)(2,1)S(1)}, u32[]{:S(2)}, u32[]{:S(2)}) collective-permute-start(bf16[2,384,384]{2,1,0:T(8,128)(2,1)S(1)} %collective-permute-done.1.rest_4_), channel_id=1, source_target_pairs={{0,4},{4,0},{8,12},{12,8},{16,20},{20,16},{24,28},{28,24},{1,5},{5... | collective-permute-start | bytes 1769480 | tf_op jit(solution)/shard_map/ppermute | solution.py:246
  26.6 7.1 %collective-permute-done.5 = bf16[384,384]{1,0:T(8,128)(2,1)S(1)} collective-permute-done((bf16[384,384]{1,0:T(8,128)(2,1)S(1)}, bf16[384,384]{1,0:T(8,128)(2,1)S(1)}, u32[]{:S(2)}, u32[]{:S(2)}) %collective-permute-start.5) | collective-permute-done | bytes 294944 | tf_op jit(solution)/shard_map/ppermute | solution.py:243
  33.8 4.2 %collective-permute-done.3 = bf16[384,384]{1,0:T(8,128)(2,1)} collective-permute-done((bf16[384,384]{1,0:T(8,128)(2,1)S(1)}, bf16[384,384]{1,0:T(8,128)(2,1)}, u32[]{:S(2)}, u32[]{:S(2)}) %collective-permute-start.3) | collective-permute-done | bytes 294944 | tf_op jit(solution)/shard_map/ppermute | solution.py:238
  39.9 2.6 %collective-permute-start.8 = (bf16[2,384,384]{2,1,0:T(8,128)(2,1)S(1)}, bf16[2,384,384]{2,1,0:T(8,128)(2,1)S(1)}, u32[]{:S(2)}, u32[]{:S(2)}) collective-permute-start(bf16[2,384,384]{2,1,0:T(8,128)(2,1)S(1)} %pad_maximum_fusion.1.rest_2_), channel_id=1, source_target_pairs={{0,1},{1,0},{2,3},{3,2},{4,5},{5,4},{6,7},{7,6},{8,9},{9,8},{10,11... | collective-permute-start | bytes 1769480 | tf_op jit(solution)/shard_map/ppermute | solution.py:248
  42.5 7.4 %collective-permute-done.7.rest_6_ = bf16[2,384,384]{2,1,0:T(8,128)(2,1)S(1)} collective-permute-done((bf16[2,384,384]{2,1,0:T(8,128)(2,1)S(1)}, bf16[2,384,384]{2,1,0:T(8,128)(2,1)S(1)}, u32[]{:S(2)}, u32[]{:S(2)}) %collective-permute-start.7) | collective-permute-done | bytes 589856 | tf_op jit(solution)/shard_map/ppermute | solution.py:246
  49.9 4.5 %collective-permute-done.8.rest_7_ = bf16[2,384,384]{2,1,0:T(8,128)(2,1)S(1)} collective-permute-done((bf16[2,384,384]{2,1,0:T(8,128)(2,1)S(1)}, bf16[2,384,384]{2,1,0:T(8,128)(2,1)S(1)}, u32[]{:S(2)}, u32[]{:S(2)}) %collective-permute-start.8) | collective-permute-done | bytes 589856 | tf_op jit(solution)/shard_map/ppermute | solution.py:248
  54.5 18.6 %shard_map.111 = (bf16[2,384,384]{2,1,0:T(8,128)(2,1)S(1)}, bf16[2,384,384]{2,1,0:T(8,128)(2,1)}, bf16[2,384,384]{2,1,0:T(8,128)(2,1)S(1)}, bf16[2,384,384]{2,1,...) custom-call(s32[8]{0:T(128)S(1)} %copy-done.4, ...), custom_call_target="tpu_custom_call" | custom-call | flops 5096079360 | bytes 11796480 | tf_op jit(solution)/shard_map/pallas_call | solution.py:162
  73.1 1.2 collective-permute-start.13
  75.1 1.5 %collective-permute-start.21 = (bf16[2,384,384]{2,1,0:T(8,128)(2,1)S(1)}, bf16[2,384,384]{2,1,0:T(8,128)(2,1)S(1)}, u32[]{:S(2)}, u32[]{:S(2)}) collective-permute-start(bf16[2,384,384]{2,1,0:T(8,128)(2,1)S(1)} %get-tuple-element.44), channel_id=1, source_target_pairs={{0,4},{4,0},{8,12},{12,8},{16,20},{20,16},{24,28},{28,24},{1,5},{5... | collective-permute-start | bytes 1769480 | tf_op jit(solution)/shard_map/ppermute | solution.py:268
  76.5 3.6 %collective-permute-done.10 = f32[2,128]{1,0:T(2,128)S(1)} collective-permute-done((f32[2,128]{1,0:T(2,128)S(1)}, f32[2,128]{1,0:T(2,128)S(1)}, u32[]{:S(2)}, u32[]{:S(2)}) %collective-permute-start.10) | collective-permute-done | bytes 1056 | tf_op jit(solution)/shard_map/ppermute | solution.py:215
  80.2 4.6 %collective-permute-start.11 = (f32[2,128]{1,0:T(2,128)S(1)}, f32[2,128]{1,0:T(2,128)S(1)}, u32[]{:S(2)}, u32[]{:S(2)}) collective-permute-start(f32[2,128]{1,0:T(2,128)S(1)} %add.36), channel_id=1, source_target_pairs={{0,32},{32,0},{64,96},{96,64},{128,160},{160,128},{192,224},{224,1... | collective-permute-start | bytes 3080 | tf_op jit(solution)/shard_map/ppermute | solution.py:215
  86.1 2.2 %collective-permute-done.12 = f32[2,128]{1,0:T(2,128)S(1)} collective-permute-done((f32[2,128]{1,0:T(2,128)S(1)}, f32[2,128]{1,0:T(2,128)S(1)}, u32[]{:S(2)}, u32[]{:S(2)}) %collective-permute-start.12) | collective-permute-done | bytes 1056 | tf_op jit(solution)/shard_map/ppermute | solution.py:215
  89.4 7.7 %collective-permute-start.18 = (bf16[2,384,384]{2,1,0:T(8,128)(2,1)}, bf16[2,384,384]{2,1,0:T(8,128)(2,1)S(1)}, u32[]{:S(2)}, u32[]{:S(2)}) collective-permute-start(bf16[2,384,384]{2,1,0:T(8,128)(2,1)} %add_convert_fusion.2), channel_id=1, source_target_pairs={{4,8},{8,4},{20,24},{24,20},{12,16},{16,12},{5,9},{9,5},{21,25},{2... | collective-permute-start | bytes 1769480 | tf_op jit(solution)/shard_map/ppermute | solution.py:274
  97.1 1.2 collective-permute-start.15
  99.3 2.3 %collective-permute-start.20 = (bf16[2,384,384]{2,1,0:T(8,128)(2,1)}, bf16[2,384,384]{2,1,0:T(8,128)(2,1)S(1)}, u32[]{:S(2)}, u32[]{:S(2)}) collective-permute-start(bf16[2,384,384]{2,1,0:T(8,128)(2,1)} %add_convert_fusion.1), channel_id=1, source_target_pairs={{0,1},{1,0},{2,3},{3,2},{4,5},{5,4},{6,7},{7,6},{8,9},{9,8},{10,11... | collective-permute-start | bytes 1769480 | tf_op jit(solution)/shard_map/ppermute | solution.py:275
  106.9 1.3 collective-permute-start.26
  108.2 19.5 %collective-permute-done.26 = f32[2,128]{1,0:T(2,128)S(1)} collective-permute-done((f32[2,128]{1,0:T(2,128)S(1)}, f32[2,128]{1,0:T(2,128)S(1)}, u32[]{:S(2)}, u32[]{:S(2)}) %collective-permute-start.26) | collective-permute-done | bytes 1056 | tf_op jit(solution)/shard_map/ppermute | solution.py:286
  128.2 9.8 %collective-permute-done.20.rest_3_ = bf16[2,384,384]{2,1,0:T(8,128)(2,1)S(1)} collective-permute-done((bf16[2,384,384]{2,1,0:T(8,128)(2,1)}, bf16[2,384,384]{2,1,0:T(8,128)(2,1)S(1)}, u32[]{:S(2)}, u32[]{:S(2)}) %collective-permute-start.20) | collective-permute-done | bytes 589856 | tf_op jit(solution)/shard_map/ppermute | solution.py:275
  138.0 1.4 %shard_map.112 = (bf16[384,384]{1,0:T(8,128)(2,1)}, bf16[384,384]{1,0:T(8,128)(2,1)}) custom-call(f32[1,128]{1,0:T(1,128)S(1)} %bitcast.20, bf16[384,384]{1,0:T(8,128)(2,1)S(1)} %bitcast.18, bf16[2,384,384]{2,1,0:T(8,128)(2,1)S(1)} %get-tuple-element.30.rest_0_, bf16[2,384,384]{2,1,0:T(8,128)(2,1)S(1)} %collective-permute-done.17.rest_1_, ...), custom_call_target="tpu_custom_call" | custom-call | tf_op jit(solution)/shard_map/pallas_call | solution.py:195
  (64 shorter events, 14.4 us)
Async XLA Ops:
  1.8 23.2 %collective-permute-start.2 = (bf16[2,384,384]{2,1,0:T(8,128)(2,1)S(1)}, bf16[2,384,384]{2,1,0:T(8,128)(2,1)S(1)}, u32[]{:S(2)}, u32[]{:S(2)}) collective-permute-start(bf16[2,384,384]{2,1,0:T(8,128)(2,1)S(1)} %pad_maximum_fusion.rest_0_), channel_id=1, source_target_pairs={{0,4},{4,0},{8,12},{12,8},{16,20},{20,16},{24,28},{28,24},{1,5},{5... | collective-permute-start | bytes 1769480 | tf_op jit(solution)/shard_map/ppermute | solution.py:242
  2.4 22.7 %collective-permute-start.1 = (bf16[2,384,384]{2,1,0:T(8,128)(2,1)S(1)}, bf16[2,384,384]{2,1,0:T(8,128)(2,1)S(1)}, u32[]{:S(2)}, u32[]{:S(2)}) collective-permute-start(bf16[2,384,384]{2,1,0:T(8,128)(2,1)S(1)} %pad_maximum_fusion.rest_0_), channel_id=1, source_target_pairs={{1,2},{2,1},{5,6},{6,5},{9,10},{10,9},{13,14},{14,13},{17,18},{18,... | collective-permute-start | bytes 1769480 | tf_op jit(solution)/shard_map/ppermute | solution.py:241
  3.1 22.0 %collective-permute-start = (bf16[2,384,384]{2,1,0:T(8,128)(2,1)S(1)}, bf16[2,384,384]{2,1,0:T(8,128)(2,1)S(1)}, u32[]{:S(2)}, u32[]{:S(2)}) collective-permute-start(bf16[2,384,384]{2,1,0:T(8,128)(2,1)S(1)} %pad_maximum_fusion.rest_0_), channel_id=1, source_target_pairs={{0,1},{1,0},{2,3},{3,2},{4,5},{5,4},{6,7},{7,6},{8,9},{9,8},{10,11... | collective-permute-start | bytes 1769480 | tf_op jit(solution)/shard_map/ppermute | solution.py:240
  7.7 7.4 %collective-permute-start.4 = (bf16[384,384]{1,0:T(8,128)(2,1)S(1)}, bf16[384,384]{1,0:T(8,128)(2,1)S(1)}, u32[]{:S(2)}, u32[]{:S(2)}) collective-permute-start(bf16[384,384]{1,0:T(8,128)(2,1)S(1)} %bitcast.25), channel_id=1, source_target_pairs={{4,8},{8,4},{20,24},{24,20},{12,0},{16,28},{5,9},{9,5},{21,25},{25... | collective-permute-start | bytes 884744 | tf_op jit(solution)/shard_map/ppermute | solution.py:237
  15.1 18.7 %collective-permute-start.5 = (bf16[384,384]{1,0:T(8,128)(2,1)S(1)}, bf16[384,384]{1,0:T(8,128)(2,1)S(1)}, u32[]{:S(2)}, u32[]{:S(2)}) collective-permute-start(bf16[384,384]{1,0:T(8,128)(2,1)S(1)} %collective-permute-done.4), channel_id=1, source_target_pairs={{0,16},{28,12},{1,17},{29,13},{2,18},{30,14},{3,19},{31,15},{32,48... | collective-permute-start | bytes 884744 | tf_op jit(solution)/shard_map/ppermute | solution.py:243
  16.4 21.6 %collective-permute-start.3 = (bf16[384,384]{1,0:T(8,128)(2,1)S(1)}, bf16[384,384]{1,0:T(8,128)(2,1)}, u32[]{:S(2)}, u32[]{:S(2)}) collective-permute-start(bf16[384,384]{1,0:T(8,128)(2,1)S(1)} %bitcast.17), channel_id=1, source_target_pairs={{4,8},{8,4},{20,24},{24,20},{12,16},{16,12},{5,9},{9,5},{21,25},{2... | collective-permute-start | bytes 884744 | tf_op jit(solution)/shard_map/ppermute | solution.py:238
  25.1 17.4 %collective-permute-start.6 = (bf16[2,384,384]{2,1,0:T(8,128)(2,1)S(1)}, bf16[2,384,384]{2,1,0:T(8,128)(2,1)S(1)}, u32[]{:S(2)}, u32[]{:S(2)}) collective-permute-start(bf16[2,384,384]{2,1,0:T(8,128)(2,1)S(1)} %collective-permute-done.rest_3_), channel_id=1, source_target_pairs={{0,4},{4,0},{8,12},{12,8},{16,20},{20,16},{24,28},{28,24},{1,5},{5... | collective-permute-start | bytes 1769480 | tf_op jit(solution)/shard_map/ppermute | solution.py:245
  25.2 24.7 %collective-permute-start.7 = (bf16[2,384,384]{2,1,0:T(8,128)(2,1)S(1)}, bf16[2,384,384]{2,1,0:T(8,128)(2,1)S(1)}, u32[]{:S(2)}, u32[]{:S(2)}) collective-permute-start(bf16[2,384,384]{2,1,0:T(8,128)(2,1)S(1)} %collective-permute-done.1.rest_4_), channel_id=1, source_target_pairs={{0,4},{4,0},{8,12},{12,8},{16,20},{20,16},{24,28},{28,24},{1,5},{5... | collective-permute-start | bytes 1769480 | tf_op jit(solution)/shard_map/ppermute | solution.py:246
  39.2 10.8 %collective-permute-start.9 = (bf16[2,384,384]{2,1,0:T(8,128)(2,1)S(1)}, bf16[2,384,384]{2,1,0:T(8,128)(2,1)S(1)}, u32[]{:S(2)}, u32[]{:S(2)}) collective-permute-start(bf16[2,384,384]{2,1,0:T(8,128)(2,1)S(1)} %pad_maximum_fusion.1.rest_2_), channel_id=1, source_target_pairs={{1,2},{2,1},{5,6},{6,5},{9,10},{10,9},{13,14},{14,13},{17,18},{18,... | collective-permute-start | bytes 1769480 | tf_op jit(solution)/shard_map/ppermute | solution.py:249
  39.9 14.6 %collective-permute-start.8 = (bf16[2,384,384]{2,1,0:T(8,128)(2,1)S(1)}, bf16[2,384,384]{2,1,0:T(8,128)(2,1)S(1)}, u32[]{:S(2)}, u32[]{:S(2)}) collective-permute-start(bf16[2,384,384]{2,1,0:T(8,128)(2,1)S(1)} %pad_maximum_fusion.1.rest_2_), channel_id=1, source_target_pairs={{0,1},{1,0},{2,3},{3,2},{4,5},{5,4},{6,7},{7,6},{8,9},{9,8},{10,11... | collective-permute-start | bytes 1769480 | tf_op jit(solution)/shard_map/ppermute | solution.py:248
  73.1 15.2 %collective-permute-start.13 = (bf16[2,384,384]{2,1,0:T(8,128)(2,1)S(1)}, bf16[2,384,384]{2,1,0:T(8,128)(2,1)S(1)}, u32[]{:S(2)}, u32[]{:S(2)}) collective-permute-start(bf16[2,384,384]{2,1,0:T(8,128)(2,1)S(1)} %get-tuple-element.32), channel_id=1, source_target_pairs={{0,1},{1,0},{2,3},{3,2},{4,5},{5,4},{6,7},{7,6},{8,9},{9,8},{10,11... | collective-permute-start | bytes 1769480 | tf_op jit(solution)/shard_map/ppermute | solution.py:265
  74.3 14.0 %collective-permute-start.14 = (bf16[2,384,384]{2,1,0:T(8,128)(2,1)S(1)}, bf16[2,384,384]{2,1,0:T(8,128)(2,1)S(1)}, u32[]{:S(2)}, u32[]{:S(2)}) collective-permute-start(bf16[2,384,384]{2,1,0:T(8,128)(2,1)S(1)} %get-tuple-element.33), channel_id=1, source_target_pairs={{1,2},{2,1},{5,6},{6,5},{9,10},{10,9},{13,14},{14,13},{17,18},{18,... | collective-permute-start | bytes 1769480 | tf_op jit(solution)/shard_map/ppermute | solution.py:266
  75.0 23.4 %collective-permute-start.19 = (bf16[2,384,384]{2,1,0:T(8,128)(2,1)S(1)}, bf16[2,384,384]{2,1,0:T(8,128)(2,1)S(1)}, u32[]{:S(2)}, u32[]{:S(2)}) collective-permute-start(bf16[2,384,384]{2,1,0:T(8,128)(2,1)S(1)} %get-tuple-element.42), channel_id=1, source_target_pairs={{0,4},{4,0},{8,12},{12,8},{16,20},{20,16},{24,28},{28,24},{1,5},{5... | collective-permute-start | bytes 1769480 | tf_op jit(solution)/shard_map/ppermute | solution.py:267
  75.1 26.5 %collective-permute-start.21 = (bf16[2,384,384]{2,1,0:T(8,128)(2,1)S(1)}, bf16[2,384,384]{2,1,0:T(8,128)(2,1)S(1)}, u32[]{:S(2)}, u32[]{:S(2)}) collective-permute-start(bf16[2,384,384]{2,1,0:T(8,128)(2,1)S(1)} %get-tuple-element.44), channel_id=1, source_target_pairs={{0,4},{4,0},{8,12},{12,8},{16,20},{20,16},{24,28},{28,24},{1,5},{5... | collective-permute-start | bytes 1769480 | tf_op jit(solution)/shard_map/ppermute | solution.py:268
  76.5 3.6 %collective-permute-start.10 = (f32[2,128]{1,0:T(2,128)S(1)}, f32[2,128]{1,0:T(2,128)S(1)}, u32[]{:S(2)}, u32[]{:S(2)}) collective-permute-start(f32[2,128]{1,0:T(2,128)S(1)} %bitcast_reduce_fusion), channel_id=1, source_target_pairs={{0,12},{4,8},{8,4},{12,0},{16,28},{20,24},{24,20},{28,16},{1,13},{... | collective-permute-start | bytes 3080 | tf_op jit(solution)/shard_map/ppermute | solution.py:215
  80.2 5.4 %collective-permute-start.11 = (f32[2,128]{1,0:T(2,128)S(1)}, f32[2,128]{1,0:T(2,128)S(1)}, u32[]{:S(2)}, u32[]{:S(2)}) collective-permute-start(f32[2,128]{1,0:T(2,128)S(1)} %add.36), channel_id=1, source_target_pairs={{0,32},{32,0},{64,96},{96,64},{128,160},{160,128},{192,224},{224,1... | collective-permute-start | bytes 3080 | tf_op jit(solution)/shard_map/ppermute | solution.py:215
  85.6 2.7 %collective-permute-start.12 = (f32[2,128]{1,0:T(2,128)S(1)}, f32[2,128]{1,0:T(2,128)S(1)}, u32[]{:S(2)}, u32[]{:S(2)}) collective-permute-start(f32[2,128]{1,0:T(2,128)S(1)} %add.37), channel_id=1, source_target_pairs={{0,64},{32,96},{64,0},{96,32},{128,192},{160,224},{192,128},{224,1... | collective-permute-start | bytes 3080 | tf_op jit(solution)/shard_map/ppermute | solution.py:215
  89.4 38.8 %collective-permute-start.18 = (bf16[2,384,384]{2,1,0:T(8,128)(2,1)}, bf16[2,384,384]{2,1,0:T(8,128)(2,1)S(1)}, u32[]{:S(2)}, u32[]{:S(2)}) collective-permute-start(bf16[2,384,384]{2,1,0:T(8,128)(2,1)} %add_convert_fusion.2), channel_id=1, source_target_pairs={{4,8},{8,4},{20,24},{24,20},{12,16},{16,12},{5,9},{9,5},{21,25},{2... | collective-permute-start | bytes 1769480 | tf_op jit(solution)/shard_map/ppermute | solution.py:274
  97.1 4.4 %collective-permute-start.15 = (f32[2,128]{1,0:T(2,128)S(1)}, f32[2,128]{1,0:T(2,128)S(1)}, u32[]{:S(2)}, u32[]{:S(2)}) collective-permute-start(f32[2,128]{1,0:T(2,128)S(1)} %add.38), channel_id=1, source_target_pairs={{0,128},{32,160},{64,192},{96,224},{128,0},{160,32},{192,64},{224,... | collective-permute-start | bytes 3080 | tf_op jit(solution)/shard_map/ppermute | solution.py:215
  99.3 38.7 %collective-permute-start.20 = (bf16[2,384,384]{2,1,0:T(8,128)(2,1)}, bf16[2,384,384]{2,1,0:T(8,128)(2,1)S(1)}, u32[]{:S(2)}, u32[]{:S(2)}) collective-permute-start(bf16[2,384,384]{2,1,0:T(8,128)(2,1)} %add_convert_fusion.1), channel_id=1, source_target_pairs={{0,1},{1,0},{2,3},{3,2},{4,5},{5,4},{6,7},{7,6},{8,9},{9,8},{10,11... | collective-permute-start | bytes 1769480 | tf_op jit(solution)/shard_map/ppermute | solution.py:275
  101.6 2.7 %collective-permute-start.16 = (f32[2,128]{1,0:T(2,128)S(1)}, f32[2,128]{1,0:T(2,128)S(1)}, u32[]{:S(2)}, u32[]{:S(2)}) collective-permute-start(f32[2,128]{1,0:T(2,128)S(1)} %add.41), channel_id=1, source_target_pairs={{0,4},{4,0},{8,12},{12,8},{16,20},{20,16},{24,28},{28,24},{1,5},{5... | collective-permute-start | bytes 3080 | tf_op jit(solution)/shard_map/ppermute | solution.py:215
  102.6 35.5 %collective-permute-start.22 = (bf16[2,384,384]{2,1,0:T(8,128)(2,1)}, bf16[2,384,384]{2,1,0:T(8,128)(2,1)S(1)}, u32[]{:S(2)}, u32[]{:S(2)}) collective-permute-start(bf16[2,384,384]{2,1,0:T(8,128)(2,1)} %add_convert_fusion), channel_id=1, source_target_pairs={{1,2},{2,1},{5,6},{6,5},{9,10},{10,9},{13,14},{14,13},{17,18},{18,... | collective-permute-start | bytes 1769480 | tf_op jit(solution)/shard_map/ppermute | solution.py:276
  104.3 33.8 %collective-permute-start.17 = (bf16[2,384,384]{2,1,0:T(8,128)(2,1)}, bf16[2,384,384]{2,1,0:T(8,128)(2,1)S(1)}, u32[]{:S(2)}, u32[]{:S(2)}) collective-permute-start(bf16[2,384,384]{2,1,0:T(8,128)(2,1)} %get-tuple-element.40), channel_id=1, source_target_pairs={{0,4},{4,0},{8,12},{12,8},{16,20},{20,16},{24,28},{28,24},{1,5},{5... | collective-permute-start | bytes 1769480 | tf_op jit(solution)/shard_map/ppermute | solution.py:279
  106.9 20.8 %collective-permute-start.26 = (f32[2,128]{1,0:T(2,128)S(1)}, f32[2,128]{1,0:T(2,128)S(1)}, u32[]{:S(2)}, u32[]{:S(2)}) collective-permute-start(f32[2,128]{1,0:T(2,128)S(1)} %add.47), channel_id=1, source_target_pairs={{4,0},{8,12},{20,16},{24,28},{5,1},{9,13},{21,17},{25,29},{6,2},{1... | collective-permute-start | bytes 3080 | tf_op jit(solution)/shard_map/ppermute | solution.py:286
  (11 other events, 123.3 us)
